TPU v7x, 32 devices: a whole 2x2x4 slice. The times are simulated.
32 devices in a mesh: dp: 8 (over y, x, core), tensor: 4 (over z).
Axes of the slice: x: 2, y: 2, z: 4, core: 2. Of those that a mesh axis runs over, the one named last changes fastest.
Arguments:
- tokens: bfloat16 [4096, 768], P('dp'), may hold values from -6 to 6
- segments: int32 [16, 256], P('dp'), may hold values from 0 to 3, never falling along the last dimension, each value on 1 to 128 neighbouring positions
- cotangent: bfloat16 [4096, 768], P('dp'), may hold values from -6 to 6
- w_qkv: float32 [3, 768, 768], P(None, None, 'tensor'), may hold values from -0.21875 to 0.21875
- w_out: float32 [768, 768], P('tensor'), may hold values from -0.625 to 0.625
- w_up: float32 [768, 3072], P(None, 'tensor'), may hold values from -0.21875 to 0.21875
- w_down: float32 [3072, 768], P('tensor'), may hold values from -0.109375 to 0.109375
- head_bias: float32 [2, 768], P(None, 'tensor'), may hold values from -1.8 to 1.8
- ff_bias: float32 [3072], P('tensor'), may hold values from -1.8 to 1.8
- row_params: float32 [6, 768], replicated
- mom_qkv: float32 [3, 768, 768], P(None, None, 'tensor')
- mom_out: float32 [768, 768], P('tensor')
- mom_up: float32 [768, 3072], P(None, 'tensor')
- mom_down: float32 [3072, 768], P('tensor')
- mom_heads: float32 [2, 768], P(None, 'tensor')
- mom_ff: float32 [3072], P('tensor')
- mom_params: float32 [6, 768], replicated, may hold values from -192 to 192
Outputs:
- layer_out: bfloat16 [4096, 768], P('dp')
- grad_tokens: bfloat16 [4096, 768], P('dp')
- new_mom_qkv: float32 [3, 768, 768], P(None, None, 'tensor')
- new_qkv: float32 [3, 768, 768], P(None, None, 'tensor')
- low_qkv: bfloat16 [3, 768, 768], P(None, None, 'tensor')
- new_mom_out: float32 [768, 768], P('tensor')
- new_out: float32 [768, 768], P('tensor')
- low_out: bfloat16 [768, 768], P('tensor')
- new_mom_up: float32 [768, 3072], P(None, 'tensor')
- new_up: float32 [768, 3072], P(None, 'tensor')
- low_up: bfloat16 [768, 3072], P(None, 'tensor')
- new_mom_down: float32 [3072, 768], P('tensor')
- new_down: float32 [3072, 768], P('tensor')
- low_down: bfloat16 [3072, 768], P('tensor')
- new_mom_heads: float32 [2, 768], P(None, 'tensor')
- new_heads: float32 [2, 768], P(None, 'tensor')
- new_mom_ff: float32 [3072], P('tensor')
- new_ff: float32 [3072], P('tensor')
- new_mom_params: float32 [6, 768], replicated
- new_params: float32 [6, 768], replicated
Inputs may be any that keep to these rules, and one draw needn't show every extreme that they name: `segments`: within each row of 256 positions the numbers never fall; each number present covers 1 to 128 positions, and one covers exactly 128.
All inputs are finite; a program needn't handle non-finite values.
Results may differ from a plain program's by a relative error of at most 0.024.
Values may be sent and summed in bfloat16 or wider, within the bound.
A program may use at most 192 MiB of HBM per device.

v0:
```python
import math

import jax
import jax.numpy as jnp
from jax import lax
from jax.sharding import PartitionSpec as P

D = 768
HD = 64
FF = 3072
NS_STEPS = 5


HIGHEST = lax.Precision.HIGHEST
EPS_NORM = 1e-05
coef_a = 3.4445
coef_b = -4.775
coef_c = 2.0315


def layer_norm(values, gain, shift):
    center = values - jnp.mean(values, axis=-1, keepdims=True)
    inverse = lax.rsqrt(jnp.mean(center * center, axis=-1, keepdims=True) + EPS_NORM)
    normed = center * inverse
    return (normed * gain + shift, normed, inverse)


def norm_back(grad_out, normed, inverse, gain):
    scaled = grad_out * gain
    first_mean = jnp.mean(scaled, axis=-1, keepdims=True)
    second_mean = jnp.mean(scaled * normed, axis=-1, keepdims=True)
    return inverse * (scaled - first_mean - normed * second_mean)


def gelu_slope(upward):
    cdf_part = 0.5 * (1.0 + jax.scipy.special.erf(upward / math.sqrt(2.0)))
    return cdf_part + upward * jnp.exp(-0.5 * upward * upward) / math.sqrt(2.0 * math.pi)


def tdot(left, right):
    return lax.dot_general(
        left, right, (((0,), (0,)), ((), ())), preferred_element_type=jnp.float32
    )


def gram_of(block):
    return lax.dot_general(
        block,
        block,
        (((0,), (0,)), ((), ())),
        precision=HIGHEST,
        preferred_element_type=jnp.float32,
    )


def ns_update(iterate, gram_sum):
    product = jnp.dot(iterate, gram_sum, precision=HIGHEST)
    second = jnp.dot(product, gram_sum, precision=HIGHEST)
    return coef_a * iterate + coef_b * product + coef_c * second


def vector_step(param, moment, mean_sq):
    return param - 0.1 * moment * lax.rsqrt(mean_sq + 1e-06)


def local(
    tokens,
    segments,
    cotangent,
    w_qkv,
    w_out,
    w_up,
    w_down,
    head_bias,
    ff_bias,
    row_params,
    mom_qkv,
    mom_out,
    mom_up,
    mom_down,
    mom_heads,
    mom_ff,
    mom_params,
):
    tok_count, width = tokens.shape
    columns = w_qkv.shape[2]
    ff_cols = w_up.shape[1]
    local_heads = columns // HD
    seq_count, seq_len = segments.shape
    score_scale = 1.0 / math.sqrt(HD)
    tensor_size = lax.axis_size("tensor")
    tensor_pos = lax.axis_index("tensor")
    wq_low = w_qkv.astype(jnp.bfloat16)
    wo_low = w_out.astype(jnp.bfloat16)
    wu_low = w_up.astype(jnp.bfloat16)
    wd_low = w_down.astype(jnp.bfloat16)

    def split_heads(rows):
        return rows.reshape(seq_count, seq_len, local_heads, HD).transpose(0, 2, 1, 3)

    def join_heads(blocks):
        return blocks.transpose(0, 2, 1, 3).reshape(tok_count, columns)

    query_h = split_heads(
        (jnp.dot(tokens, wq_low[0], preferred_element_type=jnp.float32) + head_bias[0]).astype(
            jnp.bfloat16
        )
    )
    keys_h = split_heads(
        jnp.dot(tokens, wq_low[1], preferred_element_type=jnp.float32).astype(jnp.bfloat16)
    )
    values_h = split_heads(
        (jnp.dot(tokens, wq_low[2], preferred_element_type=jnp.float32) + head_bias[1]).astype(
            jnp.bfloat16
        )
    )
    same_seg = (segments[:, :, None] == segments[:, None, :])[:, None]
    scores = (
        jnp.einsum("shqd,shkd->shqk", query_h, keys_h, preferred_element_type=jnp.float32)
        * score_scale
    )
    scores = jnp.where(same_seg, scores, -1e30)
    row_max = jnp.max(scores, axis=-1, keepdims=True)
    expo = jnp.exp(scores - row_max)
    probs = expo / jnp.sum(expo, axis=-1, keepdims=True)
    probs_low = probs.astype(jnp.bfloat16)
    context = jnp.einsum("shqk,shkd->shqd", probs_low, values_h, preferred_element_type=jnp.float32)
    context_low = join_heads(context.astype(jnp.bfloat16))
    attn = lax.psum(
        jnp.dot(context_low, wo_low, preferred_element_type=jnp.float32).astype(jnp.bfloat16),
        "tensor",
    ).astype(jnp.float32)
    first_in = tokens.astype(jnp.float32) + attn + row_params[0]
    hidden_one, normed_one, inverse_one = layer_norm(first_in, row_params[2], row_params[3])
    hidden_low = hidden_one.astype(jnp.bfloat16)
    upward = jnp.dot(hidden_low, wu_low, preferred_element_type=jnp.float32) + ff_bias
    activated_low = jax.nn.gelu(upward, approximate=False).astype(jnp.bfloat16)
    mlp = lax.psum(
        jnp.dot(activated_low, wd_low, preferred_element_type=jnp.float32).astype(jnp.bfloat16),
        "tensor",
    ).astype(jnp.float32)
    second_in = hidden_one + mlp + row_params[1]
    output_rows, normed_two, inverse_two = layer_norm(second_in, row_params[4], row_params[5])
    grad_out = cotangent.astype(jnp.float32)
    grad_second = norm_back(grad_out, normed_two, inverse_two, row_params[4])
    grad_mlp_low = grad_second.astype(jnp.bfloat16)
    grad_down = tdot(activated_low, grad_mlp_low)
    grad_act = jnp.dot(grad_mlp_low, wd_low.T, preferred_element_type=jnp.float32)
    grad_up_low = (grad_act * gelu_slope(upward)).astype(jnp.bfloat16)
    grad_upw = tdot(hidden_low, grad_up_low)
    grad_hidden = (
        lax.psum(
            jnp.dot(grad_up_low, wu_low.T, preferred_element_type=jnp.float32).astype(jnp.bfloat16),
            "tensor",
        ).astype(jnp.float32)
        + grad_second
    )
    grad_first = norm_back(grad_hidden, normed_one, inverse_one, row_params[2])
    grad_attn_low = grad_first.astype(jnp.bfloat16)
    grad_outw = tdot(context_low, grad_attn_low)
    grad_context = split_heads(
        jnp.dot(grad_attn_low, wo_low.T, preferred_element_type=jnp.float32).astype(jnp.bfloat16)
    )
    grad_values = jnp.einsum(
        "shqk,shqd->shkd", probs_low, grad_context, preferred_element_type=jnp.float32
    )
    grad_probs = jnp.einsum(
        "shqd,shkd->shqk", grad_context, values_h, preferred_element_type=jnp.float32
    )
    grad_scores = (
        probs * (grad_probs - jnp.sum(probs * grad_probs, axis=-1, keepdims=True))
    ).astype(jnp.bfloat16)
    grad_query = (
        jnp.einsum("shqk,shkd->shqd", grad_scores, keys_h, preferred_element_type=jnp.float32)
        * score_scale
    )
    grad_keys = (
        jnp.einsum("shqk,shqd->shkd", grad_scores, query_h, preferred_element_type=jnp.float32)
        * score_scale
    )
    gq_low = join_heads(grad_query.astype(jnp.bfloat16))
    gk_low = join_heads(grad_keys.astype(jnp.bfloat16))
    gv_low = join_heads(grad_values.astype(jnp.bfloat16))
    grad_qkv = jnp.stack([tdot(tokens, gq_low), tdot(tokens, gk_low), tdot(tokens, gv_low)])
    back_terms = jnp.dot(gq_low, wq_low[0].T, preferred_element_type=jnp.float32)
    back_terms = back_terms + jnp.dot(gk_low, wq_low[1].T, preferred_element_type=jnp.float32)
    back_terms = back_terms + jnp.dot(gv_low, wq_low[2].T, preferred_element_type=jnp.float32)
    grad_inputs = (
        lax.psum(back_terms.astype(jnp.bfloat16), "tensor").astype(jnp.float32) + grad_first
    )
    share = tok_count // tensor_size
    row_start = tensor_pos * share

    def own_sum(values):
        return jnp.sum(lax.dynamic_slice_in_dim(values, row_start, share, 0), axis=0)

    param_grad = jnp.stack(
        [
            own_sum(grad_first),
            own_sum(grad_second),
            own_sum(grad_hidden * normed_one),
            own_sum(grad_hidden),
            own_sum(grad_out * normed_two),
            own_sum(grad_out),
        ]
    )
    heads_part = jnp.stack(
        [jnp.sum(gq_low.astype(jnp.float32), axis=0), jnp.sum(gv_low.astype(jnp.float32), axis=0)]
    )
    heads_full = lax.dynamic_update_slice(
        jnp.zeros((2, width), jnp.float32), heads_part, (jnp.int32(0), tensor_pos * columns)
    )
    ff_part = jnp.sum(grad_up_low.astype(jnp.float32), axis=0)
    ff_full = lax.dynamic_update_slice(
        jnp.zeros((ff_cols * tensor_size,), jnp.float32), ff_part, (tensor_pos * ff_cols,)
    )
    param_sum, heads_sum, ff_sum = lax.psum((param_grad, heads_full, ff_full), ("dp", "tensor"))
    heads_own = lax.dynamic_slice_in_dim(heads_sum, tensor_pos * columns, columns, 1)
    ff_own = lax.dynamic_slice_in_dim(ff_sum, tensor_pos * ff_cols, ff_cols, 0)
    new_mom_heads = 0.5 * mom_heads + heads_own
    new_mom_ff = 0.5 * mom_ff + ff_own
    new_mom_params = 0.5 * mom_params + param_sum
    vec_squares = jnp.concatenate(
        [jnp.sum(new_mom_heads * new_mom_heads, axis=1), jnp.sum(new_mom_ff * new_mom_ff)[None]]
    )
    olds = (mom_qkv, mom_out, mom_up, mom_down)
    weights = (w_qkv, w_out, w_up, w_down)
    wide = math.sqrt(FF / D)
    factors = (0.8 * math.sqrt(3.0), 0.8, 0.8 * wide, 0.8 * wide)
    summed = (
        lax.psum(grad_qkv.astype(jnp.bfloat16), "dp").astype(jnp.float32),
        lax.psum(grad_outw.astype(jnp.bfloat16), "dp").astype(jnp.float32),
        lax.psum(grad_upw.astype(jnp.bfloat16), "dp").astype(jnp.float32),
        lax.psum(grad_down.astype(jnp.bfloat16), "dp").astype(jnp.float32),
    )
    moments = [0.5 * old_mom + new_grad for old_mom, new_grad in zip(olds, summed)]
    new_mom_qkv, new_mom_out, new_mom_up, new_mom_down = moments
    qkv_part = moments[0]
    blocks = [
        qkv_part.transpose(0, 2, 1).reshape(3 * qkv_part.shape[2], width),
        moments[1],
        moments[2].T,
        moments[3],
    ]
    squares = jnp.concatenate(
        [jnp.stack([jnp.sum(block * block) for block in blocks]), vec_squares]
    )
    totals = lax.psum(squares, "tensor")
    iterates = [block / (jnp.sqrt(totals[place]) + 1e-07) for place, block in enumerate(blocks)]
    for sweep in range(NS_STEPS):
        partials = [gram_of(iterate) for iterate in iterates]
        grams = (
            lax.psum(partials[0].astype(jnp.bfloat16), "tensor").astype(jnp.float32),
            lax.psum(partials[1].astype(jnp.bfloat16), "tensor").astype(jnp.float32),
            lax.psum(partials[2].astype(jnp.bfloat16), "tensor").astype(jnp.float32),
            lax.psum(partials[3].astype(jnp.bfloat16), "tensor").astype(jnp.float32),
        )
        iterates = [ns_update(iterate, gram_sum) for iterate, gram_sum in zip(iterates, grams)]
    orth = (
        iterates[0].reshape(3, columns, width).transpose(0, 2, 1),
        iterates[1],
        iterates[2].T,
        iterates[3],
    )
    new_qkv, new_out, new_up, new_down = [
        weight - factor * step for weight, factor, step in zip(weights, factors, orth)
    ]
    new_heads = vector_step(
        head_bias, new_mom_heads, (totals[4:6] / (columns * tensor_size))[:, None]
    )
    new_ff = vector_step(ff_bias, new_mom_ff, totals[6] / (ff_cols * tensor_size))
    new_params = vector_step(
        row_params,
        new_mom_params,
        jnp.mean(new_mom_params * new_mom_params, axis=-1, keepdims=True),
    )
    return (
        output_rows.astype(jnp.bfloat16),
        grad_inputs.astype(jnp.bfloat16),
        new_mom_qkv,
        new_qkv,
        new_qkv.astype(jnp.bfloat16),
        new_mom_out,
        new_out,
        new_out.astype(jnp.bfloat16),
        new_mom_up,
        new_up,
        new_up.astype(jnp.bfloat16),
        new_mom_down,
        new_down,
        new_down.astype(jnp.bfloat16),
        new_mom_heads,
        new_heads,
        new_mom_ff,
        new_ff,
        new_mom_params,
        new_params,
    )


def solution(mesh):
    placed = (
        P("dp", None),
        P("dp", None),
        P("dp", None),
        P(None, None, "tensor"),
        P("tensor", None),
        P(None, "tensor"),
        P("tensor", None),
        P(None, "tensor"),
        P("tensor"),
        P(),
        P(None, None, "tensor"),
        P("tensor", None),
        P(None, "tensor"),
        P("tensor", None),
        P(None, "tensor"),
        P("tensor"),
        P(),
    )
    return jax.shard_map(
        local,
        mesh=mesh,
        in_specs=placed,
        out_specs=(
            P("dp", None),
            P("dp", None),
            P(None, None, "tensor"),
            P(None, None, "tensor"),
            P(None, None, "tensor"),
            P("tensor", None),
            P("tensor", None),
            P("tensor", None),
            P(None, "tensor"),
            P(None, "tensor"),
            P(None, "tensor"),
            P("tensor", None),
            P("tensor", None),
            P("tensor", None),
            P(None, "tensor"),
            P(None, "tensor"),
            P("tensor"),
            P("tensor"),
            P(),
            P(),
        ),
        check_vma=False,
    )
```

profile of v0, /device:TPU:13, one launch (start us, length us, event | category | flops | bytes accessed | tf_op | source)
XLA Modules:
  0.0 1470.8 jit_solution(3367583528718260006)
XLA Ops:
  14.9 43.7 %all-reduce.17.cloned.1.call-done = bf16[512,768]{1,0:T(8,128)(2,1)} async-done(((bf16[512,768]{1,0:T(8,128)(2,1)}), bf16[512,768]{1,0:T(8,128)(2,1)}) %all-reduce.17.cloned.1.call-update) | async-done | bytes 786448 | tf_op jit(solution)/shard_map/psum | solution.py:129
  62.3 5.0 fusion.15
  69.9 43.1 %all-reduce.19.cloned.1.call-done = bf16[512,768]{1,0:T(8,128)(2,1)} async-done(((bf16[512,768]{1,0:T(8,128)(2,1)}), bf16[512,768]{1,0:T(8,128)(2,1)}) %all-reduce.19.cloned.1.call-update) | async-done | bytes 786448 | tf_op jit(solution)/shard_map/psum | solution.py:138
  124.8 3.0 convolution_convert_fusion.19
  129.6 38.0 %all-reduce.21.cloned.1.call-done = bf16[512,768]{1,0:T(8,128)(2,1)} async-done(((bf16[512,768]{1,0:T(8,128)(2,1)}), bf16[512,768]{1,0:T(8,128)(2,1)}) %all-reduce.21.cloned.1.call-update) | async-done | bytes 786448 | tf_op jit(solution)/shard_map/psum | solution.py:152
  188.9 40.6 %all-reduce = (f32[2,768]{1,0:T(2,128)S(1)}, f32[3072]{0:T(1024)S(1)}, f32[6,768]{1,0:T(8,128)}) all-reduce(f32[2,768]{1,0:T(2,128)S(1)} %dynamic_update_slice.6, f32[3072]{0:T(1024)S(1)} %dynamic_update_slice.7, f32[6,768]{1,0:T(8,128)S(1)} %stack.75), channel_id=1, replica_groups=mesh['dp'=8,'tensor'=4] {'dp','tensor'}, use_global_device_ids=true, to_apply=%region_25.26 | all-reduce | flops 9216 | bytes 73728 | tf_op jit(solution)/shard_map/psum | solution.py:217
  230.4 26.7 %all-reduce.23.cloned.1.call-done = (bf16[3,768,192]{1,2,0:T(8,128)(2,1)}, bf16[192,768]{1,0:T(8,128)(2,1)}, bf16[768,768]{1,0:T(8,128)(2,1)}, bf16[768,768]{1,0:T(8,128)(2,1)}) async-done(((bf16[3,768,192]{1,2,0:T(8,128)(2,1)}, bf16[192,768]{1,0:T(8,128)(2,1)}, bf16[768,768]{1,0:T(8,128)(2,1)}, bf16[768,768]{1,0:T(8,128)(2,1)}), (bf16[3,768,192]{1,2,0:T(8,128)(2,1)}, bf16[192,768]{1,0:T(8,128)(2,1)}, ...) | async-done | bytes 3538960 | tf_op jit(solution)/shard_map/psum | solution.py:231
  257.0 3.0 multiply_reduce_fusion.2
  267.5 3.3 concatenate.3
  270.8 7.2 psum.234
  279.5 7.0 bitcast_convert_fusion
  288.7 3.1 convolution_convert_fusion.14
  291.9 7.1 convolution_convert_fusion.9
  298.9 7.0 convolution_convert_fusion.4
  306.2 173.4 %all-reduce.33.cloned.1.call-done = (bf16[768,768]{1,0:T(8,128)(2,1)}, bf16[768,768]{1,0:T(8,128)(2,1)}, bf16[768,768]{1,0:T(8,128)(2,1)}, bf16[768,768]{1,0:T(8,128)(2,1)}) async-done(((bf16[768,768]{1,0:T(8,128)(2,1)}, bf16[768,768]{1,0:T(8,128)(2,1)}, bf16[768,768]{1,0:T(8,128)(2,1)}, bf16[768,768]{1,0:T(8,128)(2,1)}), (bf16[768,768]{1,0:T(8,128)(2,1)}, bf16[768,768]{1,0:T(8,128)(2,1)}, ...) | async-done | bytes 4718608 | tf_op jit(solution)/shard_map/psum | solution.py:253
  479.6 3.7 fusion.114
  486.1 7.0 convolution_convert_fusion.18
  496.2 3.1 convolution_convert_fusion.13
  499.3 4.7 fusion.102
  504.0 3.0 copy.77
  507.0 7.2 fusion.8
  514.3 6.9 convolution_convert_fusion.8
  521.2 3.1 fusion.100
  524.3 3.7 multiply_add_fusion.3
  529.5 7.4 convolution_convert_fusion.3
  537.3 171.6 %all-reduce.31.cloned.1.call-done = (bf16[768,768]{1,0:T(8,128)(2,1)}, bf16[768,768]{1,0:T(8,128)(2,1)}, bf16[768,768]{1,0:T(8,128)(2,1)}, bf16[768,768]{1,0:T(8,128)(2,1)}) async-done(((bf16[768,768]{1,0:T(8,128)(2,1)}, bf16[768,768]{1,0:T(8,128)(2,1)}, bf16[768,768]{1,0:T(8,128)(2,1)}, bf16[768,768]{1,0:T(8,128)(2,1)}), (bf16[768,768]{1,0:T(8,128)(2,1)}, bf16[768,768]{1,0:T(8,128)(2,1)}, ...) | async-done | bytes 4718608 | tf_op jit(solution)/shard_map/psum | solution.py:253
  708.9 3.7 fusion.115
  715.4 7.0 convolution_convert_fusion.17
  724.5 3.1 convolution_convert_fusion.12
  727.6 4.8 fusion.123
  732.4 3.0 copy.81
  735.4 7.3 add_add_fusion.2
  742.8 6.8 convolution_convert_fusion.7
  749.6 3.1 fusion.127
  752.7 3.9 multiply_add_fusion.2
  758.1 7.4 convolution_convert_fusion.2
  765.8 171.9 %all-reduce.29.cloned.1.call-done = (bf16[768,768]{1,0:T(8,128)(2,1)}, bf16[768,768]{1,0:T(8,128)(2,1)}, bf16[768,768]{1,0:T(8,128)(2,1)}, bf16[768,768]{1,0:T(8,128)(2,1)}) async-done(((bf16[768,768]{1,0:T(8,128)(2,1)}, bf16[768,768]{1,0:T(8,128)(2,1)}, bf16[768,768]{1,0:T(8,128)(2,1)}, bf16[768,768]{1,0:T(8,128)(2,1)}), (bf16[768,768]{1,0:T(8,128)(2,1)}, bf16[768,768]{1,0:T(8,128)(2,1)}, ...) | async-done | bytes 4718608 | tf_op jit(solution)/shard_map/psum | solution.py:253
  937.6 3.7 fusion.116
  944.1 7.2 convolution_convert_fusion.16
  953.6 3.1 convolution_convert_fusion.11
  956.8 3.4 fusion.124
  963.5 8.4 add_add_fusion.1
  971.9 6.8 convolution_convert_fusion.6
  978.8 3.3 fusion.128
  982.1 3.5 multiply_add_fusion.1
  987.0 7.3 convolution_convert_fusion.1
  998.5 168.0 %all-reduce.27.cloned.1.call-done = (bf16[768,768]{1,0:T(8,128)(2,1)}, bf16[768,768]{1,0:T(8,128)(2,1)}, bf16[768,768]{1,0:T(8,128)(2,1)}, bf16[768,768]{1,0:T(8,128)(2,1)}) async-done(((bf16[768,768]{1,0:T(8,128)(2,1)}, bf16[768,768]{1,0:T(8,128)(2,1)}, bf16[768,768]{1,0:T(8,128)(2,1)}, bf16[768,768]{1,0:T(8,128)(2,1)}), (bf16[768,768]{1,0:T(8,128)(2,1)}, bf16[768,768]{1,0:T(8,128)(2,1)}, ...) | async-done | bytes 4718608 | tf_op jit(solution)/shard_map/psum | solution.py:253
  1166.5 4.9 fusion.125
  1172.8 4.6 fusion.126
  1177.3 3.4 copy.91
  1180.8 4.3 fusion.117
  1187.8 7.2 convolution_convert_fusion.15
  1197.1 3.1 convolution_convert_fusion.10
  1200.2 3.1 fusion.129
  1203.4 3.5 multiply_add_fusion
  1208.3 7.5 convolution_convert_fusion
  1215.9 7.7 convolution_convert_fusion.5
  1227.2 194.3 %all-reduce.25.cloned.1.call-done = (bf16[512,768]{1,0:T(8,128)(2,1)}, bf16[768,768]{1,0:T(8,128)(2,1)}, bf16[768,768]{1,0:T(8,128)(2,1)}, bf16[768,768]{1,0:T(8,128)(2,1)}, bf16[768,768]{1,0:T(8,128)(2,1)}) async-done(((bf16[512,768]{1,0:T(8,128)(2,1)}, bf16[768,768]{1,0:T(8,128)(2,1)}, bf16[768,768]{1,0:T(8,128)(2,1)}, bf16[768,768]{1,0:T(8,128)(2,1)}, bf16[768,768]{1,0:T(8,128)(2,1)}), ...) | async-done | bytes 5505040 | tf_op jit(solution)/shard_map/psum | solution.py:189
  1426.7 3.2 add_multiply_fusion
  1434.7 3.7 fusion.101
  1441.5 3.4 copy.96
  1444.9 3.1 fusion.130
  1448.1 5.3 fusion.113
  1453.4 10.7 fusion.112
  (363 shorter events, 109.2 us)
Async XLA Ops:
  7.2 51.4 %all-reduce.17.cloned.1.call-start = ((), (), s32[]{:S(2)}) async-start(), calls=%async_computation | async-start | bytes 1572864 | tf_op jit(solution)/shard_map/psum | solution.py:129
  14.1 98.8 %all-reduce.19.cloned.1.call-start = ((), (), s32[]{:S(2)}) async-start(), calls=%async_computation.1 | async-start | bytes 1572864 | tf_op jit(solution)/shard_map/psum | solution.py:138
  62.2 5.9 copy-start.39
  69.8 97.8 %all-reduce.21.cloned.1.call-start = ((), (), s32[]{:S(2)}) async-start(), calls=%async_computation.2 | async-start | bytes 1572864 | tf_op jit(solution)/shard_map/psum | solution.py:152
  116.6 3.5 copy-start.118
  117.9 49.7 %copy-start.29 = (f32[512,768]{1,0:T(8,128)}, f32[512,768]{1,0:T(8,128)S(1)}, u32[]{:S(2)}) copy-start(f32[512,768]{1,0:T(8,128)S(1)} %get-tuple-element.80) | copy-start | bytes 4718596
  124.5 132.5 %all-reduce.23.cloned.1.call-start = ((), (), s32[]{:S(2)}) async-start(), calls=%async_computation.3 | async-start | bytes 7077888 | tf_op jit(solution)/shard_map/psum | solution.py:231
  170.8 16.5 %copy-start.20 = (f32[512,768]{1,0:T(8,128)}, f32[512,768]{1,0:T(8,128)S(1)}, u32[]{:S(2)}) copy-start(f32[512,768]{1,0:T(8,128)S(1)} %subtract_multiply_fusion) | copy-start | bytes 4718596
  182.1 297.5 %all-reduce.33.cloned.1.call-start = ((), (), s32[]{:S(2)}) async-start(), calls=%async_computation.8 | async-start | bytes 9437184 | tf_op jit(solution)/shard_map/psum | solution.py:253
  182.1 4.7 copy-start.113
  184.5 44.9 %copy-start.114 = (f32[2,192]{1,0:T(2,128)S(1)}, f32[2,192]{1,0:T(2,128)}, u32[]{:S(2)}) copy-start(f32[2,192]{1,0:T(2,128)} %param.31) | copy-start | bytes 4612
  184.5 45.1 %copy-start.112 = (f32[768]{0:T(1024)S(1)}, f32[768]{0:T(1024)}, u32[]{:S(2)}) copy-start(f32[768]{0:T(1024)} %param.32) | copy-start | bytes 9220
  229.7 996.3 %copy-start.107 = (f32[2,192]{1,0:T(2,128)}, f32[2,192]{1,0:T(2,128)S(1)}, u32[]{:S(2)}) copy-start(f32[2,192]{1,0:T(2,128)S(1)} %get-tuple-element.69) | copy-start | bytes 4612
  230.4 996.2 %copy-start.103 = (f32[768]{0:T(1024)}, f32[768]{0:T(1024)S(1)}, u32[]{:S(2)}) copy-start(f32[768]{0:T(1024)S(1)} %get-tuple-element.67) | copy-start | bytes 9220
  257.0 4.5 copy-start.70
  260.0 19.4 %copy-start.46 = (f32[3,768,192]{1,2,0:T(8,128)}, f32[3,768,192]{1,2,0:T(8,128)S(1)}, u32[]{:S(2)}) copy-start(f32[3,768,192]{1,2,0:T(8,128)S(1)} %get-tuple-element.77) | copy-start | bytes 5308420
  279.5 9.2 copy-start.92
  286.5 5.4 copy-start.30
  291.9 7.1 copy-start.72
  305.9 403.0 %all-reduce.31.cloned.1.call-start = ((), (), s32[]{:S(2)}) async-start(), calls=%async_computation.7 | async-start | bytes 9437184 | tf_op jit(solution)/shard_map/psum | solution.py:253
  479.6 3.8 copy-start.57
  486.0 7.0 copy-start.93
  486.0 7.0 copy-start.117
  493.9 5.3 copy-start.116
  514.3 6.9 copy-start.27
  514.3 6.9 copy-start.73
  514.3 6.9 copy-start.115
  536.9 400.8 %all-reduce.29.cloned.1.call-start = ((), (), s32[]{:S(2)}) async-start(), calls=%async_computation.6 | async-start | bytes 9437184 | tf_op jit(solution)/shard_map/psum | solution.py:253
  708.9 3.8 copy-start.58
  715.4 7.0 copy-start.38
  715.4 7.0 copy-start.62
  723.3 4.3 copy-start.82
  742.7 6.9 copy-start.10
  742.7 6.9 copy-start.19
  742.8 6.9 copy-start.65
  765.5 401.0 %all-reduce.27.cloned.1.call-start = ((), (), s32[]{:S(2)}) async-start(), calls=%async_computation.5 | async-start | bytes 9437184 | tf_op jit(solution)/shard_map/psum | solution.py:253
  937.6 3.8 copy-start.59
  944.1 7.2 copy-start.8
  944.1 7.2 copy-start.63
  952.2 4.5 copy-start.83
  953.6 3.1 copy-start.11
  971.9 6.9 copy-start.5
  971.9 6.9 copy-start.66
  994.4 427.1 %all-reduce.25.cloned.1.call-start = ((), (), s32[]{:S(2)}) async-start(), calls=%async_computation.4 | async-start | bytes 11010048 | tf_op jit(solution)/shard_map/psum | solution.py:189
  1166.5 6.3 copy-start.86
  1180.7 4.4 copy-start.9
  1180.8 4.4 copy-start.56
  1187.8 7.2 copy-start.6
  1187.8 7.2 copy-start.61
  1195.9 4.3 copy-start.64
  1208.3 7.5 copy-start.12
  1208.3 7.5 copy-start.15
  1224.5 202.2 %copy-start.97 = (f32[6,768]{1,0:T(8,128)}, f32[6,768]{1,0:T(8,128)S(1)}, u32[]{:S(2)}) copy-start(f32[6,768]{1,0:T(8,128)S(1)} %get-tuple-element.63) | copy-start | bytes 55300
  1426.7 3.2 copy-start.45
  1429.9 4.7 copy-start.52
  1441.5 3.4 copy-start.1
  1441.5 3.4 copy-start.54
  1444.9 8.4 copy-start.32
  1444.9 8.4 copy-start.53
  1448.0 5.3 copy-start.14
  1448.0 5.3 copy-start.17
  1448.0 5.3 copy-start.23
  1448.1 5.3 copy-start.24
  1448.1 5.3 copy-start.26
  (64 other events, 115.2 us)
Sparse Core Ops, SparseCore 0:
  14.3 44.2 all-reduce.16
  70.0 42.9 all-reduce.18
  124.6 42.9 all-reduce.20
  182.2 74.7 all-reduce.22
  306.1 173.5 all-reduce.32
  537.0 171.9 all-reduce.30
  765.6 171.9 all-reduce.28
  994.5 171.9 all-reduce.26
  1223.8 197.6 all-reduce.24
where the time goes:
time: 1480 us; the launch traced here: 1470 us
  waiting for transfers between devices  1030 us (70%)
  matrix products  290 us (20%)
  blocking collectives  47.8 us (3%)
  local copies, waits for them, and re-layouts  45.3 us (3%)
  other arithmetic  36.4 us (2%)
  between operations  19.2 us (1%)
    psum x4, waiting for transfers between devices, local(): lax.psum(partials[0].astype(jnp.bfloat16), 'tensor').astype(jnp.float32)  685 us
    psum x1, waiting for transfers between devices, local(): lax.psum(back_terms.astype(jnp.bfloat16), 'tensor').astype(jnp.float32)  194 us
    dot_general x20, matrix products, gram_of(): lax.dot_general(block, block, (((0,), (0,)), ((), ())), precision=HIGHEST...  123 us
    dot_general x20, matrix products, ns_update(): second = jnp.dot(product, gram_sum, precision=HIGHEST)  79 us
    dot_general x20, matrix products, ns_update(): product = jnp.dot(iterate, gram_sum, precision=HIGHEST)  59.8 us
    psum x1, waiting for transfers between devices, local(): lax.psum(jnp.dot(context_low, wo_low, preferred_element_type=jnp.float32)...  43.7 us
    psum x1, waiting for transfers between devices, local(): lax.psum(jnp.dot(activated_low, wd_low, preferred_element_type=jnp.float3...  43.1 us
    psum x1, blocking collectives, local(): lax.psum((param_grad, heads_full, ff_full), ('dp', 'tensor'))  40.6 us
  transfers between devices with their start and end apart: 9, of which 9 were waited for; matrix products, arithmetic and copies ran while one was open for 1% of the time, Pallas kernels for 0%

commit v1 on v0

v1 whole, which is shorter than its diff:
```python
import functools
import math

import jax
import jax.numpy as jnp
from jax import lax
from jax.experimental import pallas as pl
from jax.experimental.pallas import tpu as pltpu
from jax.sharding import PartitionSpec as P

HD = 64
EPS_NORM = 1e-05
coef_a = 3.4445
coef_b = -4.775
coef_c = 2.0315
BF = jnp.bfloat16
F32 = jnp.float32
MESH = pl.DeviceIdType.MESH
SUBS = 2
VMEM_LIMIT = 56 * 1024 * 1024


def remote(src, dst, send_sem, recv_sem, device):
    return pltpu.make_async_remote_copy(
        src_ref=src,
        dst_ref=dst,
        send_sem=send_sem,
        recv_sem=recv_sem,
        device_id=device,
        device_id_type=MESH,
    )


def greet(devices):
    barrier = pltpu.get_barrier_semaphore()
    for device in devices:
        pl.semaphore_signal(barrier, inc=1, device_id=device, device_id_type=MESH)
    pl.semaphore_wait(barrier, len(devices))


def z_peers(t):
    return [{"tensor": (t + k) % 4} for k in range(1, 4)]


def line_scratch(rows, width, dtype):
    part = rows // 4
    return [
        pltpu.VMEM((part, width), dtype),
        pltpu.VMEM((part, width), dtype),
        pltpu.VMEM((2 * part, width), dtype),
        pltpu.VMEM((2 * part, width), dtype),
        pltpu.SemaphoreType.DMA((8 * SUBS,)),
        pltpu.SemaphoreType.DMA((8 * SUBS,)),
    ]


def line_sum(t, x, o, scratch):
    raw, cmb, fwd, mix, ssem, rsem = scratch
    part = raw.shape[0]
    half = part // SUBS
    subs = range(SUBS)
    mate = t + 1 - 2 * (t % 2)
    outer = (t % 3) == 0
    inner = (t % 3) != 0

    def at(ref, chunk, s):
        return ref.at[pl.ds(pl.multiple_of(chunk * part + s * half, half), half)]

    def to(index, src, dst, recv, device):
        return remote(src, dst, ssem.at[index], rsem.at[recv], {"tensor": device})

    def ag_sem(chunk, s):
        return (4 + chunk) * SUBS + s

    def o_far(s):
        return to(s, at(x, 3 - t, s), at(fwd, 0, s), 2 * SUBS + s, mate)

    def o_near(s):
        return to(SUBS + s, at(x, 3 - mate, s), at(fwd, 1, s), 3 * SUBS + s, mate)

    def o_raw(s):
        return to(2 * SUBS + s, at(x, mate, s), at(raw, 0, s), s, mate)

    def o_own(s):
        return to(3 * SUBS + s, at(o, t, s), at(o, t, s), ag_sem(t, s), mate)

    def i_raw(s):
        return to(s, at(x, mate, s), at(raw, 0, s), s, mate)

    def i_far(s):
        return to(SUBS + s, at(mix, 0, s), at(cmb, 0, s), SUBS + s, 3 - mate)

    def i_near(s):
        return to(2 * SUBS + s, at(mix, 1, s), at(cmb, 0, s), SUBS + s, 3 - t)

    def i_ag(place, chunk, s, device):
        return to(place * SUBS + s, at(o, chunk, s), at(o, chunk, s), ag_sem(chunk, s), device)

    def got(dst, recv):
        remote(dst, dst, ssem.at[0], rsem.at[recv], {"tensor": mate}).wait_recv()

    def add(dst, *terms):
        total = terms[0][...].astype(F32)
        for term in terms[1:]:
            total = total + term[...].astype(F32)
        dst[...] = total.astype(dst.dtype)

    def start():
        @pl.when(outer)
        def _():
            for build in (o_far, o_near, o_raw):
                for s in subs:
                    build(s).start()

        @pl.when(inner)
        def _():
            for s in subs:
                i_raw(s).start()

    def combine():
        @pl.when(inner)
        def _():
            for slot, chunk, build in ((0, 3 - mate, i_far), (1, 3 - t, i_near)):
                for s in subs:
                    got(at(fwd, slot, s), (2 + slot) * SUBS + s)
                    add(at(mix, slot, s), at(fwd, slot, s), at(x, chunk, s))
                    build(s).start()

    def settle():
        for s in subs:
            got(at(raw, 0, s), s)
            got(at(cmb, 0, s), SUBS + s)
            add(at(o, t, s), at(x, t, s), at(raw, 0, s), at(cmb, 0, s))

            @pl.when(outer)
            def _(s=s):
                o_own(s).start()

            @pl.when(inner)
            def _(s=s):
                i_ag(3, t, s, 3 - t).start()
                i_ag(4, t, s, mate).start()

    def pass_on():
        @pl.when(inner)
        def _():
            for s in subs:
                got(at(o, mate, s), ag_sem(mate, s))
                i_ag(5, mate, s, 3 - t).start()
            for s in subs:
                got(at(o, 3 - t, s), ag_sem(3 - t, s))
                i_ag(6, 3 - t, s, mate).start()
            for s in subs:
                got(at(o, 3 - mate, s), ag_sem(3 - mate, s))
                i_ag(7, 3 - mate, s, mate).start()

    def finish():
        @pl.when(outer)
        def _():
            for chunk in (mate, 3 - mate, 3 - t):
                for s in subs:
                    got(at(o, chunk, s), ag_sem(chunk, s))
            for build in (o_far, o_near, o_raw, o_own):
                for s in subs:
                    build(s).wait_send()

        @pl.when(inner)
        def _():
            for s in subs:
                for build in (i_raw, i_far, i_near):
                    build(s).wait_send()
                i_ag(3, t, s, 3 - t).wait_send()
                i_ag(4, t, s, mate).wait_send()
                i_ag(5, mate, s, 3 - t).wait_send()
                i_ag(6, 3 - t, s, mate).wait_send()
                i_ag(7, 3 - mate, s, mate).wait_send()

    return [start, combine, settle, pass_on, finish]


def line_kernel(x, o, *scratch):
    t = lax.axis_index("tensor")
    greet(z_peers(t))
    for step in line_sum(t, x, o, scratch):
        step()


def params(collective_id):
    return pltpu.CompilerParams(
        collective_id=collective_id, has_side_effects=True, vmem_limit_bytes=VMEM_LIMIT
    )


IN_VMEM = pl.BlockSpec(memory_space=pltpu.VMEM)
IN_ANY = pl.BlockSpec(memory_space=pl.ANY)


def sum_tensor(partial, collective_id):
    rows, width = partial.shape
    return pl.pallas_call(
        line_kernel,
        out_shape=jax.ShapeDtypeStruct(partial.shape, partial.dtype),
        in_specs=[IN_VMEM],
        out_specs=IN_VMEM,
        scratch_shapes=line_scratch(rows, width, partial.dtype),
        compiler_params=params(collective_id),
        name="sum_tensor",
    )(partial)


def plane_scratch(count, rows, width):
    pairs = count // 2
    side = width // 2
    block = rows // pairs
    return [
        pltpu.VMEM((rows, side), BF),
        pltpu.VMEM((rows, side), BF),
        pltpu.VMEM((pairs, block, side), BF),
        pltpu.SemaphoreType.DMA((5, pairs)),
        pltpu.SemaphoreType.DMA((4, pairs)),
    ]


def plane_sum(count, p, x, o, scratch):
    from_mate, paired, slots, ssem, rsem = scratch
    pairs = count // 2
    side = from_mate.shape[1]
    block = slots.shape[1]
    pair = p // 2
    core = p % 2
    mate = {"dp": p + 1 - 2 * core}

    def rows_of(index):
        return pl.ds(pl.multiple_of(index * block, block), block)

    def cols_of(which):
        return pl.ds(pl.multiple_of(which * side, side), side)

    def after(k):
        return (pair + k) % pairs

    def before(k):
        return (pair + pairs - k) % pairs

    def give(k):
        spot = rows_of(after(k))
        return remote(
            x.at[spot, cols_of(1 - core)], from_mate.at[spot], ssem.at[0, k % pairs], rsem.at[0, k % pairs], mate
        )

    def hand(k):
        spot = rows_of(after(k))
        return remote(
            paired.at[spot], slots.at[k], ssem.at[1, k], rsem.at[1, k], {"dp": 2 * after(k) + core}
        )

    def spread(k):
        spot = o.at[rows_of(pair), cols_of(core)]
        return remote(spot, spot, ssem.at[2, k], rsem.at[2, k], {"dp": 2 * after(k) + core})

    def share(k):
        spot = o.at[rows_of(before(k)), cols_of(core)]
        return remote(spot, spot, ssem.at[3, k], rsem.at[3, k], mate)

    def start():
        for k in range(1, pairs + 1):
            give(k).start()

    def pair_up():
        for k in range(1, pairs + 1):
            spot = rows_of(after(k))
            give(k).wait_recv()
            total = x[spot, cols_of(core)].astype(F32) + from_mate[spot].astype(F32)
            paired[spot] = total.astype(BF)
            if k < pairs:
                hand(k).start()

    def settle():
        spot = rows_of(pair)
        total = paired[spot].astype(F32)
        for k in range(1, pairs):
            hand(k).wait_recv()
            total = total + slots[k].astype(F32)
        o[spot, cols_of(core)] = total.astype(BF)
        for k in range(1, pairs):
            spread(k).start()
        share(0).start()

    def pass_on():
        for k in range(1, pairs):
            spot = o.at[rows_of(before(k)), cols_of(core)]
            remote(spot, spot, ssem.at[2, k], rsem.at[2, k], mate).wait_recv()
            share(k).start()

    def finish():
        for k in range(pairs):
            spot = o.at[rows_of(before(k)), cols_of(1 - core)]
            remote(spot, spot, ssem.at[3, k], rsem.at[3, k], mate).wait_recv()
        for k in range(1, pairs + 1):
            give(k).wait_send()
        for k in range(1, pairs):
            hand(k).wait_send()
            spread(k).wait_send()
        for k in range(pairs):
            share(k).wait_send()

    return [start, pair_up, settle, pass_on, finish]


def vector_scratch(count, shape):
    return [
        pltpu.VMEM((count,) + shape, F32),
        pltpu.SemaphoreType.DMA((count,)),
        pltpu.SemaphoreType.DMA((count,)),
    ]


def vector_sum(axis, count, p, v, o, scratch):
    slots, ssem, rsem = scratch

    def send(k):
        return remote(v, slots.at[p], ssem.at[k], rsem.at[k], {axis: (p + k) % count})

    def start():
        slots[p] = v[...]
        for k in range(1, count):
            send(k).start()

    def finish():
        for k in range(1, count):
            spot = slots.at[(p + count - k) % count]
            remote(v, spot, ssem.at[k], rsem.at[k], {axis: (p + k) % count}).wait_recv()
        total = slots[0]
        for k in range(1, count):
            total = total + slots[k]
        o[...] = total
        for k in range(1, count):
            send(k).wait_send()

    return [start, finish]


def dp_kernel(count, x, v, o, vo, *scratch):
    p = lax.axis_index("dp")
    greet([{"dp": (p + k) % count} for k in range(1, count)])
    plane = plane_sum(count, p, x, o, scratch[:5])
    vector = vector_sum("dp", count, p, v, vo, scratch[5:])
    vector[0]()
    for step in plane:
        step()
    vector[1]()


def sum_dp(count, grads, vectors, collective_id):
    rows, width = grads.shape
    return pl.pallas_call(
        functools.partial(dp_kernel, count),
        out_shape=(
            jax.ShapeDtypeStruct(grads.shape, BF),
            jax.ShapeDtypeStruct(vectors.shape, F32),
        ),
        in_specs=[IN_VMEM, IN_VMEM],
        out_specs=(IN_VMEM, IN_VMEM),
        scratch_shapes=plane_scratch(count, rows, width) + vector_scratch(count, vectors.shape),
        compiler_params=params(collective_id),
        name="sum_dp",
    )(grads, vectors)


def dp_only_kernel(count, x, o, *scratch):
    p = lax.axis_index("dp")
    greet([{"dp": (p + k) % count} for k in range(1, count)])
    for step in plane_sum(count, p, x, o, scratch):
        step()


def sum_dp_only(count, grads, collective_id):
    rows, width = grads.shape
    return pl.pallas_call(
        functools.partial(dp_only_kernel, count),
        out_shape=jax.ShapeDtypeStruct(grads.shape, BF),
        in_specs=[IN_VMEM],
        out_specs=IN_VMEM,
        scratch_shapes=plane_scratch(count, rows, width),
        compiler_params=params(collective_id),
        name="sum_dp_only",
    )(grads)


def cut(values):
    high = values.astype(BF)
    return high, (values - high.astype(F32)).astype(BF)


def dot3(lh, ll, rh, rl, dims=(((1,), (0,)), ((), ()))):
    def dot(left, right):
        return lax.dot_general(left, right, dims, preferred_element_type=F32)

    return dot(lh, rh) + (dot(lh, rl) + dot(ll, rh))


def muon_kernel(
    count, sizes,
    mq, mo, mu, md, ga, gb, vs,
    xo, vt,
    zf, gf, zh, zl, gx, go, gp, af, ah, al, dh, dl, sf, sh, sl, xf, lsem, psem, asem_s, asem_r, *scratch,
):
    p = lax.axis_index("dp")
    t = lax.axis_index("tensor")
    width = zf.shape[1]
    group = count // 4
    which = p // group
    core = p % 2
    pairs = count // 2
    pair = p // 2
    mate = {"dp": p + 1 - 2 * core}
    share = xf.shape[0]
    tile = width // 3
    greet(z_peers(t) + [{"dp": (p + k) % count} for k in range(1, count)])
    vector = vector_sum("tensor", 4, t, vs, vt, scratch[6:])
    vector[0]()
    qkv_rows, out_rows, _, _ = sizes
    gsrc = (
        (ga, 0, qkv_rows), (ga, qkv_rows, out_rows), (gb, 0, width), (gb, width, width)
    )
    for index, moment in enumerate((mq, mo, mu, md)):
        grads, first, rows = gsrc[index]

        @pl.when(which == index)
        def _(moment=moment, grads=grads, first=first, rows=rows):
            one = pltpu.make_async_copy(moment, zf.at[pl.ds(0, rows)], lsem.at[0])
            two = pltpu.make_async_copy(
                grads.at[pl.ds(first, rows)], gf.at[pl.ds(0, rows)], lsem.at[1]
            )
            one.start()
            two.start()
            if rows < width:
                zf[pl.ds(rows, width - rows)] = jnp.zeros((width - rows, width), F32)
                gf[pl.ds(rows, width - rows)] = jnp.zeros((width - rows, width), BF)
            one.wait()
            two.wait()

    for i in range(3):
        spot = pl.ds(i * tile, tile)
        z = 0.5 * zf[spot] + gf[spot].astype(F32)
        zf[spot] = z
        zh[spot], zl[spot] = cut(z)

    def cols(index):
        return pl.ds(pl.multiple_of(index * tile, tile), tile)

    over_rows = (((0,), (0,)), ((), ()))
    for j, (row, col) in enumerate(((core, core), (core, core + 1), (2 * core, 2))):
        gx[:, pl.ds(j * tile, tile)] = dot3(
            zh[:, cols(row)], zl[:, cols(row)], zh[:, cols(col)], zl[:, cols(col)], over_rows
        )
    for step in line_sum(t, gx, go, scratch[:6]):
        step()
    swap = remote(go, gp, psem.at[0], psem.at[1], mate)
    swap.start()
    swap.wait()
    diagonal = lax.broadcasted_iota(jnp.int32, (tile, tile), 0) == lax.broadcasted_iota(
        jnp.int32, (tile, tile), 1
    )

    def upper(first, second):
        trace = jnp.float32(0.0)
        for block in (first[:, 0:tile], second[:, 0:tile], second[:, 2 * tile :]):
            trace = trace + jnp.sum(jnp.where(diagonal, block, 0.0))
        inverse = 1.0 / (jnp.sqrt(jnp.full((1, 1), trace, F32)) + 1e-07)
        scale = inverse * inverse
        blocks = (
            (0, 0, first, 0), (0, 1, first, 1), (0, 2, first, 2),
            (1, 1, second, 0), (1, 2, second, 1), (2, 2, second, 2),
        )
        for row, col, source, j in blocks:
            block = source[:, j * tile : (j + 1) * tile] * scale
            for r, c, value in ((row, col, block),) + (((col, row, block.T),) if row != col else ()):
                spot = (pl.ds(r * tile, tile), pl.ds(c * tile, tile))
                af[spot] = value
                ah[spot], al[spot] = cut(value)
        rank = p % group
        xf[...] = zf[pl.ds(pl.multiple_of(rank * share, share), share)] * inverse

    @pl.when(core == 0)
    def _():
        upper(go, gp)

    @pl.when(core == 1)
    def _():
        upper(gp, go)

    vector[1]()

    def make_d():
        for i in range(3):
            spot = pl.ds(i * tile, tile)
            value = coef_b * af[spot] + coef_c * dot3(ah[spot], al[spot], ah[...], al[...])
            dh[spot], dl[spot] = cut(value)

    def move_x():
        xh, xl = cut(xf[...])
        xf[...] = coef_a * xf[...] + dot3(xh, xl, dh[...], dl[...])

    def sweep(k, carry):
        make_d()
        move_x()
        for i in range(3):
            spot = pl.ds(i * tile, tile)
            value = coef_a * af[spot] + dot3(ah[spot], al[spot], dh[...], dl[...])
            sf[spot] = value
            sh[spot], sl[spot] = cut(value)
        for i in range(3):
            spot = pl.ds(i * tile, tile)
            value = coef_a * sf[spot] + dot3(sh[spot], sl[spot], dh[...], dl[...])
            af[spot] = value
            ah[spot], al[spot] = cut(value)
        return carry

    lax.fori_loop(0, 4, sweep, 0)
    make_d()
    move_x()

    def rows_of(device):
        return xo.at[pl.ds(pl.multiple_of(device * share, share), share)]

    def after(k):
        return 2 * ((pair + k) % pairs) + core

    def before(k):
        return 2 * ((pair + pairs - k) % pairs) + core

    def send(k):
        return remote(rows_of(p), rows_of(p), asem_s.at[0, k], asem_r.at[0, k], {"dp": after(k)})

    def hand(k):
        spot = rows_of(before(k))
        return remote(spot, spot, asem_s.at[1, k], asem_r.at[1, k], mate)

    xo[pl.ds(pl.multiple_of(p * share, share), share)] = xf[...].astype(BF)
    for k in range(1, pairs):
        send(k).start()
    hand(0).start()
    for k in range(1, pairs):
        spot = rows_of(before(k))
        remote(spot, spot, asem_s.at[0, k], asem_r.at[0, k], mate).wait_recv()
        hand(k).start()
    for k in range(pairs):
        spot = rows_of(before(k) + 1 - 2 * core)
        remote(spot, spot, asem_s.at[1, k], asem_r.at[1, k], mate).wait_recv()
    for k in range(1, pairs):
        send(k).wait_send()
    for k in range(pairs):
        hand(k).wait_send()


def muon(count, moments, ga, gb, squares, collective_id):
    width = ga.shape[1]
    tile = width // 3
    share = width // (count // 4)
    pairs = count // 2
    sizes = tuple(moment.shape[0] for moment in moments)

    def vmem(dtype, rows=width, columns=width):
        return pltpu.VMEM((rows, columns), dtype)

    scratch = (
        [vmem(F32), vmem(BF), vmem(BF), vmem(BF)]
        + [vmem(F32, tile)] * 3
        + [vmem(F32), vmem(BF), vmem(BF), vmem(BF), vmem(BF), vmem(F32), vmem(BF), vmem(BF)]
        + [vmem(F32, share)]
        + [pltpu.SemaphoreType.DMA((2,)), pltpu.SemaphoreType.DMA((2,))]
        + [pltpu.SemaphoreType.DMA((2, pairs)), pltpu.SemaphoreType.DMA((2, pairs))]
        + line_scratch(tile, width, F32)
        + vector_scratch(4, squares.shape)
    )
    return pl.pallas_call(
        functools.partial(muon_kernel, count, sizes),
        out_shape=(
            jax.ShapeDtypeStruct((4 * width, width), BF),
            jax.ShapeDtypeStruct(squares.shape, F32),
        ),
        in_specs=[IN_ANY] * 6 + [IN_VMEM],
        out_specs=(IN_VMEM, IN_VMEM),
        scratch_shapes=scratch,
        compiler_params=params(collective_id),
        name="muon",
    )(*moments, ga, gb, squares)


def layer_norm(values, gain, shift):
    center = values - jnp.mean(values, axis=-1, keepdims=True)
    inverse = lax.rsqrt(jnp.mean(center * center, axis=-1, keepdims=True) + EPS_NORM)
    normed = center * inverse
    return (normed * gain + shift, normed, inverse)


def norm_back(grad_out, normed, inverse, gain):
    scaled = grad_out * gain
    first_mean = jnp.mean(scaled, axis=-1, keepdims=True)
    second_mean = jnp.mean(scaled * normed, axis=-1, keepdims=True)
    return inverse * (scaled - first_mean - normed * second_mean)


def gelu_slope(upward):
    cdf_part = 0.5 * (1.0 + jax.scipy.special.erf(upward / math.sqrt(2.0)))
    return cdf_part + upward * jnp.exp(-0.5 * upward * upward) / math.sqrt(2.0 * math.pi)


def dot(left, right):
    return jnp.dot(left, right, preferred_element_type=F32)


def tdot(left, right):
    return lax.dot_general(left, right, (((0,), (0,)), ((), ())), preferred_element_type=F32)


def vector_step(param, moment, mean_sq):
    return param - 0.1 * moment * lax.rsqrt(mean_sq + 1e-06)


def local(
    tokens, segments, cotangent,
    w_qkv, w_out, w_up, w_down, head_bias, ff_bias, row_params,
    mom_qkv, mom_out, mom_up, mom_down, mom_heads, mom_ff, mom_params,
):
    tok_count, width = tokens.shape
    columns = w_qkv.shape[2]
    ff_cols = w_up.shape[1]
    local_heads = columns // HD
    seq_count, seq_len = segments.shape
    score_scale = 1.0 / math.sqrt(HD)
    tensor_size = lax.axis_size("tensor")
    count = lax.axis_size("dp")
    wq_low = w_qkv.astype(BF)
    wo_low = w_out.astype(BF)
    wu_low = w_up.astype(BF)
    wd_low = w_down.astype(BF)

    def split_heads(rows):
        return rows.reshape(seq_count, seq_len, local_heads, HD).transpose(0, 2, 1, 3)

    def join_heads(blocks):
        return blocks.transpose(0, 2, 1, 3).reshape(tok_count, columns)

    query_h = split_heads((dot(tokens, wq_low[0]) + head_bias[0]).astype(BF))
    keys_h = split_heads(dot(tokens, wq_low[1]).astype(BF))
    values_h = split_heads((dot(tokens, wq_low[2]) + head_bias[1]).astype(BF))
    same_seg = (segments[:, :, None] == segments[:, None, :])[:, None]
    scores = (
        jnp.einsum("shqd,shkd->shqk", query_h, keys_h, preferred_element_type=F32) * score_scale
    )
    scores = jnp.where(same_seg, scores, -1e30)
    row_max = jnp.max(scores, axis=-1, keepdims=True)
    expo = jnp.exp(scores - row_max)
    probs = expo / jnp.sum(expo, axis=-1, keepdims=True)
    probs_low = probs.astype(BF)
    context = jnp.einsum("shqk,shkd->shqd", probs_low, values_h, preferred_element_type=F32)
    context_low = join_heads(context.astype(BF))
    attn = sum_tensor(dot(context_low, wo_low).astype(BF), 1).astype(F32)
    first_in = tokens.astype(F32) + attn + row_params[0]
    hidden_one, normed_one, inverse_one = layer_norm(first_in, row_params[2], row_params[3])
    hidden_low = hidden_one.astype(BF)
    upward = dot(hidden_low, wu_low) + ff_bias
    activated_low = jax.nn.gelu(upward, approximate=False).astype(BF)
    mlp = sum_tensor(dot(activated_low, wd_low).astype(BF), 2).astype(F32)
    second_in = hidden_one + mlp + row_params[1]
    output_rows, normed_two, inverse_two = layer_norm(second_in, row_params[4], row_params[5])
    grad_out = cotangent.astype(F32)
    grad_second = norm_back(grad_out, normed_two, inverse_two, row_params[4])
    grad_mlp_low = grad_second.astype(BF)
    grad_act = dot(grad_mlp_low, wd_low.T)
    grad_up_low = (grad_act * gelu_slope(upward)).astype(BF)
    back_hidden = sum_tensor(dot(grad_up_low, wu_low.T).astype(BF), 3).astype(F32)
    grads_b = jnp.concatenate(
        [tdot(grad_up_low, hidden_low).astype(BF), tdot(activated_low, grad_mlp_low).astype(BF)]
    )
    sum_b = sum_dp_only(count, grads_b, 4)
    grad_hidden = back_hidden + grad_second
    grad_first = norm_back(grad_hidden, normed_one, inverse_one, row_params[2])
    grad_attn_low = grad_first.astype(BF)
    grad_context = split_heads(dot(grad_attn_low, wo_low.T).astype(BF))
    grad_values = jnp.einsum("shqk,shqd->shkd", probs_low, grad_context, preferred_element_type=F32)
    grad_probs = jnp.einsum("shqd,shkd->shqk", grad_context, values_h, preferred_element_type=F32)
    grad_scores = (
        probs * (grad_probs - jnp.sum(probs * grad_probs, axis=-1, keepdims=True))
    ).astype(BF)
    grad_query = (
        jnp.einsum("shqk,shkd->shqd", grad_scores, keys_h, preferred_element_type=F32) * score_scale
    )
    grad_keys = (
        jnp.einsum("shqk,shqd->shkd", grad_scores, query_h, preferred_element_type=F32)
        * score_scale
    )
    gq_low = join_heads(grad_query.astype(BF))
    gk_low = join_heads(grad_keys.astype(BF))
    gv_low = join_heads(grad_values.astype(BF))
    grads_a = jnp.concatenate(
        [
            tdot(jnp.concatenate([gq_low, gk_low, gv_low], axis=1), tokens).astype(BF),
            tdot(context_low, grad_attn_low).astype(BF),
        ]
    )

    def over_rows(values):
        return jnp.sum(values, axis=0)

    heads_part = jnp.concatenate(
        [
            over_rows(gq_low.astype(F32)),
            over_rows(gv_low.astype(F32)),
            jnp.zeros((width - 2 * columns,), F32),
        ]
    )
    vectors = jnp.stack(
        [
            over_rows(grad_first),
            over_rows(grad_second),
            over_rows(grad_hidden * normed_one),
            over_rows(grad_hidden),
            over_rows(grad_out * normed_two),
            over_rows(grad_out),
            over_rows(grad_up_low.astype(F32)),
            heads_part,
        ]
    )
    sum_a, vector_total = sum_dp(count, grads_a, vectors, 5)
    param_sum = vector_total[0:6]
    ff_own = vector_total[6]
    heads_own = vector_total[7, : 2 * columns].reshape(2, columns)
    new_mom_heads = 0.5 * mom_heads + heads_own
    new_mom_ff = 0.5 * mom_ff + ff_own
    new_mom_params = 0.5 * mom_params + param_sum
    squares = jnp.broadcast_to(
        jnp.concatenate(
            [
                jnp.sum(new_mom_heads * new_mom_heads, axis=1),
                jnp.sum(new_mom_ff * new_mom_ff)[None],
                jnp.zeros((5,), F32),
            ]
        )[:, None],
        (8, 128),
    )
    qkv_rows = 3 * columns
    moments = (
        mom_qkv.transpose(0, 2, 1).reshape(qkv_rows, width),
        mom_out,
        mom_up.T,
        mom_down,
    )
    steps, totals = muon(count, moments, sum_a, sum_b, squares, 6)
    back_terms = dot(gq_low, wq_low[0].T)
    back_terms = back_terms + dot(gk_low, wq_low[1].T)
    back_terms = back_terms + dot(gv_low, wq_low[2].T)
    grad_inputs = sum_tensor(back_terms.astype(BF), 7).astype(F32) + grad_first

    def to_qkv(rows):
        return rows.reshape(3, columns, width).transpose(0, 2, 1)

    new_mom_qkv = 0.5 * mom_qkv + to_qkv(sum_a[:qkv_rows].astype(F32))
    new_mom_out = 0.5 * mom_out + sum_a[qkv_rows:].astype(F32)
    new_mom_up = 0.5 * mom_up + sum_b[:ff_cols].astype(F32).T
    new_mom_down = 0.5 * mom_down + sum_b[ff_cols:].astype(F32)
    wide = math.sqrt(ff_cols * tensor_size / width)
    new_qkv = w_qkv - 0.8 * math.sqrt(3.0) * to_qkv(steps[:qkv_rows].astype(F32))
    new_out = w_out - 0.8 * steps[width : width + columns].astype(F32)
    new_up = w_up - 0.8 * wide * steps[2 * width : 3 * width].astype(F32).T
    new_down = w_down - 0.8 * wide * steps[3 * width :].astype(F32)
    new_heads = vector_step(head_bias, new_mom_heads, totals[0:2, 0:1] / (columns * tensor_size))
    new_ff = vector_step(ff_bias, new_mom_ff, totals[2, 0] / (ff_cols * tensor_size))
    new_params = vector_step(
        row_params,
        new_mom_params,
        jnp.mean(new_mom_params * new_mom_params, axis=-1, keepdims=True),
    )
    return (
        output_rows.astype(BF),
        grad_inputs.astype(BF),
        new_mom_qkv, new_qkv, new_qkv.astype(BF),
        new_mom_out, new_out, new_out.astype(BF),
        new_mom_up, new_up, new_up.astype(BF),
        new_mom_down, new_down, new_down.astype(BF),
        new_mom_heads, new_heads,
        new_mom_ff, new_ff,
        new_mom_params, new_params,
    )


def solution(mesh):
    placed = (
        P("dp", None), P("dp", None), P("dp", None),
        P(None, None, "tensor"), P("tensor", None), P(None, "tensor"), P("tensor", None),
        P(None, "tensor"), P("tensor"), P(),
        P(None, None, "tensor"), P("tensor", None), P(None, "tensor"), P("tensor", None),
        P(None, "tensor"), P("tensor"), P(),
    )
    triple = ((P(None, None, "tensor"),) * 3, (P("tensor", None),) * 3, (P(None, "tensor"),) * 3)
    return jax.shard_map(
        local,
        mesh=mesh,
        in_specs=placed,
        out_specs=(
            (P("dp", None), P("dp", None))
            + triple[0] + triple[1] + triple[2] + triple[1]
            + (P(None, "tensor"), P(None, "tensor"), P("tensor"), P("tensor"), P(), P())
        ),
        check_vma=False,
    )
```

time: 1480 us -> 415 us (0.28)
  the two profiles are of different devices: /device:TPU:13 before, /device:TPU:0 now
where the time goes in v1:
time: 415 us; the launch traced here: 408 us
  Pallas kernels  307 us (74%)
  other arithmetic  44.5 us (11%)
  local copies, waits for them, and re-layouts  27.6 us (7%)
  matrix products  26.3 us (6%)
    pallas_call x4, Pallas kernels, sum_tensor(): pl.pallas_call(line_kernel, out_shape=jax.ShapeDtypeStruct(partial.shape,...  129 us
    pallas_call x1, Pallas kernels, muon(): pl.pallas_call(functools.partial(muon_kernel, count, sizes), out_shape=(j...  116 us
    pallas_call x1, Pallas kernels, sum_dp_only(): pl.pallas_call(functools.partial(dp_only_kernel, count), out_shape=jax.Sh...  38.4 us
    pallas_call x1, Pallas kernels, sum_dp(): pl.pallas_call(functools.partial(dp_kernel, count), out_shape=(jax.ShapeD...  24.1 us
    dot_general x12, matrix products, dot(): return jnp.dot(left, right, preferred_element_type=F32)  17.8 us
    unnamed x117, local copies, waits for them, and re-layouts  17.6 us

profile of v1, /device:TPU:0, one launch (start us, length us, event | category | flops | bytes accessed | tf_op | source)
XLA Modules:
  0.0 408.2 jit_solution(10414191810625727278)
XLA Ops:
  0.7 0.8 fusion.94
  1.4 1.0 slice_reduce_fusion.2
  2.5 0.9 broadcast_compare_fusion
  3.4 1.6 convert_element_type.165
  6.4 0.7 fusion.95
  7.5 0.8 copy-done.22
  8.7 1.3 convolution_convert_fusion.5.x
  10.0 34.9 %sum_tensor.4 = bf16[512,768]{1,0:T(8,128)(2,1)} custom-call(bf16[512,768]{1,0:T(8,128)(2,1)} %convolution_convert_fusion.5.x), custom_call_target="tpu_custom_call" | custom-call | tf_op jit(solution)/shard_map/sum_tensor/pallas_call | solution.py:200
  44.9 1.5 fusion.28
  46.9 3.1 copy.62
  49.9 3.1 copy.64
  53.0 7.1 %fusion.11 = (bf16[512,768]{1,0:T(8,128)(2,1)S(1)}, f32[512,768]{1,0:T(8,128)}) fusion(f32[768]{0:T(1024)S(1)} %copy-done.49, f32[768,768]{1,0:T(8,128)} %param.22, f32[768]{0:T(1024)S(1)} %get-tuple-element.79, f32[768]{0:T(1024)S(1)} %get-tuple-element.80, f32[512]{0:T(512)S(1)} %add_rsqrt_fusion.1, f32[512]{0:T(512)S(1)} %broadcast_multiply_fusion.5, ...), kind=kOutput, calls=%fused_computation.23 | convolution fusion | flops 634060800 | bytes 6307840 | tf_op jit(solution)/shard_map/dot_general | solution.py:611
  60.2 1.7 convolution_convert_fusion.4.x
  61.8 30.6 %sum_tensor.5 = bf16[512,768]{1,0:T(8,128)(2,1)} custom-call(bf16[512,768]{1,0:T(8,128)(2,1)} %convolution_convert_fusion.4.x), custom_call_target="tpu_custom_call" | custom-call | tf_op jit(solution)/shard_map/sum_tensor/pallas_call | solution.py:200
  92.5 1.9 fusion.93
  94.7 0.8 copy-done.20
  95.5 0.8 fusion.12
  96.4 1.5 fusion.7
  98.7 1.2 convert_reduce_fusion.1
  100.0 1.8 convolution_convert_fusion
  101.8 1.7 convolution_convert_fusion.3.x
  103.5 30.6 %sum_tensor.6 = bf16[512,768]{1,0:T(8,128)(2,1)} custom-call(bf16[512,768]{1,0:T(8,128)(2,1)} %convolution_convert_fusion.3.x), custom_call_target="tpu_custom_call" | custom-call | tf_op jit(solution)/shard_map/sum_tensor/pallas_call | solution.py:200
  134.1 2.2 multiply_reduce_fusion
  136.4 0.8 fusion.92
  137.1 1.0 convolution_convert_fusion.1
  138.7 1.6 pad_maximum_fusion.x
  140.3 38.4 %sum_dp_only.1.gb = bf16[1536,768]{1,0:T(8,128)(2,1)} custom-call(bf16[1536,768]{1,0:T(8,128)(2,1)} %pad_maximum_fusion.x), custom_call_target="tpu_custom_call" | custom-call | tf_op jit(solution)/shard_map/sum_dp_only/pallas_call | solution.py:379
  179.8 1.0 convolution_convert_fusion.6
  181.4 1.9 convert_reduce_fusion.2
  183.2 0.6 reduce_sum.222
  184.1 0.7 copy.75
  185.2 1.4 copy.71
  186.7 3.8 bitcast_add_fusion
  191.2 0.6 copy-done.30
  192.8 0.7 stack.35.v
  194.6 0.6 convolution_convert_fusion.2
  195.6 1.1 pad_maximum_fusion.1.x
  196.7 24.1 %sum_dp.1 = (bf16[768,768]{1,0:T(8,128)(2,1)}, f32[8,768]{1,0:T(8,128)}) custom-call(bf16[768,768]{1,0:T(8,128)(2,1)} %pad_maximum_fusion.1.x, f32[8,768]{1,0:T(8,128)} %stack.35.v), custom_call_target="tpu_custom_call" | custom-call | tf_op jit(solution)/shard_map/sum_dp/pallas_call | solution.py:356
  220.8 0.8 slice_reduce_fusion.7
  221.8 0.8 slice_reduce_fusion
  222.6 0.9 multiply_reduce_fusion.6
  223.5 0.6 multiply_reduce_fusion.7
  224.1 0.7 pad_maximum_fusion.3
  224.8 0.7 broadcast_in_dim.22.vs
  225.5 0.7 multiply_subtract_fusion.2
  226.1 2.0 convert_add_fusion.2
  228.2 1.4 fusion.4
  229.6 115.6 %muon.1 = (bf16[3072,768]{1,0:T(8,128)(2,1)}, f32[8,128]{1,0:T(8,128)}) custom-call(f32[576,768]{1,0:T(8,128)} %bitcast.126, f32[192,768]{1,0:T(8,128)} %mo.1, f32[768,768]{1,0:T(8,128)} %bitcast.125, f32[768,768]{1,0:T(8,128)} %md.1, bf16[768,768]{1,0:T(8,128)(2,1)} %get-tuple-element.24.ga, bf16[1536,768]{1,0:T(8,128)(2,1)} %sum_dp_only.1.gb, ...), custom_call_target="tpu_custom_call" | custom-call | tf_op jit(solution)/shard_map/muon/pallas_call | solution.py:577
  345.2 1.2 slice.99
  347.1 0.8 multiply_reduce_fusion.9
  348.0 3.5 convert_add_fusion
  351.4 0.6 multiply_subtract_fusion.4
  352.7 1.9 fusion.90
  354.6 3.0 fusion.89
  357.6 1.4 copy.66
  359.1 1.5 fusion.52
  361.0 1.3 add_convert_fusion.1.x
  362.3 33.2 %sum_tensor.7 = bf16[512,768]{1,0:T(8,128)(2,1)} custom-call(bf16[512,768]{1,0:T(8,128)(2,1)} %add_convert_fusion.1.x), custom_call_target="tpu_custom_call" | custom-call | tf_op jit(solution)/shard_map/sum_tensor/pallas_call | solution.py:200
  395.5 2.2 add_convert_fusion
  397.6 1.5 convert_multiply_fusion.2
  399.6 3.6 fusion.88
  403.2 1.7 fusion.91
  404.9 0.9 copy-done.5
  405.8 1.9 copy.65
  (153 shorter events, 11.5 us)
Async XLA Ops:
  0.7 4.3 %copy-start.2 = (bf16[512,768]{1,0:T(8,128)(2,1)S(1)}, bf16[512,768]{1,0:T(8,128)(2,1)}, u32[]{:S(2)}) copy-start(bf16[512,768]{1,0:T(8,128)(2,1)} %param.17) | copy-start | bytes 2359300
  4.9 1.0 copy-start.18
  5.4 1.8 copy-start.35
  5.9 1.2 copy-start.29
  6.4 0.7 copy-start.27
  7.2 1.1 copy-start.22
  7.2 174.2 %copy-start.44 = (f32[2,3,256]{2,1,0:T(4,128)}, f32[2,3,256]{2,1,0:T(4,128)S(1)}, u32[]{:S(2)}) copy-start(f32[2,3,256]{2,1,0:T(4,128)S(1)} %get-tuple-element.105) | copy-start | bytes 18436
  7.2 1.5 copy-start.13
  44.9 1.6 copy-start
  49.9 3.1 copy-start.49
  53.0 7.2 %copy-start.6 = (f32[768,768]{1,0:T(8,128)S(1)}, f32[768,768]{1,0:T(8,128)}, u32[]{:S(2)}) copy-start(f32[768,768]{1,0:T(8,128)} %param.23) | copy-start | bytes 7077892
  94.4 1.1 copy-start.20
  96.3 1.8 copy-start.7
  96.3 2.4 copy-start.53
  100.0 1.8 copy-start.9
  134.1 2.3 copy-start.11
  137.1 1.6 copy-start.17
  178.7 2.2 copy-start.14
  183.9 1.3 slice-start
  186.7 3.8 copy-start.23
  186.7 3.8 copy-start.36
  186.7 3.8 copy-start.45
  190.9 0.9 copy-start.30
  190.9 1.3 copy-start.28
  191.8 0.8 copy-start.51
  191.8 0.9 copy-start.41
  191.8 0.9 copy-start.42
  191.8 0.9 copy-start.43
  192.2 2.4 copy-start.3
  192.2 2.4 copy-start.25
  193.6 0.7 copy-start.31
  193.9 0.7 copy-start.33
  194.6 1.0 copy-start.24
  195.5 26.1 %copy-start.52 = (f32[2,192]{1,0:T(2,128)S(1)}, f32[2,192]{1,0:T(2,128)}, u32[]{:S(2)}) copy-start(f32[2,192]{1,0:T(2,128)} %param.31) | copy-start | bytes 4612
  195.6 27.0 %copy-start.39 = (f32[6,768]{1,0:T(8,128)S(1)}, f32[6,768]{1,0:T(8,128)}, u32[]{:S(2)}) copy-start(f32[6,768]{1,0:T(8,128)} %param.33) | copy-start | bytes 55300
  195.6 27.9 %copy-start.48 = (f32[768]{0:T(1024)S(1)}, f32[768]{0:T(1024)}, u32[]{:S(2)}) copy-start(f32[768]{0:T(1024)} %param.32) | copy-start | bytes 9220
  195.6 29.9 %copy-start.38 = (f32[6,768]{1,0:T(8,128)S(1)}, f32[6,768]{1,0:T(8,128)}, u32[]{:S(2)}) copy-start(f32[6,768]{1,0:T(8,128)} %param.26) | copy-start | bytes 55300
  195.6 30.6 %copy-start.21 = (f32[192,768]{1,0:T(8,128)S(1)}, f32[192,768]{1,0:T(8,128)}, u32[]{:S(2)}) copy-start(f32[192,768]{1,0:T(8,128)} %mo.1) | copy-start | bytes 1769476
  220.8 7.3 %copy-start.16 = (bf16[768,768]{1,0:T(8,128)(2,1)S(1)}, bf16[768,768]{1,0:T(8,128)(2,1)}, u32[]{:S(2)}) copy-start(bf16[768,768]{1,0:T(8,128)(2,1)} %get-tuple-element.24.ga) | copy-start | bytes 3538948
  221.8 129.6 %copy-start.47 = (f32[2,192]{1,0:T(2,128)}, f32[2,192]{1,0:T(2,128)S(1)}, u32[]{:S(2)}) copy-start(f32[2,192]{1,0:T(2,128)S(1)} %get-tuple-element.94) | copy-start | bytes 4612
  223.4 4.7 %copy-start.37 = (f32[6,768]{1,0:T(8,128)}, f32[6,768]{1,0:T(8,128)S(1)}, u32[]{:S(2)}) copy-start(f32[6,768]{1,0:T(8,128)S(1)} %get-tuple-element.84) | copy-start | bytes 55300
  224.1 128.0 %copy-start.40 = (f32[768]{0:T(1024)}, f32[768]{0:T(1024)S(1)}, u32[]{:S(2)}) copy-start(f32[768]{0:T(1024)S(1)} %get-tuple-element.96) | copy-start | bytes 9220
  226.1 2.0 copy-start.10
  229.6 118.3 %copy-start.1 = (bf16[1536,768]{1,0:T(8,128)(2,1)S(1)}, bf16[1536,768]{1,0:T(8,128)(2,1)}, u32[]{:S(2)}) copy-start(bf16[1536,768]{1,0:T(8,128)(2,1)} %sum_dp_only.1.gb) | copy-start | bytes 7077892
  347.9 3.5 copy-start.46
  347.9 4.2 %copy-start.50 = (f32[768]{0:T(1024)S(1)}, f32[768]{0:T(1024)}, u32[]{:S(2)}) copy-start(f32[768]{0:T(1024)} %param.25) | copy-start | bytes 9220
  347.9 4.7 %copy-start.15 = (f32[192,768]{1,0:T(8,128)S(1)}, f32[192,768]{1,0:T(8,128)}, u32[]{:S(2)}) copy-start(f32[192,768]{1,0:T(8,128)} %param.21) | copy-start | bytes 1769476
  348.0 6.7 %copy-start.4 = (f32[768,768]{0,1:T(8,128)S(1)}, f32[768,768]{0,1:T(8,128)}, u32[]{:S(2)}) copy-start(f32[768,768]{0,1:T(8,128)} %copy.64) | copy-start | bytes 7077892
  357.6 1.4 copy-start.34
  359.1 1.5 copy-start.19
  359.1 1.5 copy-start.32
  359.1 1.9 copy-start.26
  397.6 1.9 copy-start.8
  399.6 3.6 copy-start.12
  403.2 2.6 copy-start.5

commit v2 on v1

--- a/solution.py
+++ b/solution.py
@@ -18,6 +18,7 @@
 MESH = pl.DeviceIdType.MESH
 SUBS = 2
 VMEM_LIMIT = 56 * 1024 * 1024
+PLACE = (1, 2, 0, 3)
 
 
 def remote(src, dst, send_sem, recv_sem, device):
@@ -367,24 +368,31 @@
     )(grads, vectors)
 
 
-def dp_only_kernel(count, x, o, *scratch):
+def both_kernel(count, x, g, o, go, *scratch):
     p = lax.axis_index("dp")
-    greet([{"dp": (p + k) % count} for k in range(1, count)])
-    for step in plane_sum(count, p, x, o, scratch):
-        step()
-
-
-def sum_dp_only(count, grads, collective_id):
-    rows, width = grads.shape
+    t = lax.axis_index("tensor")
+    greet(z_peers(t) + [{"dp": (p + k) % count} for k in range(1, count)])
+    line = line_sum(t, x, o, scratch[:6])
+    plane = plane_sum(count, p, g, go, scratch[6:])
+    for steps in zip(line, plane):
+        for step in steps:
+            step()
+
+
+def sum_both(count, partial, grads, collective_id):
     return pl.pallas_call(
-        functools.partial(dp_only_kernel, count),
-        out_shape=jax.ShapeDtypeStruct(grads.shape, BF),
-        in_specs=[IN_VMEM],
-        out_specs=IN_VMEM,
-        scratch_shapes=plane_scratch(count, rows, width),
+        functools.partial(both_kernel, count),
+        out_shape=(
+            jax.ShapeDtypeStruct(partial.shape, partial.dtype),
+            jax.ShapeDtypeStruct(grads.shape, BF),
+        ),
+        in_specs=[IN_VMEM] * 2,
+        out_specs=(IN_VMEM,) * 2,
+        scratch_shapes=line_scratch(*partial.shape, partial.dtype)
+        + plane_scratch(count, *grads.shape),
         compiler_params=params(collective_id),
-        name="sum_dp_only",
-    )(grads)
+        name="sum_both",
+    )(partial, grads)
 
 
 def cut(values):
@@ -401,8 +409,8 @@
 
 def muon_kernel(
     count, sizes,
-    mq, mo, mu, md, ga, gb, vs,
-    xo, vt,
+    mq, mo, mu, md, ga, gb, vs, bx,
+    xo, vt, bo,
     zf, gf, zh, zl, gx, go, gp, af, ah, al, dh, dl, sf, sh, sl, xf, lsem, psem, asem_s, asem_r, *scratch,
 ):
     p = lax.axis_index("dp")
@@ -417,7 +425,8 @@
     share = xf.shape[0]
     tile = width // 3
     greet(z_peers(t) + [{"dp": (p + k) % count} for k in range(1, count)])
-    vector = vector_sum("tensor", 4, t, vs, vt, scratch[6:])
+    vector = vector_sum("tensor", 4, t, vs, vt, scratch[12:])
+    back = line_sum(t, bx, bo, scratch[6:12])
     vector[0]()
     qkv_rows, out_rows, _, _ = sizes
     gsrc = (
@@ -426,7 +435,7 @@
     for index, moment in enumerate((mq, mo, mu, md)):
         grads, first, rows = gsrc[index]
 
-        @pl.when(which == index)
+        @pl.when(which == PLACE[index])
         def _(moment=moment, grads=grads, first=first, rows=rows):
             one = pltpu.make_async_copy(moment, zf.at[pl.ds(0, rows)], lsem.at[0])
             two = pltpu.make_async_copy(
@@ -458,6 +467,7 @@
         step()
     swap = remote(go, gp, psem.at[0], psem.at[1], mate)
     swap.start()
+    back[0]()
     swap.wait()
     diagonal = lax.broadcasted_iota(jnp.int32, (tile, tile), 0) == lax.broadcasted_iota(
         jnp.int32, (tile, tile), 1
@@ -479,8 +489,18 @@
                 spot = (pl.ds(r * tile, tile), pl.ds(c * tile, tile))
                 af[spot] = value
                 ah[spot], al[spot] = cut(value)
-        rank = p % group
-        xf[...] = zf[pl.ds(pl.multiple_of(rank * share, share), share)] * inverse
+        if group == 2:
+            for index, rows in enumerate(sizes):
+
+                @pl.when(which == PLACE[index])
+                def _(half=rows // 2):
+                    xf[0:half] = zf[pl.ds(pl.multiple_of(core * half, half), half)] * inverse
+                    if half < share:
+                        xf[half:share] = jnp.zeros((share - half, width), F32)
+
+        else:
+            rank = p % group
+            xf[...] = zf[pl.ds(pl.multiple_of(rank * share, share), share)] * inverse
 
     @pl.when(core == 0)
     def _():
@@ -492,11 +512,22 @@
 
     vector[1]()
 
+    def product(left, right, base, base_scale, scale, targets):
+        (lh, ll), (rh, rl) = left, right
+        for i in range(3):
+            rows = pl.ds(i * tile, tile)
+            for j in range(i, 3):
+                columns = pl.ds(j * tile, tile)
+                value = base_scale * base[rows, columns] + scale * dot3(
+                    lh[rows], ll[rows], rh[:, columns], rl[:, columns]
+                )
+                for target, part in zip(targets, (*cut(value), value)):
+                    target[rows, columns] = part
+                    if i != j:
+                        target[columns, rows] = part.T
+
     def make_d():
-        for i in range(3):
-            spot = pl.ds(i * tile, tile)
-            value = coef_b * af[spot] + coef_c * dot3(ah[spot], al[spot], ah[...], al[...])
-            dh[spot], dl[spot] = cut(value)
+        product((ah, al), (ah, al), af, coef_b, coef_c, (dh, dl))
 
     def move_x():
         xh, xl = cut(xf[...])
@@ -505,21 +536,104 @@
     def sweep(k, carry):
         make_d()
         move_x()
-        for i in range(3):
-            spot = pl.ds(i * tile, tile)
-            value = coef_a * af[spot] + dot3(ah[spot], al[spot], dh[...], dl[...])
-            sf[spot] = value
-            sh[spot], sl[spot] = cut(value)
-        for i in range(3):
-            spot = pl.ds(i * tile, tile)
-            value = coef_a * sf[spot] + dot3(sh[spot], sl[spot], dh[...], dl[...])
-            af[spot] = value
-            ah[spot], al[spot] = cut(value)
+        product((ah, al), (dh, dl), af, coef_a, 1.0, (sh, sl, sf))
+        product((sh, sl), (dh, dl), sf, coef_a, 1.0, (ah, al, af))
+        for i in range(1, 4):
+            pl.when(k == i - 1)(back[i])
         return carry
 
     lax.fori_loop(0, 4, sweep, 0)
     make_d()
     move_x()
+    back[4]()
+
+    if pairs == 4:
+        gather_square(pair, core, mate, sizes, xf, xo, asem_s, asem_r)
+    else:
+        gather_any(p, core, pairs, mate, xf, xo, asem_s, asem_r)
+
+
+def gather_square(pair, core, mate, sizes, xf, xo, ssem, rsem):
+    width = xf.shape[1]
+
+    def piece(index, side, part):
+        half = sizes[index] // 4
+        first = index * width + side * 2 * half + part * half
+        return xo.at[pl.ds(pl.multiple_of(first, half), half)]
+
+    def copy(index, part, route, device):
+        spot = piece(index, core, part)
+        return remote(spot, spot, ssem.at[index, part, route], rsem.at[index, part, route], device)
+
+    def other(away):
+        return {"dp": 2 * (pair + away * (1 - 2 * ((pair // away) % 2))) + core}
+
+    def place_is(index, away):
+        return pair == (PLACE[index] ^ away)
+
+    def wait_in(index, part, route, side):
+        spot = piece(index, side, part)
+        remote(spot, spot, ssem.at[index, part, route], rsem.at[index, part, route], mate).wait_recv()
+
+    for index, rows in enumerate(sizes):
+        half = rows // 4
+
+        @pl.when(place_is(index, 0))
+        def _(index=index, half=half):
+            for part in range(2):
+                piece(index, core, part)[...] = xf[pl.ds(part * half, half)].astype(BF)
+            for part in range(2):
+                copy(index, part, 0, other(1)).start()
+                copy(index, 1 - part, 1, other(2)).start()
+            for part in range(2):
+                copy(index, part, 3, mate).start()
+
+    for index in range(4):
+        for away, route, onward in ((1, 0, 2), (2, 1, 1)):
+
+            @pl.when(place_is(index, away))
+            def _(index=index, away=away, route=route, onward=onward):
+                first = away - 1
+                wait_in(index, first, route, core)
+                copy(index, first, 2, other(onward)).start()
+                copy(index, first, 3, mate).start()
+
+    for index in range(4):
+        for away, route, onward in ((1, 0, 2), (2, 1, 1)):
+
+            @pl.when(place_is(index, away))
+            def _(index=index, away=away, route=route):
+                second = 2 - away
+                wait_in(index, second, route, core)
+                copy(index, second, 3, mate).start()
+
+        @pl.when(place_is(index, 3))
+        def _(index=index):
+            for part in range(2):
+                wait_in(index, part, 2, core)
+                copy(index, part, 3, mate).start()
+
+    for index in range(4):
+        for part in range(2):
+            wait_in(index, part, 3, 1 - core)
+            copy(index, part, 3, mate).wait_send()
+
+        @pl.when(place_is(index, 0))
+        def _(index=index):
+            for part in range(2):
+                copy(index, part, 0, other(1)).wait_send()
+                copy(index, part, 1, other(2)).wait_send()
+
+        for away, onward in ((1, 2), (2, 1)):
+
+            @pl.when(place_is(index, away))
+            def _(index=index, away=away, onward=onward):
+                copy(index, away - 1, 2, other(onward)).wait_send()
+
+
+def gather_any(p, core, pairs, mate, xf, xo, asem_s, asem_r):
+    pair = p // 2
+    share = xf.shape[0]
 
     def rows_of(device):
         return xo.at[pl.ds(pl.multiple_of(device * share, share), share)]
@@ -554,7 +668,7 @@
         hand(k).wait_send()
 
 
-def muon(count, moments, ga, gb, squares, collective_id):
+def muon(count, moments, ga, gb, squares, back, collective_id):
     width = ga.shape[1]
     tile = width // 3
     share = width // (count // 4)
@@ -570,8 +684,9 @@
         + [vmem(F32), vmem(BF), vmem(BF), vmem(BF), vmem(BF), vmem(F32), vmem(BF), vmem(BF)]
         + [vmem(F32, share)]
         + [pltpu.SemaphoreType.DMA((2,)), pltpu.SemaphoreType.DMA((2,))]
-        + [pltpu.SemaphoreType.DMA((2, pairs)), pltpu.SemaphoreType.DMA((2, pairs))]
+        + [pltpu.SemaphoreType.DMA((4, 2, 4) if pairs == 4 else (2, pairs))] * 2
         + line_scratch(tile, width, F32)
+        + line_scratch(*back.shape, BF)
         + vector_scratch(4, squares.shape)
     )
     return pl.pallas_call(
@@ -579,13 +694,14 @@
         out_shape=(
             jax.ShapeDtypeStruct((4 * width, width), BF),
             jax.ShapeDtypeStruct(squares.shape, F32),
+            jax.ShapeDtypeStruct(back.shape, BF),
         ),
-        in_specs=[IN_ANY] * 6 + [IN_VMEM],
-        out_specs=(IN_VMEM, IN_VMEM),
+        in_specs=[IN_ANY] * 6 + [IN_VMEM] * 2,
+        out_specs=(IN_VMEM,) * 3,
         scratch_shapes=scratch,
         compiler_params=params(collective_id),
         name="muon",
-    )(*moments, ga, gb, squares)
+    )(*moments, ga, gb, squares, back)
 
 
 def layer_norm(values, gain, shift):
@@ -671,12 +787,11 @@
     grad_mlp_low = grad_second.astype(BF)
     grad_act = dot(grad_mlp_low, wd_low.T)
     grad_up_low = (grad_act * gelu_slope(upward)).astype(BF)
-    back_hidden = sum_tensor(dot(grad_up_low, wu_low.T).astype(BF), 3).astype(F32)
     grads_b = jnp.concatenate(
         [tdot(grad_up_low, hidden_low).astype(BF), tdot(activated_low, grad_mlp_low).astype(BF)]
     )
-    sum_b = sum_dp_only(count, grads_b, 4)
-    grad_hidden = back_hidden + grad_second
+    back_hidden, sum_b = sum_both(count, dot(grad_up_low, wu_low.T).astype(BF), grads_b, 3)
+    grad_hidden = back_hidden.astype(F32) + grad_second
     grad_first = norm_back(grad_hidden, normed_one, inverse_one, row_params[2])
     grad_attn_low = grad_first.astype(BF)
     grad_context = split_heads(dot(grad_attn_low, wo_low.T).astype(BF))
@@ -748,11 +863,11 @@
         mom_up.T,
         mom_down,
     )
-    steps, totals = muon(count, moments, sum_a, sum_b, squares, 6)
     back_terms = dot(gq_low, wq_low[0].T)
     back_terms = back_terms + dot(gk_low, wq_low[1].T)
     back_terms = back_terms + dot(gv_low, wq_low[2].T)
-    grad_inputs = sum_tensor(back_terms.astype(BF), 7).astype(F32) + grad_first
+    steps, totals, back = muon(count, moments, sum_a, sum_b, squares, back_terms.astype(BF), 6)
+    grad_inputs = back.astype(F32) + grad_first
 
     def to_qkv(rows):
         return rows.reshape(3, columns, width).transpose(0, 2, 1)
@@ -761,11 +876,15 @@
     new_mom_out = 0.5 * mom_out + sum_a[qkv_rows:].astype(F32)
     new_mom_up = 0.5 * mom_up + sum_b[:ff_cols].astype(F32).T
     new_mom_down = 0.5 * mom_down + sum_b[ff_cols:].astype(F32)
+    def step_of(index, rows):
+        first = (index if count == 8 else PLACE[index]) * width
+        return steps[first : first + rows].astype(F32)
+
     wide = math.sqrt(ff_cols * tensor_size / width)
-    new_qkv = w_qkv - 0.8 * math.sqrt(3.0) * to_qkv(steps[:qkv_rows].astype(F32))
-    new_out = w_out - 0.8 * steps[width : width + columns].astype(F32)
-    new_up = w_up - 0.8 * wide * steps[2 * width : 3 * width].astype(F32).T
-    new_down = w_down - 0.8 * wide * steps[3 * width :].astype(F32)
+    new_qkv = w_qkv - 0.8 * math.sqrt(3.0) * to_qkv(step_of(0, qkv_rows))
+    new_out = w_out - 0.8 * step_of(1, columns)
+    new_up = w_up - 0.8 * wide * step_of(2, ff_cols).T
+    new_down = w_down - 0.8 * wide * step_of(3, ff_cols)
     new_heads = vector_step(head_bias, new_mom_heads, totals[0:2, 0:1] / (columns * tensor_size))
     new_ff = vector_step(ff_bias, new_mom_ff, totals[2, 0] / (ff_cols * tensor_size))
     new_params = vector_step(

time: 415 us -> 353 us (0.85)
  the two profiles are of different devices: /device:TPU:0 before, /device:TPU:13 now
where the time goes in v2:
time: 353 us; the launch traced here: 346 us
  Pallas kernels  239 us (68%)
  other arithmetic  45.7 us (13%)
  local copies, waits for them, and re-layouts  31.9 us (9%)
  matrix products  27.3 us (8%)
    pallas_call x1, Pallas kernels, muon(): pl.pallas_call(functools.partial(muon_kernel, count, sizes), out_shape=(j...  104 us
    pallas_call x2, Pallas kernels, sum_tensor(): pl.pallas_call(line_kernel, out_shape=jax.ShapeDtypeStruct(partial.shape,...  60.1 us
    pallas_call x1, Pallas kernels, sum_both(): pl.pallas_call(functools.partial(both_kernel, count), out_shape=(jax.Shap...  49.5 us
    pallas_call x1, Pallas kernels, sum_dp(): pl.pallas_call(functools.partial(dp_kernel, count), out_shape=(jax.ShapeD...  25.4 us
    dot_general x12, matrix products, dot(): return jnp.dot(left, right, preferred_element_type=F32)  16.8 us
    unnamed x100, local copies, waits for them, and re-layouts  15.3 us

profile of v2, /device:TPU:13, one launch (start us, length us, event | category | flops | bytes accessed | tf_op | source)
XLA Modules:
  0.0 346.1 jit_solution(14723883907526684128)
XLA Ops:
  0.7 0.8 fusion.94
  1.4 1.6 slice_reduce_fusion.2
  3.1 0.9 broadcast_compare_fusion
  4.0 1.6 convert_element_type.165
  7.0 0.7 fusion.95
  8.0 0.8 copy-done.19
  9.3 1.3 convolution_convert_fusion.5.x
  10.6 29.9 %sum_tensor.2 = bf16[512,768]{1,0:T(8,128)(2,1)} custom-call(bf16[512,768]{1,0:T(8,128)(2,1)} %convolution_convert_fusion.5.x), custom_call_target="tpu_custom_call" | custom-call | tf_op jit(solution)/shard_map/sum_tensor/pallas_call | solution.py:201
  40.4 1.5 fusion.28
  42.5 3.0 copy.55
  45.5 3.1 copy.64
  48.6 7.2 %fusion.11 = (bf16[512,768]{1,0:T(8,128)(2,1)S(1)}, f32[512,768]{1,0:T(8,128)}) fusion(f32[768]{0:T(1024)S(1)} %copy-done.42, f32[768,768]{1,0:T(8,128)} %param.22, f32[768]{0:T(1024)S(1)} %copy-done.32, f32[768]{0:T(1024)S(1)} %get-tuple-element.86, f32[512]{0:T(512)S(1)} %add_rsqrt_fusion.1, f32[512]{0:T(512)S(1)} %broadcast_multiply_fusion.5, ...), kind=kOutput, calls=%fused_computation.23 | convolution fusion | flops 634060800 | bytes 6307840 | tf_op jit(solution)/shard_map/dot_general | solution.py:727
  55.8 1.7 convolution_convert_fusion.4.x
  57.4 30.3 %sum_tensor.3 = bf16[512,768]{1,0:T(8,128)(2,1)} custom-call(bf16[512,768]{1,0:T(8,128)(2,1)} %convolution_convert_fusion.4.x), custom_call_target="tpu_custom_call" | custom-call | tf_op jit(solution)/shard_map/sum_tensor/pallas_call | solution.py:201
  87.7 1.9 fusion.93
  90.0 0.8 copy-done.14
  90.8 0.8 fusion.12
  92.7 1.5 fusion.7
  94.2 1.2 convert_reduce_fusion.1
  95.5 0.8 convolution_convert_fusion
  96.3 0.8 copy-done.6
  97.1 1.7 convolution_convert_fusion.3.x
  98.8 1.0 convolution_convert_fusion.1
  99.9 1.6 pad_maximum_fusion.g
  101.4 49.5 %sum_both.1 = (bf16[512,768]{1,0:T(8,128)(2,1)}, bf16[1536,768]{1,0:T(8,128)(2,1)}) custom-call(bf16[512,768]{1,0:T(8,128)(2,1)} %convolution_convert_fusion.3.x, bf16[1536,768]{1,0:T(8,128)(2,1)} %pad_maximum_fusion.g), custom_call_target="tpu_custom_call" | custom-call | tf_op jit(solution)/shard_map/sum_both/pallas_call | solution.py:383
  151.0 2.2 multiply_reduce_fusion
  153.8 1.4 fusion.92
  157.0 1.0 convolution_convert_fusion.6
  158.7 1.9 convert_reduce_fusion.2
  160.7 0.6 reduce_sum.222
  161.6 2.1 multiply_reduce_fusion.1
  164.0 0.6 copy-done.23
  164.7 1.0 fusion.36
  165.7 0.9 convert_reduce_fusion.3
  166.6 0.8 reduce_sum.220
  167.4 0.8 pad_maximum_fusion.2
  168.2 1.4 stack.35.v
  169.5 1.1 copy.60
  171.9 1.1 pad_maximum_fusion.1.x
  173.0 25.4 %sum_dp.1 = (bf16[768,768]{1,0:T(8,128)(2,1)}, f32[8,768]{1,0:T(8,128)}) custom-call(bf16[768,768]{1,0:T(8,128)(2,1)} %pad_maximum_fusion.1.x, f32[8,768]{1,0:T(8,128)} %stack.35.v), custom_call_target="tpu_custom_call" | custom-call | tf_op jit(solution)/shard_map/sum_dp/pallas_call | solution.py:357
  198.4 0.7 slice_reduce_fusion.7
  199.4 0.8 slice_reduce_fusion
  200.2 0.9 multiply_reduce_fusion.6
  201.7 0.7 pad_maximum_fusion.3
  202.4 0.7 broadcast_in_dim.22.vs
  203.1 0.7 multiply_subtract_fusion.2
  203.8 2.0 convert_add_fusion.2
  205.8 1.4 fusion.4
  208.1 1.3 add_convert_fusion.1.bx
  209.4 103.7 %muon.1 = (bf16[3072,768]{1,0:T(8,128)(2,1)}, f32[8,128]{1,0:T(8,128)}, bf16[512,768]{1,0:T(8,128)(2,1)}) custom-call(f32[576,768]{1,0:T(8,128)} %bitcast.127, f32[192,768]{1,0:T(8,128)} %mo.1, f32[768,768]{1,0:T(8,128)} %bitcast.125, f32[768,768]{1,0:T(8,128)} %md.1, bf16[768,768]{1,0:T(8,128)(2,1)} %get-tuple-element.28.ga, ...), custom_call_target="tpu_custom_call" | custom-call | tf_op jit(solution)/shard_map/muon/pallas_call | solution.py:692
  313.0 1.2 slice.99
  315.0 2.3 add_convert_fusion
  317.3 0.8 multiply_reduce_fusion.9
  318.1 0.6 multiply_subtract_fusion.4
  319.3 1.9 fusion.90
  321.3 3.1 fusion.89
  324.3 1.4 copy.66
  325.8 1.5 convert_multiply_fusion.2
  327.7 3.6 %fusion.88 = (bf16[768,768]{1,0:T(8,128)(2,1)}, f32[768,768]{1,0:T(8,128)}) fusion(f32[768,768]{1,0:T(8,128)S(1)} %copy-done.5, bf16[3072,768]{1,0:T(8,128)(2,1)} %get-tuple-element.32), kind=kLoop, calls=%fused_computation.172 | loop fusion | flops 2359296 | bytes 7077888 | tf_op jit(solution)/shard_map/convert_element_type | solution.py:901
  331.3 1.7 fusion.91
  333.0 3.2 copy.65
  336.2 3.3 convert_add_fusion
  339.5 2.4 copy.63
  342.0 3.6 %bitcast_add_fusion = f32[768,768]{1,0:T(8,128)} fusion(f32[768,768]{1,0:T(8,128)} %param.29, bf16[1536,768]{0,1:T(8,128)(2,1)} %copy.63), kind=kLoop, calls=%fused_computation.8 | loop fusion | flops 1769472 | bytes 5898240 | tf_op jit(solution)/shard_map/add | solution.py:877
  (133 shorter events, 11.6 us)
Async XLA Ops:
  0.7 4.9 %copy-start.1 = (bf16[512,768]{1,0:T(8,128)(2,1)S(1)}, bf16[512,768]{1,0:T(8,128)(2,1)}, u32[]{:S(2)}) copy-start(bf16[512,768]{1,0:T(8,128)(2,1)} %param.17) | copy-start | bytes 2359300
  5.5 1.0 copy-start.12
  6.0 1.7 copy-start.24
  6.5 1.2 copy-start.22
  7.7 1.1 copy-start.19
  7.7 1.1 copy-start.37
  7.8 1.5 copy-start.9
  40.4 1.6 copy-start
  42.5 108.5 %copy-start.28 = (f32[512]{0:T(512)}, f32[512]{0:T(512)S(1)}, u32[]{:S(2)}) copy-start(f32[512]{0:T(512)S(1)} %add_rsqrt_fusion.1) | copy-start | bytes 6148
  45.5 3.1 copy-start.32
  45.5 3.1 copy-start.42
  48.6 7.2 %copy-start.4 = (f32[768,768]{1,0:T(8,128)S(1)}, f32[768,768]{1,0:T(8,128)}, u32[]{:S(2)}) copy-start(f32[768,768]{1,0:T(8,128)} %param.23) | copy-start | bytes 7077892
  55.8 1.7 copy-start.16
  57.4 30.3 %copy-start.33 = (f32[768]{0:T(1024)S(1)}, f32[768]{0:T(1024)}, u32[]{:S(2)}) copy-start(f32[768]{0:T(1024)} %get-tuple-element.84) | copy-start | bytes 9220
  89.6 1.1 copy-start.14
  90.0 2.8 copy-start.30
  92.7 1.5 copy-start.45
  94.2 1.2 copy-start.17
  95.5 1.7 copy-start.6
  151.0 2.8 copy-start.15
  155.2 2.8 copy-start.10
  158.0 0.7 copy-start.38
  158.7 1.9 copy-start.25
  161.6 2.2 copy-start.20
  163.7 0.9 copy-start.23
  164.7 3.5 %copy-start.34 = (f32[1,768]{1,0:T(1,128)S(1)}, f32[1,768]{1,0:T(1,128)}, u32[]{:S(2)}) copy-start(f32[1,768]{1,0:T(1,128)} %stack.31) | copy-start | bytes 9220
  164.7 3.5 %copy-start.35 = (f32[1,768]{1,0:T(1,128)S(1)}, f32[1,768]{1,0:T(1,128)}, u32[]{:S(2)}) copy-start(f32[1,768]{1,0:T(1,128)} %stack.32) | copy-start | bytes 9220
  164.7 3.5 %copy-start.36 = (f32[1,768]{1,0:T(1,128)S(1)}, f32[1,768]{1,0:T(1,128)}, u32[]{:S(2)}) copy-start(f32[1,768]{1,0:T(1,128)} %stack.29) | copy-start | bytes 9220
  170.9 1.0 copy-start.21
  171.9 27.3 %copy-start.44 = (f32[2,192]{1,0:T(2,128)S(1)}, f32[2,192]{1,0:T(2,128)}, u32[]{:S(2)}) copy-start(f32[2,192]{1,0:T(2,128)} %param.31) | copy-start | bytes 4612
  171.9 28.3 %copy-start.29 = (f32[6,768]{1,0:T(8,128)S(1)}, f32[6,768]{1,0:T(8,128)}, u32[]{:S(2)}) copy-start(f32[6,768]{1,0:T(8,128)} %param.33) | copy-start | bytes 55300
  171.9 29.2 %copy-start.41 = (f32[768]{0:T(1024)S(1)}, f32[768]{0:T(1024)}, u32[]{:S(2)}) copy-start(f32[768]{0:T(1024)} %param.32) | copy-start | bytes 9220
  171.9 31.2 %copy-start.27 = (f32[6,768]{1,0:T(8,128)S(1)}, f32[6,768]{1,0:T(8,128)}, u32[]{:S(2)}) copy-start(f32[6,768]{1,0:T(8,128)} %param.26) | copy-start | bytes 55300
  171.9 31.9 %copy-start.18 = (f32[192,768]{1,0:T(8,128)S(1)}, f32[192,768]{1,0:T(8,128)}, u32[]{:S(2)}) copy-start(f32[192,768]{1,0:T(8,128)} %mo.1) | copy-start | bytes 1769476
  199.2 6.5 %copy-start.11 = (bf16[768,768]{1,0:T(8,128)(2,1)S(1)}, bf16[768,768]{1,0:T(8,128)(2,1)}, u32[]{:S(2)}) copy-start(bf16[768,768]{1,0:T(8,128)(2,1)} %get-tuple-element.28.ga) | copy-start | bytes 3538948
  199.4 118.7 %copy-start.40 = (f32[2,192]{1,0:T(2,128)}, f32[2,192]{1,0:T(2,128)S(1)}, u32[]{:S(2)}) copy-start(f32[2,192]{1,0:T(2,128)S(1)} %get-tuple-element.100) | copy-start | bytes 4612
  201.1 4.7 %copy-start.26 = (f32[6,768]{1,0:T(8,128)}, f32[6,768]{1,0:T(8,128)S(1)}, u32[]{:S(2)}) copy-start(f32[6,768]{1,0:T(8,128)S(1)} %get-tuple-element.90) | copy-start | bytes 55300
  201.7 117.0 %copy-start.31 = (f32[768]{0:T(1024)}, f32[768]{0:T(1024)S(1)}, u32[]{:S(2)}) copy-start(f32[768]{0:T(1024)S(1)} %get-tuple-element.102) | copy-start | bytes 9220
  203.8 2.0 copy-start.8
  205.8 1.4 copy-start.13
  314.9 3.2 copy-start.39
  314.9 3.8 %copy-start.43 = (f32[768]{0:T(1024)S(1)}, f32[768]{0:T(1024)}, u32[]{:S(2)}) copy-start(f32[768]{0:T(1024)} %param.25) | copy-start | bytes 9220
  315.0 6.3 %copy-start.3 = (f32[768,768]{0,1:T(8,128)S(1)}, f32[768,768]{0,1:T(8,128)}, u32[]{:S(2)}) copy-start(f32[768,768]{0,1:T(8,128)} %copy.64) | copy-start | bytes 7077892
  325.8 1.9 copy-start.5
  327.7 3.6 %copy-start.7 = (f32[3,768,192]{1,2,0:T(8,128)S(1)}, f32[3,768,192]{1,2,0:T(8,128)}, u32[]{:S(2)}) copy-start(f32[3,768,192]{1,2,0:T(8,128)} %param.20) | copy-start | bytes 5308420
  333.0 3.2 copy-start.2

commit v3 on v2

--- a/solution.py
+++ b/solution.py
@@ -179,13 +179,6 @@
     return [start, combine, settle, pass_on, finish]
 
 
-def line_kernel(x, o, *scratch):
-    t = lax.axis_index("tensor")
-    greet(z_peers(t))
-    for step in line_sum(t, x, o, scratch):
-        step()
-
-
 def params(collective_id):
     return pltpu.CompilerParams(
         collective_id=collective_id, has_side_effects=True, vmem_limit_bytes=VMEM_LIMIT
@@ -194,19 +187,6 @@
 
 IN_VMEM = pl.BlockSpec(memory_space=pltpu.VMEM)
 IN_ANY = pl.BlockSpec(memory_space=pl.ANY)
-
-
-def sum_tensor(partial, collective_id):
-    rows, width = partial.shape
-    return pl.pallas_call(
-        line_kernel,
-        out_shape=jax.ShapeDtypeStruct(partial.shape, partial.dtype),
-        in_specs=[IN_VMEM],
-        out_specs=IN_VMEM,
-        scratch_shapes=line_scratch(rows, width, partial.dtype),
-        compiler_params=params(collective_id),
-        name="sum_tensor",
-    )(partial)
 
 
 def plane_scratch(count, rows, width):
@@ -341,58 +321,328 @@
     return [start, finish]
 
 
-def dp_kernel(count, x, v, o, vo, *scratch):
-    p = lax.axis_index("dp")
-    greet([{"dp": (p + k) % count} for k in range(1, count)])
-    plane = plane_sum(count, p, x, o, scratch[:5])
-    vector = vector_sum("dp", count, p, v, vo, scratch[5:])
-    vector[0]()
-    for step in plane:
-        step()
-    vector[1]()
-
-
-def sum_dp(count, grads, vectors, collective_id):
-    rows, width = grads.shape
-    return pl.pallas_call(
-        functools.partial(dp_kernel, count),
-        out_shape=(
-            jax.ShapeDtypeStruct(grads.shape, BF),
-            jax.ShapeDtypeStruct(vectors.shape, F32),
-        ),
-        in_specs=[IN_VMEM, IN_VMEM],
-        out_specs=(IN_VMEM, IN_VMEM),
-        scratch_shapes=plane_scratch(count, rows, width) + vector_scratch(count, vectors.shape),
-        compiler_params=params(collective_id),
-        name="sum_dp",
-    )(grads, vectors)
-
-
-def both_kernel(count, x, g, o, go, *scratch):
+ROW_STEP = 32
+
+
+def tdot(left, right):
+    return lax.dot_general(left, right, (((0,), (0,)), ((), ())), preferred_element_type=F32)
+
+
+def dot(left, right):
+    return jnp.dot(left, right, preferred_element_type=F32)
+
+
+def dot_t(left, right):
+    return lax.dot_general(left, right, (((1,), (1,)), ((), ())), preferred_element_type=F32)
+
+
+def layer_kernel(
+    count,
+    x, cot, seg, rp, hb, fb, wq_hbm, wo_hbm, wu_hbm, wd_hbm,
+    y, dz1, bt, ga, gb, vec,
+    wq_f, wo_f, wu_f, wd_f, wq, wo, wu, wd,
+    q_s, k_s, v_s, ctx_s, p_s, n1_s, inv1_s, h1l_s, u_s, act_s, slope_s, dz2_s, dm_s, du_s, da_s,
+    dq_s, dk_s, dv_s, part_s, red_s, gap, gbp, vecp, wsem, *scratch,
+):
     p = lax.axis_index("dp")
     t = lax.axis_index("tensor")
+    tokens, width = x.shape
+    half = tokens // 2
+    columns = q_s.shape[1]
+    heads = columns // HD
+    scale = 1.0 / math.sqrt(HD)
     greet(z_peers(t) + [{"dp": (p + k) % count} for k in range(1, count)])
-    line = line_sum(t, x, o, scratch[:6])
-    plane = plane_sum(count, p, g, go, scratch[6:])
-    for steps in zip(line, plane):
-        for step in steps:
-            step()
-
-
-def sum_both(count, partial, grads, collective_id):
+    loads = [
+        pltpu.make_async_copy(source, target, wsem.at[i])
+        for i, (source, target) in enumerate(
+            ((wq_hbm, wq_f), (wo_hbm, wo_f), (wu_hbm, wu_f), (wd_hbm, wd_f))
+        )
+    ]
+    for load in loads:
+        load.start()
+    sums = []
+    for h in range(2):
+        place = pl.ds(h * half, half)
+        sums.append(
+            line_sum(t, part_s.at[place], red_s.at[place], scratch[6 * h : 6 * h + 6])
+        )
+    plane_b = plane_sum(count, p, gbp, gb, scratch[12:17])
+    plane_a = plane_sum(count, p, gap, ga, scratch[17:22])
+    vector = vector_sum("dp", count, p, vecp, vec, scratch[22:25])
+    vecp[...] = jnp.zeros_like(vecp)
+    lane = lax.broadcasted_iota(jnp.int32, (1, columns), 1)
+
+    def in_head(index):
+        return (lane // HD) == index
+
+    def rows_of(h):
+        return pl.ds(h * half, half)
+
+    def over_rows(h, body, init=0):
+        def step(i, carry):
+            first = h * half + i * ROW_STEP
+            return body(pl.ds(pl.multiple_of(first, ROW_STEP), ROW_STEP), carry)
+
+        return lax.fori_loop(0, half // ROW_STEP, step, init)
+
+    def fold(values):
+        return values.reshape(ROW_STEP // 8, 8, values.shape[1]).sum(axis=0)
+
+    def add_vec(row, folded):
+        vecp[row : row + 1, 0 : folded.shape[1]] += jnp.sum(folded, axis=0, keepdims=True)
+
+    def narrow(index, source, target):
+        loads[index].wait()
+        if len(source.shape) == 3:
+            for i in range(source.shape[0]):
+                target[i] = source[i].astype(BF)
+        else:
+            target[...] = source[...].astype(BF)
+
+    def attention(h):
+        r = rows_of(h)
+        xb = x[r]
+        q = (dot(xb, wq[0]) + hb[0:1]).astype(BF)
+        k = dot(xb, wq[1]).astype(BF)
+        v = (dot(xb, wq[2]) + hb[1:2]).astype(BF)
+        q_s[r], k_s[r], v_s[r] = q, k, v
+        down = jnp.broadcast_to(seg[h : h + 1].astype(F32), (half, half))
+        same = down == down.T
+        context = jnp.zeros((half, columns), F32)
+        for index in range(heads):
+            mine = jnp.where(in_head(index), q, jnp.zeros_like(q))
+            scores = jnp.where(same, dot_t(mine, k) * scale, -1e30)
+            expo = jnp.exp(scores - jnp.max(scores, axis=-1, keepdims=True))
+            probs = expo / jnp.sum(expo, axis=-1, keepdims=True)
+            p_s[h * heads + index] = probs
+            context = jnp.where(in_head(index), dot(probs.astype(BF), v), context)
+        low = context.astype(BF)
+        ctx_s[r] = low
+        part_s[r] = dot(low, wo[...]).astype(BF)
+
+    def up(h):
+        def norm(r, carry):
+            z = x[r].astype(F32) + red_s[r].astype(F32) + rp[0:1]
+            center = z - jnp.mean(z, axis=-1, keepdims=True)
+            inverse = lax.rsqrt(jnp.mean(center * center, axis=-1, keepdims=True) + EPS_NORM)
+            normed = center * inverse
+            n1_s[r] = normed
+            inv1_s[r] = jnp.broadcast_to(inverse, (ROW_STEP, 128))
+            h1l_s[r] = (normed * rp[2:3] + rp[3:4]).astype(BF)
+            return carry
+
+        over_rows(h, norm)
+        u_s[rows_of(h)] = dot(h1l_s[rows_of(h)], wu[...])
+
+        def gelu(r, carry):
+            u = u_s[r] + fb[0:1]
+            cdf = 0.5 * (1.0 + lax.erf(u * (1.0 / math.sqrt(2.0))))
+            act_s[r] = (u * cdf).astype(BF)
+            slope_s[r] = cdf + u * jnp.exp(-0.5 * u * u) * (1.0 / math.sqrt(2.0 * math.pi))
+            return carry
+
+        over_rows(h, gelu)
+
+    def down(h):
+        r = rows_of(h)
+        part_s[r] = dot(act_s[r], wd[...]).astype(BF)
+
+    def out_back(h):
+        def norm(r, carry):
+            s_dz2, s_dyn, s_dy = carry
+            h1 = n1_s[r] * rp[2:3] + rp[3:4]
+            z = h1 + red_s[r].astype(F32) + rp[1:2]
+            center = z - jnp.mean(z, axis=-1, keepdims=True)
+            inverse = lax.rsqrt(jnp.mean(center * center, axis=-1, keepdims=True) + EPS_NORM)
+            normed = center * inverse
+            y[r] = (normed * rp[4:5] + rp[5:6]).astype(BF)
+            dy = cot[r].astype(F32)
+            scaled = dy * rp[4:5]
+            first = jnp.mean(scaled, axis=-1, keepdims=True)
+            second = jnp.mean(scaled * normed, axis=-1, keepdims=True)
+            dz2 = inverse * (scaled - first - normed * second)
+            dz2_s[r] = dz2
+            dm_s[r] = dz2.astype(BF)
+            return s_dz2 + fold(dz2), s_dyn + fold(dy * normed), s_dy + fold(dy)
+
+        zero = jnp.zeros((8, width), F32)
+        for row, total in zip((1, 4, 5), over_rows(h, norm, (zero, zero, zero))):
+            add_vec(row, total)
+        u_s[rows_of(h)] = dot_t(dm_s[rows_of(h)], wd[...])
+
+        def slope(r, carry):
+            du = (u_s[r] * slope_s[r]).astype(BF)
+            du_s[r] = du
+            return carry + fold(du.astype(F32))
+
+        add_vec(6, over_rows(h, slope, zero))
+
+    def up_back(h):
+        r = rows_of(h)
+        part_s[r] = dot_t(du_s[r], wu[...]).astype(BF)
+
+    def grads_b():
+        gbp[0:width] = tdot(du_s[...], h1l_s[...]).astype(BF)
+        gbp[width : 2 * width] = tdot(act_s[...], dm_s[...]).astype(BF)
+
+    def attention_back(h):
+        def norm(r, carry):
+            s_dz1, s_dhn, s_dh = carry
+            dh1 = red_s[r].astype(F32) + dz2_s[r]
+            normed = n1_s[r]
+            scaled = dh1 * rp[2:3]
+            first = jnp.mean(scaled, axis=-1, keepdims=True)
+            second = jnp.mean(scaled * normed, axis=-1, keepdims=True)
+            grad = inv1_s[r][:, 0:1] * (scaled - first - normed * second)
+            dz1[r] = grad
+            da_s[r] = grad.astype(BF)
+            return s_dz1 + fold(grad), s_dhn + fold(dh1 * normed), s_dh + fold(dh1)
+
+        zero = jnp.zeros((8, width), F32)
+        for row, total in zip((0, 2, 3), over_rows(h, norm, (zero, zero, zero))):
+            add_vec(row, total)
+        r = rows_of(h)
+        dc = dot_t(da_s[r], wo[...]).astype(BF)
+        q, k, v = q_s[r], k_s[r], v_s[r]
+        dq = dk = dv = jnp.zeros((half, columns), F32)
+        for index in range(heads):
+            probs = p_s[h * heads + index]
+            mine = jnp.where(in_head(index), dc, jnp.zeros_like(dc))
+            dp = dot_t(mine, v)
+            ds = (probs * (dp - jnp.sum(probs * dp, axis=-1, keepdims=True))).astype(BF)
+            dv = jnp.where(in_head(index), tdot(probs.astype(BF), dc), dv)
+            dq = jnp.where(in_head(index), dot(ds, k), dq)
+            dk = jnp.where(in_head(index), tdot(ds, q), dk)
+        dq = (dq * scale).astype(BF)
+        dk = (dk * scale).astype(BF)
+        dv = dv.astype(BF)
+        dq_s[r], dk_s[r], dv_s[r] = dq, dk, dv
+        add_vec(7, jnp.sum(dq.astype(F32), axis=0, keepdims=True))
+        add_vec(8, jnp.sum(dv.astype(F32), axis=0, keepdims=True))
+
+    def grads_a():
+        for i, source in enumerate((dq_s, dk_s, dv_s)):
+            gap[i * columns : (i + 1) * columns] = tdot(source[...], x[...]).astype(BF)
+        gap[3 * columns : 4 * columns] = tdot(ctx_s[...], da_s[...]).astype(BF)
+
+    def back_terms(h):
+        r = rows_of(h)
+        total = dot_t(dq_s[r], wq[0]) + dot_t(dk_s[r], wq[1]) + dot_t(dv_s[r], wq[2])
+        bt[r] = total.astype(BF)
+
+    (a_start, a_mix, a_settle, a_pass, a_end), (b_start, b_mix, b_settle, b_pass, b_end) = sums
+    narrow(0, wq_f, wq)
+    narrow(1, wo_f, wo)
+    attention(0)
+    a_start()
+    attention(1)
+    a_mix()
+    b_start()
+    narrow(2, wu_f, wu)
+    a_settle()
+    b_mix()
+    a_pass()
+    b_settle()
+    narrow(3, wd_f, wd)
+    a_end()
+    up(0)
+    b_pass()
+    down(0)
+    a_start()
+    b_end()
+    up(1)
+    a_mix()
+    down(1)
+    b_start()
+    a_settle()
+    b_mix()
+    a_pass()
+    b_settle()
+    a_end()
+    out_back(0)
+    b_pass()
+    up_back(0)
+    a_start()
+    b_end()
+    out_back(1)
+    a_mix()
+    up_back(1)
+    b_start()
+    grads_b()
+    plane_b[0]()
+    a_settle()
+    b_mix()
+    plane_b[1]()
+    a_pass()
+    b_settle()
+    a_end()
+    attention_back(0)
+    b_pass()
+    b_end()
+    attention_back(1)
+    grads_a()
+    plane_a[0]()
+    vector[0]()
+    plane_b[2]()
+    plane_a[1]()
+    back_terms(0)
+    back_terms(1)
+    plane_b[3]()
+    plane_a[2]()
+    plane_b[4]()
+    plane_a[3]()
+    plane_a[4]()
+    vector[1]()
+
+
+def layer(count, tokens, cotangent, segments, row_params, head_bias, ff_bias, weights, collective_id):
+    rows, width = tokens.shape
+    w_qkv, w_out, w_up, w_down = weights
+    columns = w_qkv.shape[2]
+    heads = columns // HD
+    half = rows // 2
+
+    def low(*shape):
+        return pltpu.VMEM(shape, BF)
+
+    def full(*shape):
+        return pltpu.VMEM(shape, F32)
+
+    def out(shape, dtype):
+        return jax.ShapeDtypeStruct(shape, dtype)
+
+    scratch = (
+        [full(*weight.shape) for weight in weights]
+        + [low(*weight.shape) for weight in weights]
+        + [low(rows, columns)] * 4
+        + [full(2 * heads, half, half), full(rows, width), full(rows, 128), low(rows, width)]
+        + [full(rows, width), low(rows, width), full(rows, width), full(rows, width)]
+        + [low(rows, width)] * 3
+        + [low(rows, columns)] * 3
+        + [low(rows, width)] * 2
+        + [low(4 * columns, width), low(2 * width, width), full(16, width)]
+        + [pltpu.SemaphoreType.DMA((4,))]
+        + line_scratch(half, width, BF) * 2
+        + plane_scratch(count, 2 * width, width)
+        + plane_scratch(count, 4 * columns, width)
+        + vector_scratch(count, (16, width))
+    )
     return pl.pallas_call(
-        functools.partial(both_kernel, count),
+        functools.partial(layer_kernel, count),
         out_shape=(
-            jax.ShapeDtypeStruct(partial.shape, partial.dtype),
-            jax.ShapeDtypeStruct(grads.shape, BF),
+            out((rows, width), BF),
+            out((rows, width), F32),
+            out((rows, width), BF),
+            out((4 * columns, width), BF),
+            out((2 * width, width), BF),
+            out((16, width), F32),
         ),
-        in_specs=[IN_VMEM] * 2,
-        out_specs=(IN_VMEM,) * 2,
-        scratch_shapes=line_scratch(*partial.shape, partial.dtype)
-        + plane_scratch(count, *grads.shape),
+        in_specs=[IN_VMEM] * 6 + [IN_ANY] * 4,
+        out_specs=(IN_VMEM,) * 6,
+        scratch_shapes=scratch,
         compiler_params=params(collective_id),
-        name="sum_both",
-    )(partial, grads)
+        name="layer",
+    )(tokens, cotangent, segments, row_params, head_bias, ff_bias, *weights)
 
 
 def cut(values):
@@ -704,33 +954,6 @@
     )(*moments, ga, gb, squares, back)
 
 
-def layer_norm(values, gain, shift):
-    center = values - jnp.mean(values, axis=-1, keepdims=True)
-    inverse = lax.rsqrt(jnp.mean(center * center, axis=-1, keepdims=True) + EPS_NORM)
-    normed = center * inverse
-    return (normed * gain + shift, normed, inverse)
-
-
-def norm_back(grad_out, normed, inverse, gain):
-    scaled = grad_out * gain
-    first_mean = jnp.mean(scaled, axis=-1, keepdims=True)
-    second_mean = jnp.mean(scaled * normed, axis=-1, keepdims=True)
-    return inverse * (scaled - first_mean - normed * second_mean)
-
-
-def gelu_slope(upward):
-    cdf_part = 0.5 * (1.0 + jax.scipy.special.erf(upward / math.sqrt(2.0)))
-    return cdf_part + upward * jnp.exp(-0.5 * upward * upward) / math.sqrt(2.0 * math.pi)
-
-
-def dot(left, right):
-    return jnp.dot(left, right, preferred_element_type=F32)
-
-
-def tdot(left, right):
-    return lax.dot_general(left, right, (((0,), (0,)), ((), ())), preferred_element_type=F32)
-
-
 def vector_step(param, moment, mean_sq):
     return param - 0.1 * moment * lax.rsqrt(mean_sq + 1e-06)
 
@@ -740,109 +963,18 @@
     w_qkv, w_out, w_up, w_down, head_bias, ff_bias, row_params,
     mom_qkv, mom_out, mom_up, mom_down, mom_heads, mom_ff, mom_params,
 ):
-    tok_count, width = tokens.shape
+    width = tokens.shape[1]
     columns = w_qkv.shape[2]
     ff_cols = w_up.shape[1]
-    local_heads = columns // HD
-    seq_count, seq_len = segments.shape
-    score_scale = 1.0 / math.sqrt(HD)
     tensor_size = lax.axis_size("tensor")
     count = lax.axis_size("dp")
-    wq_low = w_qkv.astype(BF)
-    wo_low = w_out.astype(BF)
-    wu_low = w_up.astype(BF)
-    wd_low = w_down.astype(BF)
-
-    def split_heads(rows):
-        return rows.reshape(seq_count, seq_len, local_heads, HD).transpose(0, 2, 1, 3)
-
-    def join_heads(blocks):
-        return blocks.transpose(0, 2, 1, 3).reshape(tok_count, columns)
-
-    query_h = split_heads((dot(tokens, wq_low[0]) + head_bias[0]).astype(BF))
-    keys_h = split_heads(dot(tokens, wq_low[1]).astype(BF))
-    values_h = split_heads((dot(tokens, wq_low[2]) + head_bias[1]).astype(BF))
-    same_seg = (segments[:, :, None] == segments[:, None, :])[:, None]
-    scores = (
-        jnp.einsum("shqd,shkd->shqk", query_h, keys_h, preferred_element_type=F32) * score_scale
-    )
-    scores = jnp.where(same_seg, scores, -1e30)
-    row_max = jnp.max(scores, axis=-1, keepdims=True)
-    expo = jnp.exp(scores - row_max)
-    probs = expo / jnp.sum(expo, axis=-1, keepdims=True)
-    probs_low = probs.astype(BF)
-    context = jnp.einsum("shqk,shkd->shqd", probs_low, values_h, preferred_element_type=F32)
-    context_low = join_heads(context.astype(BF))
-    attn = sum_tensor(dot(context_low, wo_low).astype(BF), 1).astype(F32)
-    first_in = tokens.astype(F32) + attn + row_params[0]
-    hidden_one, normed_one, inverse_one = layer_norm(first_in, row_params[2], row_params[3])
-    hidden_low = hidden_one.astype(BF)
-    upward = dot(hidden_low, wu_low) + ff_bias
-    activated_low = jax.nn.gelu(upward, approximate=False).astype(BF)
-    mlp = sum_tensor(dot(activated_low, wd_low).astype(BF), 2).astype(F32)
-    second_in = hidden_one + mlp + row_params[1]
-    output_rows, normed_two, inverse_two = layer_norm(second_in, row_params[4], row_params[5])
-    grad_out = cotangent.astype(F32)
-    grad_second = norm_back(grad_out, normed_two, inverse_two, row_params[4])
-    grad_mlp_low = grad_second.astype(BF)
-    grad_act = dot(grad_mlp_low, wd_low.T)
-    grad_up_low = (grad_act * gelu_slope(upward)).astype(BF)
-    grads_b = jnp.concatenate(
-        [tdot(grad_up_low, hidden_low).astype(BF), tdot(activated_low, grad_mlp_low).astype(BF)]
-    )
-    back_hidden, sum_b = sum_both(count, dot(grad_up_low, wu_low.T).astype(BF), grads_b, 3)
-    grad_hidden = back_hidden.astype(F32) + grad_second
-    grad_first = norm_back(grad_hidden, normed_one, inverse_one, row_params[2])
-    grad_attn_low = grad_first.astype(BF)
-    grad_context = split_heads(dot(grad_attn_low, wo_low.T).astype(BF))
-    grad_values = jnp.einsum("shqk,shqd->shkd", probs_low, grad_context, preferred_element_type=F32)
-    grad_probs = jnp.einsum("shqd,shkd->shqk", grad_context, values_h, preferred_element_type=F32)
-    grad_scores = (
-        probs * (grad_probs - jnp.sum(probs * grad_probs, axis=-1, keepdims=True))
-    ).astype(BF)
-    grad_query = (
-        jnp.einsum("shqk,shkd->shqd", grad_scores, keys_h, preferred_element_type=F32) * score_scale
-    )
-    grad_keys = (
-        jnp.einsum("shqk,shqd->shkd", grad_scores, query_h, preferred_element_type=F32)
-        * score_scale
-    )
-    gq_low = join_heads(grad_query.astype(BF))
-    gk_low = join_heads(grad_keys.astype(BF))
-    gv_low = join_heads(grad_values.astype(BF))
-    grads_a = jnp.concatenate(
-        [
-            tdot(jnp.concatenate([gq_low, gk_low, gv_low], axis=1), tokens).astype(BF),
-            tdot(context_low, grad_attn_low).astype(BF),
-        ]
-    )
-
-    def over_rows(values):
-        return jnp.sum(values, axis=0)
-
-    heads_part = jnp.concatenate(
-        [
-            over_rows(gq_low.astype(F32)),
-            over_rows(gv_low.astype(F32)),
-            jnp.zeros((width - 2 * columns,), F32),
-        ]
-    )
-    vectors = jnp.stack(
-        [
-            over_rows(grad_first),
-            over_rows(grad_second),
-            over_rows(grad_hidden * normed_one),
-            over_rows(grad_hidden),
-            over_rows(grad_out * normed_two),
-            over_rows(grad_out),
-            over_rows(grad_up_low.astype(F32)),
-            heads_part,
-        ]
-    )
-    sum_a, vector_total = sum_dp(count, grads_a, vectors, 5)
+    output_rows, grad_first, back_terms, sum_a, sum_b, vector_total = layer(
+        count, tokens, cotangent, segments, row_params, head_bias, ff_bias.reshape(1, ff_cols),
+        (w_qkv, w_out, w_up, w_down), 1,
+    )
     param_sum = vector_total[0:6]
     ff_own = vector_total[6]
-    heads_own = vector_total[7, : 2 * columns].reshape(2, columns)
+    heads_own = vector_total[7:9, :columns]
     new_mom_heads = 0.5 * mom_heads + heads_own
     new_mom_ff = 0.5 * mom_ff + ff_own
     new_mom_params = 0.5 * mom_params + param_sum
@@ -863,10 +995,7 @@
         mom_up.T,
         mom_down,
     )
-    back_terms = dot(gq_low, wq_low[0].T)
-    back_terms = back_terms + dot(gk_low, wq_low[1].T)
-    back_terms = back_terms + dot(gv_low, wq_low[2].T)
-    steps, totals, back = muon(count, moments, sum_a, sum_b, squares, back_terms.astype(BF), 6)
+    steps, totals, back = muon(count, moments, sum_a, sum_b, squares, back_terms, 2)
     grad_inputs = back.astype(F32) + grad_first
 
     def to_qkv(rows):
@@ -893,7 +1022,7 @@
         jnp.mean(new_mom_params * new_mom_params, axis=-1, keepdims=True),
     )
     return (
-        output_rows.astype(BF),
+        output_rows,
         grad_inputs.astype(BF),
         new_mom_qkv, new_qkv, new_qkv.astype(BF),
         new_mom_out, new_out, new_out.astype(BF),

time: 353 us -> 288 us (0.82); the launches traced: 346 us -> 287 us
  matrix products: 27.3 us -> 0 us
  other arithmetic: 45.7 us -> 25 us
  local copies, waits for them, and re-layouts: 31.9 us -> 23.2 us
    dot_general x21 -> x0, matrix products: 26.6 us -> none  [the longest x12 16.8 us: dot(): return jnp.dot(left, right, preferred_element_type=F32)]
    reduce_sum x7 -> x0, other arithmetic: 8.63 us -> none  [the longest x3 4.43 us: over_rows(): return jnp.sum(values, axis=0)]
    add x3 -> x0, other arithmetic: 6.66 us -> none  [the longest x1 3.3 us: local(): new_mom_down = 0.5 * mom_down + sum_b[ff_cols:].astype(F32)]
    another operation x11 -> x1, local copies, waits for them, and re-layouts: 4.96 us -> 0.01 us  [the longest x9 4.87 us: local(): jnp.stack([over_rows(grad_first), over_rows(grad_second), over_rows(grad_...]
    pallas_call x4 -> x1, Pallas kernels: 135 us -> 131 us  [layer(): pl.pallas_call(functools.partial(layer_kernel, count), out_shape=(out((ro...]
    unnamed x100 -> x46, local copies, waits for them, and re-layouts: 15.3 us -> 12.8 us
where the time goes in v3:
time: 288 us; the launch traced here: 287 us
  Pallas kernels  237 us (82%)
  other arithmetic  25 us (9%)
  local copies, waits for them, and re-layouts  23.2 us (8%)
    pallas_call x1, Pallas kernels, layer(): pl.pallas_call(functools.partial(layer_kernel, count), out_shape=(out((ro...  131 us
    pallas_call x1, Pallas kernels, muon(): pl.pallas_call(functools.partial(muon_kernel, count, sizes), out_shape=(j...  106 us
    unnamed x46, local copies, waits for them, and re-layouts  12.8 us

profile of v3, /device:TPU:13, one launch (start us, length us, event | category | flops | bytes accessed | tf_op | source)
XLA Modules:
  0.0 286.9 jit_solution(15298058797884279336)
XLA Ops:
  0.7 1.3 reshape.71.fb
  1.9 2.9 %copy.43.wq_hbm = f32[3,768,192]{2,1,0:T(8,128)} copy(f32[3,768,192]{1,2,0:T(8,128)} %param.20) | data formatting | bytes 3538944 | tf_op args[3]
  4.9 2.0 copy.46
  6.9 3.0 %copy.44 = f32[768,768]{0,1:T(8,128)} copy(f32[768,768]{1,0:T(8,128)} %param.29) | data formatting | bytes 4718592 | tf_op args[12]
  10.0 0.0 copy-start.19
  10.0 0.0 copy-start.13
  10.0 0.0 copy-start.18
  10.0 0.0 copy-start.12
  10.0 131.1 %layer.1 = (bf16[512,768]{1,0:T(8,128)(2,1)}, f32[512,768]{1,0:T(8,128)}, bf16[512,768]{1,0:T(8,128)(2,1)}, bf16[768,768]{1,0:T(8,128)(2,1)}, bf16[1536,768]{1,0:T(8,128)(2,1)}, /*index=5*/f32[16,768]{1,0:T(8,128)}) custom-call(bf16[512,768]{1,0:T(8,128)(2,1)} %x.1, bf16[512,768]{1,0:T(8,128)(2,1)} %cot.1, s32[2,256]{1,0:T(2,128)} %seg.1, f32[6,768]{1,0:T(8,128)} %rp.1, ...), custom_call_target="tpu_custom_call" | custom-call | tf_op jit(solution)/shard_map/layer/pallas_call | solution.py:630
  141.0 0.0 copy-done.19
  141.0 0.8 multiply_reduce_fusion.2
  141.9 0.0 copy-start.17
  141.9 0.8 slice_reduce_fusion
  142.6 0.0 copy-done.13
  142.7 0.9 multiply_reduce_fusion
  143.5 0.0 copy-start.11
  143.5 0.0 copy-done.18
  143.5 0.6 multiply_reduce_fusion.1
  144.2 0.7 pad_maximum_fusion
  144.9 0.7 broadcast_in_dim.5.vs
  145.5 0.0 copy-done.11
  145.5 0.0 copy-done.12
  145.5 0.7 multiply_subtract_fusion.2
  146.2 2.1 slice.41
  148.4 4.3 %copy.45 = bf16[1536,768]{0,1:T(8,128)(2,1)} copy(bf16[1536,768]{1,0:T(8,128)(2,1)} %get-tuple-element.31.gb) | data formatting | bytes 4718592 | tf_op jit(solution)/shard_map/layer/pallas_call | solution.py:630
  152.6 106.2 %muon.1 = (bf16[3072,768]{1,0:T(8,128)(2,1)}, f32[8,128]{1,0:T(8,128)}, bf16[512,768]{1,0:T(8,128)(2,1)}) custom-call(f32[576,768]{1,0:T(8,128)} %bitcast.22, f32[192,768]{1,0:T(8,128)} %mo.1, f32[768,768]{1,0:T(8,128)} %bitcast.20, f32[768,768]{1,0:T(8,128)} %md.1, bf16[768,768]{1,0:T(8,128)(2,1)} %get-tuple-element.30.ga, ...), custom_call_target="tpu_custom_call" | custom-call | tf_op jit(solution)/shard_map/muon/pallas_call | solution.py:942
  258.8 0.0 copy-start
  258.8 1.3 slice.50
  260.9 2.6 add_convert_fusion
  263.5 0.0 copy-done.3
  263.5 0.0 copy-done.4
  263.5 0.0 copy-done
  263.5 0.0 copy-start.16
  263.5 0.0 copy-start.15
  263.5 0.0 copy-start.8
  263.5 0.0 copy-start.9
  263.6 4.2 %bitcast_add_fusion = (f32[768,768]{1,0:T(8,128)}, f32[768,768]{1,0:T(8,128)}) fusion(f32[768,768]{1,0:T(8,128)S(1)} %copy-done.3, bf16[1536,768]{0,1:T(8,128)(2,1)} %copy.45, bf16[1536,768]{1,0:T(8,128)(2,1)S(1)} %copy-done, f32[768,768]{1,0:T(8,128)S(1)} %copy-done.4), kind=kLoop, calls=%fused_computation.1 | loop fusion | flops 3538944 | bytes 11796480 | tf_op jit(solution)/shard_map/add | solution.py:1006
  267.7 0.8 multiply_reduce_fusion.3
  268.5 0.0 copy-done.17
  268.5 0.0 copy-done.16
  268.5 0.6 multiply_subtract_fusion.4
  269.2 0.0 copy-done.14
  269.2 0.0 copy-done.15
  269.2 0.6 multiply_subtract_fusion.3
  269.8 0.0 copy-done.8
  269.8 0.0 copy-done.9
  269.8 2.2 fusion.3
  272.0 3.0 %fusion.2 = (bf16[768,768]{0,1:T(8,128)(2,1)S(1)}, f32[768,768]{0,1:T(8,128)}) fusion(f32[768,768]{0,1:T(8,128)S(1)} %copy.46, bf16[3072,768]{1,0:T(8,128)(2,1)} %get-tuple-element.36), kind=kLoop, calls=%fused_computation.24 | loop fusion | flops 2359296 | bytes 7077888 | tf_op jit(solution)/shard_map/convert_element_type | solution.py:1029
  275.0 1.4 copy.48
  276.5 1.3 convert_multiply_fusion
  277.8 0.0 copy-done.2
  277.8 0.0 copy-start.5
  277.8 0.0 copy-start.6
  277.8 0.0 copy-start.7
  277.8 3.5 %fusion.1 = (bf16[768,768]{1,0:T(8,128)(2,1)}, f32[768,768]{1,0:T(8,128)}) fusion(f32[768,768]{1,0:T(8,128)S(1)} %copy-done.2, bf16[3072,768]{1,0:T(8,128)(2,1)} %get-tuple-element.36), kind=kLoop, calls=%fused_computation.23 | loop fusion | flops 2359296 | bytes 7077888 | tf_op jit(solution)/shard_map/convert_element_type | solution.py:1030
  281.4 0.0 copy-done.5
  281.4 0.0 copy-done.6
  281.4 0.0 copy-done.7
  281.4 0.0 copy-start.1
  281.4 2.3 fusion.4
  283.7 0.4 copy-done.1
  284.1 1.9 copy.47
  286.1 0.0 copy-done.10
  286.1 0.9 copy.50
  (7 shorter events, 0.0 us)
Async XLA Ops:
  10.0 131.1 %copy-start.19 = (f32[2,192]{1,0:T(2,128)S(1)}, f32[2,192]{1,0:T(2,128)}, u32[]{:S(2)}) copy-start(f32[2,192]{1,0:T(2,128)} %param.31) | copy-start | bytes 4612
  10.0 132.7 %copy-start.13 = (f32[6,768]{1,0:T(8,128)S(1)}, f32[6,768]{1,0:T(8,128)}, u32[]{:S(2)}) copy-start(f32[6,768]{1,0:T(8,128)} %param.33) | copy-start | bytes 55300
  10.0 133.6 %copy-start.18 = (f32[768]{0:T(1024)S(1)}, f32[768]{0:T(1024)}, u32[]{:S(2)}) copy-start(f32[768]{0:T(1024)} %param.32) | copy-start | bytes 9220
  10.0 135.6 %copy-start.12 = (f32[6,768]{1,0:T(8,128)S(1)}, f32[6,768]{1,0:T(8,128)}, u32[]{:S(2)}) copy-start(f32[6,768]{1,0:T(8,128)} %rp.1) | copy-start | bytes 55300
  141.9 126.6 %copy-start.17 = (f32[2,192]{1,0:T(2,128)}, f32[2,192]{1,0:T(2,128)S(1)}, u32[]{:S(2)}) copy-start(f32[2,192]{1,0:T(2,128)S(1)} %get-tuple-element.130) | copy-start | bytes 4612
  143.5 2.0 copy-start.11
  144.1 125.0 %copy-start.14 = (f32[768]{0:T(1024)}, f32[768]{0:T(1024)S(1)}, u32[]{:S(2)}) copy-start(f32[768]{0:T(1024)S(1)} %get-tuple-element.132) | copy-start | bytes 9220
  152.6 110.9 %copy-start.3 = (f32[768,768]{1,0:T(8,128)S(1)}, f32[768,768]{1,0:T(8,128)}, u32[]{:S(2)}) copy-start(f32[768,768]{1,0:T(8,128)} %param.29) | copy-start | bytes 7077892
  152.6 110.9 %copy-start.4 = (f32[768,768]{1,0:T(8,128)S(1)}, f32[768,768]{1,0:T(8,128)}, u32[]{:S(2)}) copy-start(f32[768,768]{1,0:T(8,128)} %md.1) | copy-start | bytes 7077892
  258.8 4.7 %copy-start = (bf16[1536,768]{1,0:T(8,128)(2,1)S(1)}, bf16[1536,768]{1,0:T(8,128)(2,1)}, u32[]{:S(2)}) copy-start(bf16[1536,768]{1,0:T(8,128)(2,1)} %get-tuple-element.31.gb) | copy-start | bytes 7077892
  263.5 5.0 %copy-start.16 = (f32[2,192]{1,0:T(2,128)S(1)}, f32[2,192]{1,0:T(2,128)}, u32[]{:S(2)}) copy-start(f32[2,192]{1,0:T(2,128)} %hb.1) | copy-start | bytes 4612
  263.5 5.7 %copy-start.15 = (f32[768]{0:T(1024)S(1)}, f32[768]{0:T(1024)}, u32[]{:S(2)}) copy-start(f32[768]{0:T(1024)} %param.25) | copy-start | bytes 9220
  263.5 6.2 %copy-start.8 = (f32[192,768]{1,0:T(8,128)S(1)}, f32[192,768]{1,0:T(8,128)}, u32[]{:S(2)}) copy-start(f32[192,768]{1,0:T(8,128)} %wo_hbm.1) | copy-start | bytes 1769476
  263.5 6.2 %copy-start.9 = (f32[192,768]{1,0:T(8,128)S(1)}, f32[192,768]{1,0:T(8,128)}, u32[]{:S(2)}) copy-start(f32[192,768]{1,0:T(8,128)} %mo.1) | copy-start | bytes 1769476
  275.0 2.8 copy-start.2
  277.8 3.6 %copy-start.5 = (f32[3,768,192]{1,2,0:T(8,128)S(1)}, f32[3,768,192]{1,2,0:T(8,128)}, u32[]{:S(2)}) copy-start(f32[3,768,192]{1,2,0:T(8,128)} %param.20) | copy-start | bytes 5308420
  277.8 3.6 %copy-start.6 = (f32[3,768,192]{1,2,0:T(8,128)S(1)}, f32[3,768,192]{1,2,0:T(8,128)}, u32[]{:S(2)}) copy-start(f32[3,768,192]{1,2,0:T(8,128)} %param.27) | copy-start | bytes 5308420
  277.8 3.6 %copy-start.7 = (bf16[576,768]{1,0:T(8,128)(2,1)S(1)}, bf16[576,768]{1,0:T(8,128)(2,1)}, u32[]{:S(2)}) copy-start(bf16[576,768]{1,0:T(8,128)(2,1)} %slice.41) | copy-start | bytes 2654212
  281.4 2.7 copy-start.1
  284.1 1.9 copy-start.10

commit v4 on v3

--- a/solution.py
+++ b/solution.py
@@ -17,7 +17,6 @@
 F32 = jnp.float32
 MESH = pl.DeviceIdType.MESH
 SUBS = 2
-VMEM_LIMIT = 56 * 1024 * 1024
 PLACE = (1, 2, 0, 3)
 
 
@@ -179,9 +178,11 @@
     return [start, combine, settle, pass_on, finish]
 
 
-def params(collective_id):
+def params(collective_id, mebibytes):
     return pltpu.CompilerParams(
-        collective_id=collective_id, has_side_effects=True, vmem_limit_bytes=VMEM_LIMIT
+        collective_id=collective_id,
+        has_side_effects=True,
+        vmem_limit_bytes=mebibytes * 1024 * 1024,
     )
 
 
@@ -288,6 +289,249 @@
     return [start, pair_up, settle, pass_on, finish]
 
 
+def reduce_scratch(rows, width):
+    side = width // 2
+    return [
+        pltpu.VMEM((rows, side), BF),
+        pltpu.VMEM((rows, side), BF),
+        pltpu.VMEM((2 * rows, side), BF),
+        pltpu.SemaphoreType.DMA((2, 8)),
+        pltpu.SemaphoreType.DMA((2, 8)),
+    ]
+
+
+def square_reduce(p, x, kept, matrices, scratch):
+    from_mate, paired, taken, ssem, rsem = scratch
+    side = from_mate.shape[1]
+    pair = p // 2
+    core = p % 2
+    mate = {"dp": p + 1 - 2 * core}
+
+    def away_from(place, away):
+        return {"dp": 2 * (place ^ away) + core}
+
+    def cols_of(which):
+        return pl.ds(pl.multiple_of(which * side, side), side)
+
+    def give(m):
+        _, first, rows = matrices[m]
+        spot = pl.ds(first, rows)
+        return remote(x.at[spot, cols_of(1 - core)], from_mate.at[spot], ssem.at[m, 0], rsem.at[m, 0], mate)
+
+    def part_of(m, part):
+        _, first, rows = matrices[m]
+        return pl.ds(first + part * (rows // 2), rows // 2)
+
+    def slot(m, near, part):
+        _, first, rows = matrices[m]
+        return pl.ds(2 * first + near * rows + part * (rows // 2), rows // 2)
+
+    def opposite_send(m, part):
+        place = matrices[m][0]
+        return remote(
+            paired.at[part_of(m, part)], taken.at[slot(m, 0, part)],
+            ssem.at[m, 1 + part], rsem.at[m, 1], away_from(place, 1 + part),
+        )
+
+    def near_raw(m, near):
+        part = 1 - near
+        return remote(
+            paired.at[part_of(m, part)], taken.at[slot(m, near, part)],
+            ssem.at[m, 1], rsem.at[m, 2 + 2 * near], away_from(matrices[m][0], 0),
+        )
+
+    def near_mixed(m, near):
+        part = near
+        return remote(
+            paired.at[part_of(m, part)], taken.at[slot(m, near, part)],
+            ssem.at[m, 2], rsem.at[m, 3 + 2 * near], away_from(matrices[m][0], 0),
+        )
+
+    def swap(m):
+        spot = kept.at[pl.ds(0, matrices[m][2]), cols_of(core)]
+        return remote(spot, spot, ssem.at[m, 6], rsem.at[m, 6], mate)
+
+    def arrived(ref, m, index):
+        remote(ref, ref, ssem.at[m, 0], rsem.at[m, index], mate).wait_recv()
+
+    def role(m, away):
+        return pl.when(pair == (matrices[m][0] ^ away))
+
+    every = range(len(matrices))
+
+    def start():
+        for m in every:
+            give(m).start()
+
+    def pair_up():
+        for m in every:
+            _, first, rows = matrices[m]
+            spot = pl.ds(first, rows)
+            give(m).wait_recv()
+            total = x[spot, cols_of(core)].astype(F32) + from_mate[spot].astype(F32)
+            paired[spot] = total.astype(BF)
+
+            @role(m, 3)
+            def _(m=m):
+                for part in range(2):
+                    opposite_send(m, part).start()
+
+            for near in range(2):
+
+                @role(m, 1 + near)
+                def _(m=m, near=near):
+                    near_raw(m, near).start()
+
+    def mix():
+        for m in every:
+            for near in range(2):
+
+                @role(m, 1 + near)
+                def _(m=m, near=near):
+                    piece = slot(m, 0, near)
+                    arrived(taken.at[piece], m, 1)
+                    spot = part_of(m, near)
+                    total = paired[spot].astype(F32) + taken[piece].astype(F32)
+                    paired[spot] = total.astype(BF)
+                    near_mixed(m, near).start()
+
+    def settle():
+        for m in every:
+
+            @role(m, 0)
+            def _(m=m):
+                _, first, rows = matrices[m]
+                for near in range(2):
+                    arrived(taken.at[slot(m, near, 1 - near)], m, 2 + 2 * near)
+                    arrived(taken.at[slot(m, near, near)], m, 3 + 2 * near)
+                spot = pl.ds(first, rows)
+                total = x[spot, cols_of(core)].astype(F32) + from_mate[spot].astype(F32)
+                for near in range(2):
+                    total = total + taken[pl.ds(2 * first + near * rows, rows)].astype(F32)
+                kept[pl.ds(0, rows), cols_of(core)] = total.astype(BF)
+                swap(m).start()
+
+    def finish():
+        for m in every:
+            rows = matrices[m][2]
+            give(m).wait_send()
+
+            @role(m, 0)
+            def _(m=m, rows=rows):
+                arrived(kept.at[pl.ds(0, rows), cols_of(1 - core)], m, 6)
+                swap(m).wait_send()
+
+            @role(m, 3)
+            def _(m=m):
+                for part in range(2):
+                    opposite_send(m, part).wait_send()
+
+            for near in range(2):
+
+                @role(m, 1 + near)
+                def _(m=m, near=near):
+                    near_raw(m, near).wait_send()
+                    near_mixed(m, near).wait_send()
+
+    return [start, pair_up, mix, settle, finish]
+
+
+def gather_scratch():
+    return [pltpu.SemaphoreType.DMA((4, 2, 4))] * 2
+
+
+def square_gather(p, sizes, out, own, scratch):
+    ssem, rsem = scratch
+    width = out.shape[1]
+    pair = p // 2
+    core = p % 2
+    mate = {"dp": p + 1 - 2 * core}
+    firsts = [sum(sizes[:index]) for index in range(4)]
+
+    def piece(index, side, part):
+        rows = sizes[index]
+        if index == 2:
+            across = pl.ds(pl.multiple_of(side * (width // 2), width // 2), width // 2)
+            return out.at[pl.ds(firsts[index] + part * (rows // 2), rows // 2), across]
+        quarter = rows // 4
+        first = firsts[index] + side * 2 * quarter + part * quarter
+        return out.at[pl.ds(pl.multiple_of(first, quarter), quarter)]
+
+    def copy(index, part, route, device):
+        spot = piece(index, core, part)
+        return remote(spot, spot, ssem.at[index, part, route], rsem.at[index, part, route], device)
+
+    def other(away):
+        return {"dp": 2 * (pair + away * (1 - 2 * ((pair // away) % 2))) + core}
+
+    def role(index, away):
+        return pl.when(pair == (PLACE[index] ^ away))
+
+    def wait_in(index, part, route, side):
+        spot = piece(index, side, part)
+        remote(spot, spot, ssem.at[index, part, route], rsem.at[index, part, route], mate).wait_recv()
+
+    ways = ((1, 0, 2), (2, 1, 1))
+
+    def start():
+        for index in range(4):
+
+            @role(index, 0)
+            def _(index=index):
+                for part in range(2):
+                    piece(index, core, part)[...] = own(index, part)
+                for part in range(2):
+                    copy(index, part, 0, other(1)).start()
+                    copy(index, 1 - part, 1, other(2)).start()
+                for part in range(2):
+                    copy(index, part, 3, mate).start()
+
+    def pass_on():
+        for index in range(4):
+            for away, route, onward in ways:
+
+                @role(index, away)
+                def _(index=index, away=away, route=route, onward=onward):
+                    wait_in(index, away - 1, route, core)
+                    copy(index, away - 1, 2, other(onward)).start()
+                    copy(index, away - 1, 3, mate).start()
+
+    def rest():
+        for index in range(4):
+            for away, route, _ in ways:
+
+                @role(index, away)
+                def _(index=index, away=away, route=route):
+                    wait_in(index, 2 - away, route, core)
+                    copy(index, 2 - away, 3, mate).start()
+
+            @role(index, 3)
+            def _(index=index):
+                for part in range(2):
+                    wait_in(index, part, 2, core)
+                    copy(index, part, 3, mate).start()
+
+    def finish():
+        for index in range(4):
+            for part in range(2):
+                wait_in(index, part, 3, 1 - core)
+                copy(index, part, 3, mate).wait_send()
+
+            @role(index, 0)
+            def _(index=index):
+                for part in range(2):
+                    copy(index, part, 0, other(1)).wait_send()
+                    copy(index, part, 1, other(2)).wait_send()
+
+            for away, _, onward in ways:
+
+                @role(index, away)
+                def _(index=index, away=away, onward=onward):
+                    copy(index, away - 1, 2, other(onward)).wait_send()
+
+    return [start, pass_on, rest, finish]
+
+
 def vector_scratch(count, shape):
     return [
         pltpu.VMEM((count,) + shape, F32),
@@ -338,8 +582,8 @@
 
 def layer_kernel(
     count,
-    x, cot, seg, rp, hb, fb, wq_hbm, wo_hbm, wu_hbm, wd_hbm,
-    y, dz1, bt, ga, gb, vec,
+    x, cot, seg, rp, hb, fb, mh, mf, wq_hbm, wo_hbm, wu_hbm, wd_hbm,
+    y, dz1, bt, grads, vec, squares,
     wq_f, wo_f, wu_f, wd_f, wq, wo, wu, wd,
     q_s, k_s, v_s, ctx_s, p_s, n1_s, inv1_s, h1l_s, u_s, act_s, slope_s, dz2_s, dm_s, du_s, da_s,
     dq_s, dk_s, dv_s, part_s, red_s, gap, gbp, vecp, wsem, *scratch,
@@ -366,8 +610,15 @@
         sums.append(
             line_sum(t, part_s.at[place], red_s.at[place], scratch[6 * h : 6 * h + 6])
         )
-    plane_b = plane_sum(count, p, gbp, gb, scratch[12:17])
-    plane_a = plane_sum(count, p, gap, ga, scratch[17:22])
+    top = 4 * columns
+    if count == 8:
+        ends = [(PLACE[2], 0, width), (PLACE[3], width, width)]
+        plane_b = square_reduce(p, gbp, grads, ends, scratch[12:17])
+        ends = [(PLACE[0], 0, 3 * columns), (PLACE[1], 3 * columns, columns)]
+        plane_a = square_reduce(p, gap, grads, ends, scratch[17:22])
+    else:
+        plane_b = plane_sum(count, p, gbp, grads.at[pl.ds(top, 2 * width)], scratch[12:17])
+        plane_a = plane_sum(count, p, gap, grads.at[pl.ds(0, top)], scratch[17:22])
     vector = vector_sum("dp", count, p, vecp, vec, scratch[22:25])
     vecp[...] = jnp.zeros_like(vecp)
     lane = lax.broadcasted_iota(jnp.int32, (1, columns), 1)
@@ -402,9 +653,9 @@
     def attention(h):
         r = rows_of(h)
         xb = x[r]
-        q = (dot(xb, wq[0]) + hb[0:1]).astype(BF)
-        k = dot(xb, wq[1]).astype(BF)
-        v = (dot(xb, wq[2]) + hb[1:2]).astype(BF)
+        q = (dot_t(xb, wq[0]) + hb[0:1]).astype(BF)
+        k = dot_t(xb, wq[1]).astype(BF)
+        v = (dot_t(xb, wq[2]) + hb[1:2]).astype(BF)
         q_s[r], k_s[r], v_s[r] = q, k, v
         down = jnp.broadcast_to(seg[h : h + 1].astype(F32), (half, half))
         same = down == down.T
@@ -482,7 +733,7 @@
         part_s[r] = dot_t(du_s[r], wu[...]).astype(BF)
 
     def grads_b():
-        gbp[0:width] = tdot(du_s[...], h1l_s[...]).astype(BF)
+        gbp[0:width] = tdot(h1l_s[...], du_s[...]).astype(BF)
         gbp[width : 2 * width] = tdot(act_s[...], dm_s[...]).astype(BF)
 
     def attention_back(h):
@@ -527,7 +778,7 @@
 
     def back_terms(h):
         r = rows_of(h)
-        total = dot_t(dq_s[r], wq[0]) + dot_t(dk_s[r], wq[1]) + dot_t(dv_s[r], wq[2])
+        total = dot(dq_s[r], wq[0]) + dot(dk_s[r], wq[1]) + dot(dv_s[r], wq[2])
         bt[r] = total.astype(BF)
 
     (a_start, a_mix, a_settle, a_pass, a_end), (b_start, b_mix, b_settle, b_pass, b_end) = sums
@@ -576,6 +827,8 @@
     a_pass()
     b_settle()
     a_end()
+    if count == 8:
+        plane_b[2]()
     attention_back(0)
     b_pass()
     b_end()
@@ -583,24 +836,31 @@
     grads_a()
     plane_a[0]()
     vector[0]()
-    plane_b[2]()
+    if count != 8:
+        plane_b[2]()
     plane_a[1]()
     back_terms(0)
     back_terms(1)
     plane_b[3]()
     plane_a[2]()
+    vector[1]()
+    moved = 0.5 * mh[...] + vec[7:9, 0:columns]
+    squares[0:2] = jnp.broadcast_to(jnp.sum(moved * moved, axis=1, keepdims=True), (2, 128))
+    moved = 0.5 * mf[...] + vec[6:7]
+    squares[2:3] = jnp.broadcast_to(jnp.sum(moved * moved, axis=1, keepdims=True), (1, 128))
+    squares[3:8] = jnp.zeros((5, 128), F32)
+    plane_a[3]()
     plane_b[4]()
-    plane_a[3]()
     plane_a[4]()
-    vector[1]()
-
-
-def layer(count, tokens, cotangent, segments, row_params, head_bias, ff_bias, weights, collective_id):
+
+
+def layer(count, tokens, cotangent, segments, small, weights, collective_id):
     rows, width = tokens.shape
     w_qkv, w_out, w_up, w_down = weights
-    columns = w_qkv.shape[2]
+    columns = w_qkv.shape[1]
     heads = columns // HD
     half = rows // 2
+    grads = width if count == 8 else 4 * columns + 2 * width
 
     def low(*shape):
         return pltpu.VMEM(shape, BF)
@@ -623,8 +883,12 @@
         + [low(4 * columns, width), low(2 * width, width), full(16, width)]
         + [pltpu.SemaphoreType.DMA((4,))]
         + line_scratch(half, width, BF) * 2
-        + plane_scratch(count, 2 * width, width)
-        + plane_scratch(count, 4 * columns, width)
+        + (reduce_scratch(2 * width, width) if count == 8 else plane_scratch(count, 2 * width, width))
+        + (
+            reduce_scratch(4 * columns, width)
+            if count == 8
+            else plane_scratch(count, 4 * columns, width)
+        )
         + vector_scratch(count, (16, width))
     )
     return pl.pallas_call(
@@ -633,16 +897,16 @@
             out((rows, width), BF),
             out((rows, width), F32),
             out((rows, width), BF),
-            out((4 * columns, width), BF),
-            out((2 * width, width), BF),
+            out((grads, width), BF),
             out((16, width), F32),
+            out((8, 128), F32),
         ),
-        in_specs=[IN_VMEM] * 6 + [IN_ANY] * 4,
+        in_specs=[IN_VMEM] * 8 + [IN_ANY] * 4,
         out_specs=(IN_VMEM,) * 6,
         scratch_shapes=scratch,
-        compiler_params=params(collective_id),
+        compiler_params=params(collective_id, 56),
         name="layer",
-    )(tokens, cotangent, segments, row_params, head_bias, ff_bias, *weights)
+    )(tokens, cotangent, segments, *small, *weights)
 
 
 def cut(values):
@@ -659,9 +923,9 @@
 
 def muon_kernel(
     count, sizes,
-    mq, mo, mu, md, ga, gb, vs, bx,
-    xo, vt, bo,
-    zf, gf, zh, zl, gx, go, gp, af, ah, al, dh, dl, sf, sh, sl, xf, lsem, psem, asem_s, asem_r, *scratch,
+    mq, mo, mu, md, grads, vs, bx, dz1,
+    xo, gall, vt, bo,
+    zf, gf, zh, zl, gx, go, gp, af, ah, al, dh, dl, sf, sh, sl, xf, bs, lsem, psem, *scratch,
 ):
     p = lax.axis_index("dp")
     t = lax.axis_index("tensor")
@@ -669,41 +933,60 @@
     group = count // 4
     which = p // group
     core = p % 2
-    pairs = count // 2
-    pair = p // 2
     mate = {"dp": p + 1 - 2 * core}
     share = xf.shape[0]
     tile = width // 3
     greet(z_peers(t) + [{"dp": (p + k) % count} for k in range(1, count)])
-    vector = vector_sum("tensor", 4, t, vs, vt, scratch[12:])
-    back = line_sum(t, bx, bo, scratch[6:12])
+    vector = vector_sum("tensor", 4, t, vs, vt, scratch[12:15])
+    back = line_sum(t, bx, bs, scratch[6:12])
     vector[0]()
-    qkv_rows, out_rows, _, _ = sizes
-    gsrc = (
-        (ga, 0, qkv_rows), (ga, qkv_rows, out_rows), (gb, 0, width), (gb, width, width)
-    )
+    firsts = [sum(sizes[:index]) for index in range(4)]
     for index, moment in enumerate((mq, mo, mu, md)):
-        grads, first, rows = gsrc[index]
+        rows = sizes[index]
+        first = 0 if count == 8 else firsts[index]
 
         @pl.when(which == PLACE[index])
-        def _(moment=moment, grads=grads, first=first, rows=rows):
-            one = pltpu.make_async_copy(moment, zf.at[pl.ds(0, rows)], lsem.at[0])
+        def _(index=index, moment=moment, first=first, rows=rows):
+            one = pltpu.make_async_copy(moment, sf.at[pl.ds(0, rows)], lsem.at[0])
             two = pltpu.make_async_copy(
                 grads.at[pl.ds(first, rows)], gf.at[pl.ds(0, rows)], lsem.at[1]
             )
             one.start()
             two.start()
-            if rows < width:
-                zf[pl.ds(rows, width - rows)] = jnp.zeros((width - rows, width), F32)
-                gf[pl.ds(rows, width - rows)] = jnp.zeros((width - rows, width), BF)
             one.wait()
             two.wait()
-
-    for i in range(3):
-        spot = pl.ds(i * tile, tile)
-        z = 0.5 * zf[spot] + gf[spot].astype(F32)
-        zf[spot] = z
-        zh[spot], zl[spot] = cut(z)
+            for i in range(3):
+                spot = pl.ds(i * (rows // 3), rows // 3)
+                z = 0.5 * sf[spot] + gf[spot].astype(F32)
+                if index == 2:
+                    z = z.T
+                    spot = (pl.ds(0, width), spot)
+                zf[spot] = z
+                zh[spot], zl[spot] = cut(z)
+            if rows < width:
+                spot = pl.ds(rows, width - rows)
+                zf[spot] = jnp.zeros((width - rows, width), F32)
+                zh[spot] = jnp.zeros((width - rows, width), BF)
+                zl[spot] = jnp.zeros((width - rows, width), BF)
+
+    if count == 8:
+
+        def own_gradient(index, part):
+            if index == 2:
+                across = pl.ds(pl.multiple_of(core * (width // 2), width // 2), width // 2)
+                return gf[pl.ds(part * (width // 2), width // 2), across]
+            quarter = sizes[index] // 4
+            first = pl.multiple_of((2 * core + part) * quarter, quarter)
+            return gf[pl.ds(first, quarter)]
+
+        def own_step(index, part):
+            if index == 2:
+                return xf[:, pl.ds(part * (width // 2), width // 2)].T.astype(BF)
+            quarter = sizes[index] // 4
+            return xf[pl.ds(part * quarter, quarter)].astype(BF)
+
+        spread = square_gather(p, sizes, gall, own_gradient, scratch[15:17])
+        spread[0]()
 
     def cols(index):
         return pl.ds(pl.multiple_of(index * tile, tile), tile)
@@ -790,95 +1073,22 @@
         product((sh, sl), (dh, dl), sf, coef_a, 1.0, (ah, al, af))
         for i in range(1, 4):
             pl.when(k == i - 1)(back[i])
+            if count == 8 and i < 3:
+                pl.when(k == i - 1)(spread[i])
         return carry
 
     lax.fori_loop(0, 4, sweep, 0)
     make_d()
     move_x()
     back[4]()
-
-    if pairs == 4:
-        gather_square(pair, core, mate, sizes, xf, xo, asem_s, asem_r)
+    bo[...] = (bs[...].astype(F32) + dz1[...]).astype(BF)
+    if count == 8:
+        spread[3]()
+        for step in square_gather(p, sizes, xo, own_step, scratch[17:19]):
+            step()
     else:
-        gather_any(p, core, pairs, mate, xf, xo, asem_s, asem_r)
-
-
-def gather_square(pair, core, mate, sizes, xf, xo, ssem, rsem):
-    width = xf.shape[1]
-
-    def piece(index, side, part):
-        half = sizes[index] // 4
-        first = index * width + side * 2 * half + part * half
-        return xo.at[pl.ds(pl.multiple_of(first, half), half)]
-
-    def copy(index, part, route, device):
-        spot = piece(index, core, part)
-        return remote(spot, spot, ssem.at[index, part, route], rsem.at[index, part, route], device)
-
-    def other(away):
-        return {"dp": 2 * (pair + away * (1 - 2 * ((pair // away) % 2))) + core}
-
-    def place_is(index, away):
-        return pair == (PLACE[index] ^ away)
-
-    def wait_in(index, part, route, side):
-        spot = piece(index, side, part)
-        remote(spot, spot, ssem.at[index, part, route], rsem.at[index, part, route], mate).wait_recv()
-
-    for index, rows in enumerate(sizes):
-        half = rows // 4
-
-        @pl.when(place_is(index, 0))
-        def _(index=index, half=half):
-            for part in range(2):
-                piece(index, core, part)[...] = xf[pl.ds(part * half, half)].astype(BF)
-            for part in range(2):
-                copy(index, part, 0, other(1)).start()
-                copy(index, 1 - part, 1, other(2)).start()
-            for part in range(2):
-                copy(index, part, 3, mate).start()
-
-    for index in range(4):
-        for away, route, onward in ((1, 0, 2), (2, 1, 1)):
-
-            @pl.when(place_is(index, away))
-            def _(index=index, away=away, route=route, onward=onward):
-                first = away - 1
-                wait_in(index, first, route, core)
-                copy(index, first, 2, other(onward)).start()
-                copy(index, first, 3, mate).start()
-
-    for index in range(4):
-        for away, route, onward in ((1, 0, 2), (2, 1, 1)):
-
-            @pl.when(place_is(index, away))
-            def _(index=index, away=away, route=route):
-                second = 2 - away
-                wait_in(index, second, route, core)
-                copy(index, second, 3, mate).start()
-
-        @pl.when(place_is(index, 3))
-        def _(index=index):
-            for part in range(2):
-                wait_in(index, part, 2, core)
-                copy(index, part, 3, mate).start()
-
-    for index in range(4):
-        for part in range(2):
-            wait_in(index, part, 3, 1 - core)
-            copy(index, part, 3, mate).wait_send()
-
-        @pl.when(place_is(index, 0))
-        def _(index=index):
-            for part in range(2):
-                copy(index, part, 0, other(1)).wait_send()
-                copy(index, part, 1, other(2)).wait_send()
-
-        for away, onward in ((1, 2), (2, 1)):
-
-            @pl.when(place_is(index, away))
-            def _(index=index, away=away, onward=onward):
-                copy(index, away - 1, 2, other(onward)).wait_send()
+        gall[...] = jnp.zeros_like(gall)
+        gather_any(p, core, count // 2, mate, xf, xo, scratch[15], scratch[16])
 
 
 def gather_any(p, core, pairs, mate, xf, xo, asem_s, asem_r):
@@ -918,40 +1128,45 @@
         hand(k).wait_send()
 
 
-def muon(count, moments, ga, gb, squares, back, collective_id):
-    width = ga.shape[1]
+def muon(count, moments, grads, squares, back, grad_first, collective_id):
+    width = grads.shape[1]
     tile = width // 3
     share = width // (count // 4)
-    pairs = count // 2
     sizes = tuple(moment.shape[0] for moment in moments)
+    square = count == 8
 
     def vmem(dtype, rows=width, columns=width):
         return pltpu.VMEM((rows, columns), dtype)
 
+    def out(shape, dtype):
+        return jax.ShapeDtypeStruct(shape, dtype)
+
+    pair_sems = [pltpu.SemaphoreType.DMA((2, count // 2))] * 2
     scratch = (
         [vmem(F32), vmem(BF), vmem(BF), vmem(BF)]
         + [vmem(F32, tile)] * 3
         + [vmem(F32), vmem(BF), vmem(BF), vmem(BF), vmem(BF), vmem(F32), vmem(BF), vmem(BF)]
-        + [vmem(F32, share)]
+        + [vmem(F32, share), vmem(BF, back.shape[0])]
         + [pltpu.SemaphoreType.DMA((2,)), pltpu.SemaphoreType.DMA((2,))]
-        + [pltpu.SemaphoreType.DMA((4, 2, 4) if pairs == 4 else (2, pairs))] * 2
         + line_scratch(tile, width, F32)
         + line_scratch(*back.shape, BF)
         + vector_scratch(4, squares.shape)
+        + (gather_scratch() * 2 if square else pair_sems)
     )
     return pl.pallas_call(
         functools.partial(muon_kernel, count, sizes),
         out_shape=(
-            jax.ShapeDtypeStruct((4 * width, width), BF),
-            jax.ShapeDtypeStruct(squares.shape, F32),
-            jax.ShapeDtypeStruct(back.shape, BF),
+            out((sum(sizes) if square else 4 * width, width), BF),
+            out((sum(sizes), width) if square else (16, width), BF),
+            out(squares.shape, F32),
+            out(back.shape, BF),
         ),
-        in_specs=[IN_ANY] * 6 + [IN_VMEM] * 2,
-        out_specs=(IN_VMEM,) * 3,
+        in_specs=[IN_ANY] * 5 + [IN_VMEM] * 3,
+        out_specs=(IN_VMEM,) * 4,
         scratch_shapes=scratch,
-        compiler_params=params(collective_id),
+        compiler_params=params(collective_id, 44),
         name="muon",
-    )(*moments, ga, gb, squares, back)
+    )(*moments, grads, squares, back, grad_first)
 
 
 def vector_step(param, moment, mean_sq):
@@ -968,51 +1183,44 @@
     ff_cols = w_up.shape[1]
     tensor_size = lax.axis_size("tensor")
     count = lax.axis_size("dp")
-    output_rows, grad_first, back_terms, sum_a, sum_b, vector_total = layer(
-        count, tokens, cotangent, segments, row_params, head_bias, ff_bias.reshape(1, ff_cols),
-        (w_qkv, w_out, w_up, w_down), 1,
+    qkv_rows = 3 * columns
+    wq_rows = w_qkv.transpose(0, 2, 1)
+    output_rows, grad_first, back_terms, grads, vector_total, squares = layer(
+        count, tokens, cotangent, segments,
+        (row_params, head_bias, ff_bias.reshape(1, ff_cols), mom_heads, mom_ff.reshape(1, ff_cols)),
+        (wq_rows, w_out, w_up, w_down), 1,
     )
-    param_sum = vector_total[0:6]
-    ff_own = vector_total[6]
-    heads_own = vector_total[7:9, :columns]
-    new_mom_heads = 0.5 * mom_heads + heads_own
-    new_mom_ff = 0.5 * mom_ff + ff_own
-    new_mom_params = 0.5 * mom_params + param_sum
-    squares = jnp.broadcast_to(
-        jnp.concatenate(
-            [
-                jnp.sum(new_mom_heads * new_mom_heads, axis=1),
-                jnp.sum(new_mom_ff * new_mom_ff)[None],
-                jnp.zeros((5,), F32),
-            ]
-        )[:, None],
-        (8, 128),
+    new_mom_heads = 0.5 * mom_heads + vector_total[7:9, :columns]
+    new_mom_ff = 0.5 * mom_ff + vector_total[6]
+    new_mom_params = 0.5 * mom_params + vector_total[0:6]
+    moments = (mom_qkv.transpose(0, 2, 1).reshape(qkv_rows, width), mom_out, mom_up, mom_down)
+    steps, gathered, totals, grad_inputs = muon(
+        count, moments, grads, squares, back_terms, grad_first, 2
     )
-    qkv_rows = 3 * columns
-    moments = (
-        mom_qkv.transpose(0, 2, 1).reshape(qkv_rows, width),
-        mom_out,
-        mom_up.T,
-        mom_down,
-    )
-    steps, totals, back = muon(count, moments, sum_a, sum_b, squares, back_terms, 2)
-    grad_inputs = back.astype(F32) + grad_first
+    if count == 8:
+        grads = gathered
 
     def to_qkv(rows):
         return rows.reshape(3, columns, width).transpose(0, 2, 1)
 
-    new_mom_qkv = 0.5 * mom_qkv + to_qkv(sum_a[:qkv_rows].astype(F32))
-    new_mom_out = 0.5 * mom_out + sum_a[qkv_rows:].astype(F32)
-    new_mom_up = 0.5 * mom_up + sum_b[:ff_cols].astype(F32).T
-    new_mom_down = 0.5 * mom_down + sum_b[ff_cols:].astype(F32)
+    bounds = (0, qkv_rows, qkv_rows + columns, qkv_rows + columns + width)
+
+    def grad_of(index, rows):
+        return grads[bounds[index] : bounds[index] + rows].astype(F32)
+
     def step_of(index, rows):
-        first = (index if count == 8 else PLACE[index]) * width
-        return steps[first : first + rows].astype(F32)
-
+        first = bounds[index] if count == 8 else PLACE[index] * width
+        part = steps[first : first + rows].astype(F32)
+        return part.T if index == 2 and count != 8 else part
+
+    new_mom_qkv = 0.5 * mom_qkv + to_qkv(grad_of(0, qkv_rows))
+    new_mom_out = 0.5 * mom_out + grad_of(1, columns)
+    new_mom_up = 0.5 * mom_up + grad_of(2, width)
+    new_mom_down = 0.5 * mom_down + grad_of(3, ff_cols)
     wide = math.sqrt(ff_cols * tensor_size / width)
     new_qkv = w_qkv - 0.8 * math.sqrt(3.0) * to_qkv(step_of(0, qkv_rows))
     new_out = w_out - 0.8 * step_of(1, columns)
-    new_up = w_up - 0.8 * wide * step_of(2, ff_cols).T
+    new_up = w_up - 0.8 * wide * step_of(2, width)
     new_down = w_down - 0.8 * wide * step_of(3, ff_cols)
     new_heads = vector_step(head_bias, new_mom_heads, totals[0:2, 0:1] / (columns * tensor_size))
     new_ff = vector_step(ff_bias, new_mom_ff, totals[2, 0] / (ff_cols * tensor_size))
@@ -1023,7 +1231,7 @@
     )
     return (
         output_rows,
-        grad_inputs.astype(BF),
+        grad_inputs,
         new_mom_qkv, new_qkv, new_qkv.astype(BF),
         new_mom_out, new_out, new_out.astype(BF),
         new_mom_up, new_up, new_up.astype(BF),

time: 288 us -> 249 us (0.86)
  Pallas kernels: 237 us -> 222 us
  local copies, waits for them, and re-layouts: 23.2 us -> 10.6 us
  other arithmetic: 25 us -> 14.4 us
    pallas_call x1, Pallas kernels: 131 us -> 114 us  [layer(): pl.pallas_call(functools.partial(layer_kernel, count), out_shape=(out((ro...]
    convert_element_type x3 -> x0, other arithmetic: 9.18 us -> none  [the longest x1 3.54 us: local(): new_down.astype(BF)]
    unnamed x46 -> x44, local copies, waits for them, and re-layouts: 12.8 us -> 6.32 us
    pallas_call x1 -> x0, local copies, waits for them, and re-layouts: 4.27 us -> none  [layer(): pl.pallas_call(functools.partial(layer_kernel, count), out_shape=(out((ro...]
where the time goes in v4:
time: 249 us
  Pallas kernels  222 us (89%)
  other arithmetic  14.4 us (6%)
  local copies, waits for them, and re-layouts  10.6 us (4%)
    pallas_call x1, Pallas kernels, layer(): pl.pallas_call(functools.partial(layer_kernel, count), out_shape=(out((ro...  114 us
    pallas_call x1, Pallas kernels, muon(): pl.pallas_call(functools.partial(muon_kernel, count, sizes), out_shape=(o...  108 us
    unnamed x44, local copies, waits for them, and re-layouts  6.32 us
    add x1, other arithmetic, local(): new_mom_down = 0.5 * mom_down + grad_of(3, ff_cols)  6.13 us

profile of v4, /device:TPU:13, one launch (start us, length us, event | category | flops | bytes accessed | tf_op | source)
XLA Modules:
  0.0 248.6 jit_solution(6198578367702014215)
XLA Ops:
  0.7 1.3 reshape.73.fb
  1.9 1.3 reshape.74.mf
  3.2 0.0 copy-start
  3.2 0.0 copy-start.1
  3.2 0.0 copy-start.2
  3.2 113.8 %layer.1 = (bf16[512,768]{1,0:T(8,128)(2,1)}, f32[512,768]{1,0:T(8,128)}, bf16[512,768]{1,0:T(8,128)(2,1)}, bf16[768,768]{1,0:T(8,128)(2,1)}, f32[16,768]{1,0:T(8,128)}, /*index=5*/f32[8,128]{1,0:T(8,128)}) custom-call(bf16[512,768]{1,0:T(8,128)(2,1)} %x.1, bf16[512,768]{1,0:T(8,128)(2,1)} %cot.1, s32[2,256]{1,0:T(2,128)} %seg.1, f32[6,768]{1,0:T(8,128)} %rp.1, ...), custom_call_target="tpu_custom_call" | custom-call | tf_op jit(solution)/shard_map/layer/pallas_call | solution.py:894
  117.0 0.0 copy-done
  117.0 0.0 copy-done.1
  117.0 0.0 copy-done.2
  117.0 0.0 copy-start.3
  117.0 1.4 copy-done.3
  118.4 0.0 copy-start.4
  118.4 1.3 copy-done.4
  119.7 0.0 copy-start.5
  119.7 1.1 copy-done.5
  120.8 0.0 copy-start.6
  120.8 0.7 copy-done.6
  121.5 0.0 copy-start.7
  121.5 0.0 copy-start.8
  121.5 0.0 copy-start.9
  121.5 108.3 %muon.1 = (bf16[2304,768]{1,0:T(8,128)(2,1)}, bf16[2304,768]{1,0:T(8,128)(2,1)}, f32[8,128]{1,0:T(8,128)S(1)}, bf16[512,768]{1,0:T(8,128)(2,1)S(1)}) custom-call(f32[576,768]{1,0:T(8,128)S(1)} %bitcast.14, f32[192,768]{1,0:T(8,128)S(1)} %copy-done.2, f32[768,768]{1,0:T(8,128)S(1)} %copy-done, f32[768,768]{1,0:T(8,128)} %md.1, ...), custom_call_target="tpu_custom_call" | custom-call | tf_op jit(solution)/shard_map/muon/pallas_call | solution.py:1156
  229.8 0.0 copy-done.7
  229.8 0.0 copy-done.8
  229.8 0.0 copy-done.9
  229.8 0.0 copy-start.11
  229.9 6.1 %convert_add_fusion = (f32[768,768]{1,0:T(8,128)}, f32[768,768]{1,0:T(8,128)}, bf16[768,768]{1,0:T(8,128)(2,1)}, f32[768,768]{1,0:T(8,128)}, bf16[768,768]{1,0:T(8,128)(2,1)}, /*index=5*/f32[768,768]{1,0:T(8,128)}) fusion(f32[768,768]{1,0:T(8,128)S(1)} %copy-done.9, bf16[2304,768]{1,0:T(8,128)(2,1)} %get-tuple-element.36, f32[768,768]{1,0:T(8,128)S(1)} %copy-done, ...), kind=kLoop, calls=%fused_computation.1 | loop fusion | flops 8257536 | bytes 25952256 | tf_op jit(solution)/shard_map/add | solution.py:1219
  236.0 0.0 copy-done.11
  236.0 2.2 fusion.3
  238.2 0.0 copy-start.10
  238.2 1.5 convert_multiply_fusion
  239.7 1.2 slice.39
  240.9 0.0 copy-done.10
  240.9 0.0 copy-start.16
  240.9 0.0 copy-start.17
  240.9 0.0 copy-start.18
  241.0 0.0 copy-start.19
  241.0 0.0 copy-start.20
  241.0 0.0 copy-start.15
  241.0 0.0 copy-start.14
  241.0 0.0 copy-start.12
  241.0 2.4 fusion.4
  243.4 0.5 slice.50
  244.6 0.0 copy-done.16
  244.6 0.0 copy-done.17
  244.6 0.0 copy-done.18
  244.6 0.6 multiply_subtract_fusion.4
  245.2 0.1 multiply_reduce_fusion.1
  245.3 0.0 copy-done.19
  245.4 0.0 copy-done.20
  245.4 0.7 multiply_subtract_fusion.5
  246.0 0.0 copy-done.15
  246.0 0.1 multiply_reduce_fusion
  246.1 0.0 copy-start.13
  246.2 0.0 copy-done.14
  246.2 0.7 multiply_subtract_fusion.3
  246.9 0.0 copy-done.12
  246.9 0.9 copy.39
  247.7 0.9 copy.40
  248.6 0.0 copy-done.13
  (2 shorter events, 0.0 us)
Async XLA Ops:
  3.2 113.8 %copy-start = (f32[768,768]{1,0:T(8,128)S(1)}, f32[768,768]{1,0:T(8,128)}, u32[]{:S(2)}) copy-start(f32[768,768]{1,0:T(8,128)} %mu.1) | copy-start | bytes 7077892
  3.2 113.8 %copy-start.1 = (f32[3,768,192]{1,2,0:T(8,128)S(1)}, f32[3,768,192]{1,2,0:T(8,128)}, u32[]{:S(2)}) copy-start(f32[3,768,192]{1,2,0:T(8,128)} %param.27) | copy-start | bytes 5308420
  3.2 113.8 %copy-start.2 = (f32[192,768]{1,0:T(8,128)S(1)}, f32[192,768]{1,0:T(8,128)}, u32[]{:S(2)}) copy-start(f32[192,768]{1,0:T(8,128)} %mo.1) | copy-start | bytes 1769476
  117.0 1.4 copy-start.3
  118.4 1.3 copy-start.4
  119.7 1.1 copy-start.5
  120.8 0.7 copy-start.6
  121.5 108.3 %copy-start.7 = (f32[768,768]{1,0:T(8,128)S(1)}, f32[768,768]{1,0:T(8,128)}, u32[]{:S(2)}) copy-start(f32[768,768]{1,0:T(8,128)} %wu_hbm.1) | copy-start | bytes 7077892
  121.5 108.3 %copy-start.8 = (f32[768,768]{1,0:T(8,128)S(1)}, f32[768,768]{1,0:T(8,128)}, u32[]{:S(2)}) copy-start(f32[768,768]{1,0:T(8,128)} %wd_hbm.1) | copy-start | bytes 7077892
  121.5 108.3 %copy-start.9 = (f32[768,768]{1,0:T(8,128)S(1)}, f32[768,768]{1,0:T(8,128)}, u32[]{:S(2)}) copy-start(f32[768,768]{1,0:T(8,128)} %md.1) | copy-start | bytes 7077892
  229.8 6.1 %copy-start.11 = (f32[192,768]{1,0:T(8,128)S(1)}, f32[192,768]{1,0:T(8,128)}, u32[]{:S(2)}) copy-start(f32[192,768]{1,0:T(8,128)} %wo_hbm.1) | copy-start | bytes 1769476
  238.2 2.7 %copy-start.10 = (f32[3,768,192]{1,2,0:T(8,128)S(1)}, f32[3,768,192]{1,2,0:T(8,128)}, u32[]{:S(2)}) copy-start(f32[3,768,192]{1,2,0:T(8,128)} %param.20) | copy-start | bytes 5308420
  240.9 3.7 %copy-start.16 = (f32[16,768]{1,0:T(8,128)S(1)}, f32[16,768]{1,0:T(8,128)}, u32[]{:S(2)}) copy-start(f32[16,768]{1,0:T(8,128)} %get-tuple-element.38) | copy-start | bytes 147460
  240.9 3.7 %copy-start.17 = (f32[768]{0:T(1024)S(1)}, f32[768]{0:T(1024)}, u32[]{:S(2)}) copy-start(f32[768]{0:T(1024)} %param.25) | copy-start | bytes 9220
  240.9 3.7 %copy-start.18 = (f32[768]{0:T(1024)S(1)}, f32[768]{0:T(1024)}, u32[]{:S(2)}) copy-start(f32[768]{0:T(1024)} %param.32) | copy-start | bytes 9220
  241.0 4.4 %copy-start.19 = (f32[2,192]{1,0:T(2,128)S(1)}, f32[2,192]{1,0:T(2,128)}, u32[]{:S(2)}) copy-start(f32[2,192]{1,0:T(2,128)} %hb.1) | copy-start | bytes 4612
  241.0 4.4 %copy-start.20 = (f32[2,192]{1,0:T(2,128)S(1)}, f32[2,192]{1,0:T(2,128)}, u32[]{:S(2)}) copy-start(f32[2,192]{1,0:T(2,128)} %mh.1) | copy-start | bytes 4612
  241.0 5.0 %copy-start.15 = (f32[6,768]{1,0:T(8,128)S(1)}, f32[6,768]{1,0:T(8,128)}, u32[]{:S(2)}) copy-start(f32[6,768]{1,0:T(8,128)} %param.33) | copy-start | bytes 55300
  241.0 5.2 %copy-start.14 = (f32[6,768]{1,0:T(8,128)S(1)}, f32[6,768]{1,0:T(8,128)}, u32[]{:S(2)}) copy-start(f32[6,768]{1,0:T(8,128)} %rp.1) | copy-start | bytes 55300
  241.0 5.9 %copy-start.12 = (bf16[512,768]{1,0:T(8,128)(2,1)S(1)}, bf16[512,768]{1,0:T(8,128)(2,1)}, u32[]{:S(2)}) copy-start(bf16[512,768]{1,0:T(8,128)(2,1)} %get-tuple-element.84) | copy-start | bytes 2359300
  246.1 2.5 copy-start.13

commit v5 on v4

--- a/solution.py
+++ b/solution.py
@@ -178,6 +178,115 @@
     return [start, combine, settle, pass_on, finish]
 
 
+def relay_scratch(rows, width, dtype):
+    part = rows // 2
+    return [
+        pltpu.VMEM((2 * part, width), dtype),
+        pltpu.VMEM((part, width), dtype),
+        pltpu.VMEM((part, width), dtype),
+        pltpu.SemaphoreType.DMA((5 * SUBS,)),
+        pltpu.SemaphoreType.DMA((5 * SUBS,)),
+    ]
+
+
+def relay_sum(t, x, o, scratch):
+    taken, mixed, mix, ssem, rsem = scratch
+    part = mixed.shape[0]
+    piece = part // SUBS
+    subs = range(SUBS)
+    mate = t + 1 - 2 * (t % 2)
+    facing = 3 - t
+    outer = (t % 3) == 0
+    inner = (t % 3) != 0
+    near = t // 2
+    far = 1 - near
+
+    def at(ref, chunk, s):
+        return ref.at[pl.ds(pl.multiple_of(chunk * part + s * piece, piece), piece)]
+
+    def to(index, src, dst, recv, device):
+        return remote(
+            src, dst, ssem.at[index], rsem.at[recv], {"tensor": device}
+        )
+
+    def give_far(s):
+        return to(s, at(x, far, s), at(taken, 0, s), s, mate)
+
+    def give_near(s):
+        return to(SUBS + s, at(x, near, s), at(taken, 1, s), SUBS + s, mate)
+
+    def cross(s):
+        return to(s, at(mix, 0, s), at(mixed, 0, s), 2 * SUBS + s, facing)
+
+    def own_across(s):
+        return to(SUBS + s, at(o, near, s), at(o, near, s), (3 + near) * SUBS + s, facing)
+
+    def own_out(s):
+        return to(2 * SUBS + s, at(o, near, s), at(o, near, s), (3 + near) * SUBS + s, mate)
+
+    def far_out(s):
+        return to(3 * SUBS + s, at(o, far, s), at(o, far, s), (3 + far) * SUBS + s, mate)
+
+    def got(dst, recv):
+        remote(dst, dst, ssem.at[0], rsem.at[recv], {"tensor": mate}).wait_recv()
+
+    def add(dst, *terms):
+        total = terms[0][...].astype(F32)
+        for term in terms[1:]:
+            total = total + term[...].astype(F32)
+        dst[...] = total.astype(dst.dtype)
+
+    def start():
+        @pl.when(outer)
+        def _():
+            for build in (give_far, give_near):
+                for s in subs:
+                    build(s).start()
+
+    def combine():
+        @pl.when(inner)
+        def _():
+            for s in subs:
+                got(at(taken, 0, s), s)
+                add(at(mix, 0, s), at(taken, 0, s), at(x, far, s))
+                cross(s).start()
+
+    def settle():
+        @pl.when(inner)
+        def _():
+            for s in subs:
+                got(at(taken, 1, s), SUBS + s)
+                got(at(mixed, 0, s), 2 * SUBS + s)
+                add(at(o, near, s), at(x, near, s), at(taken, 1, s), at(mixed, 0, s))
+                own_across(s).start()
+                own_out(s).start()
+
+    def pass_on():
+        @pl.when(inner)
+        def _():
+            for s in subs:
+                got(at(o, far, s), (3 + far) * SUBS + s)
+                far_out(s).start()
+
+    def finish():
+        @pl.when(outer)
+        def _():
+            for chunk in (near, far):
+                for s in subs:
+                    got(at(o, chunk, s), (3 + chunk) * SUBS + s)
+            for build in (give_far, give_near):
+                for s in subs:
+                    build(s).wait_send()
+
+        @pl.when(inner)
+        def _():
+            for build in (cross, own_across, own_out, far_out):
+                for s in subs:
+                    build(s).wait_send()
+
+    return [start, combine, settle, pass_on, finish]
+
+
 def params(collective_id, mebibytes):
     return pltpu.CompilerParams(
         collective_id=collective_id,
@@ -187,7 +296,7 @@
 
 
 IN_VMEM = pl.BlockSpec(memory_space=pltpu.VMEM)
-IN_ANY = pl.BlockSpec(memory_space=pl.ANY)
+IN_HBM = pl.BlockSpec(memory_space=pltpu.HBM)
 
 
 def plane_scratch(count, rows, width):
@@ -582,9 +691,9 @@
 
 def layer_kernel(
     count,
-    x, cot, seg, rp, hb, fb, mh, mf, wq_hbm, wo_hbm, wu_hbm, wd_hbm,
+    seg, rp, hb, fb, mh, mf, x_hbm, cot_hbm, wq_hbm, wo_hbm, wu_hbm, wd_hbm,
     y, dz1, bt, grads, vec, squares,
-    wq_f, wo_f, wu_f, wd_f, wq, wo, wu, wd,
+    x, cot, wq_f, wo_f, wu_f, wd_f, wq, wo, wu, wd,
     q_s, k_s, v_s, ctx_s, p_s, n1_s, inv1_s, h1l_s, u_s, act_s, slope_s, dz2_s, dm_s, du_s, da_s,
     dq_s, dk_s, dv_s, part_s, red_s, gap, gbp, vecp, wsem, *scratch,
 ):
@@ -595,31 +704,36 @@
     columns = q_s.shape[1]
     heads = columns // HD
     scale = 1.0 / math.sqrt(HD)
-    greet(z_peers(t) + [{"dp": (p + k) % count} for k in range(1, count)])
     loads = [
         pltpu.make_async_copy(source, target, wsem.at[i])
         for i, (source, target) in enumerate(
-            ((wq_hbm, wq_f), (wo_hbm, wo_f), (wu_hbm, wu_f), (wd_hbm, wd_f))
+            (
+                (wq_hbm, wq_f), (wo_hbm, wo_f), (wu_hbm, wu_f), (wd_hbm, wd_f),
+                (x_hbm, x), (cot_hbm, cot),
+            )
         )
     ]
-    for load in loads:
-        load.start()
+    for place in (0, 4, 1, 2, 3, 5):
+        loads[place].start()
+    greet(z_peers(t) + [{"dp": (p + k) % count} for k in range(1, count)])
+    quarter = tokens // 4
     sums = []
-    for h in range(2):
-        place = pl.ds(h * half, half)
+    for q in range(4):
+        place = pl.ds(q * quarter, quarter)
         sums.append(
-            line_sum(t, part_s.at[place], red_s.at[place], scratch[6 * h : 6 * h + 6])
+            relay_sum(t, part_s.at[place], red_s.at[place], scratch[5 * q : 5 * q + 5])
         )
+    scratch = scratch[20:]
     top = 4 * columns
     if count == 8:
         ends = [(PLACE[2], 0, width), (PLACE[3], width, width)]
-        plane_b = square_reduce(p, gbp, grads, ends, scratch[12:17])
+        plane_b = square_reduce(p, gbp, grads, ends, scratch[0:5])
         ends = [(PLACE[0], 0, 3 * columns), (PLACE[1], 3 * columns, columns)]
-        plane_a = square_reduce(p, gap, grads, ends, scratch[17:22])
+        plane_a = square_reduce(p, gap, grads, ends, scratch[5:10])
     else:
-        plane_b = plane_sum(count, p, gbp, grads.at[pl.ds(top, 2 * width)], scratch[12:17])
-        plane_a = plane_sum(count, p, gap, grads.at[pl.ds(0, top)], scratch[17:22])
-    vector = vector_sum("dp", count, p, vecp, vec, scratch[22:25])
+        plane_b = plane_sum(count, p, gbp, grads.at[pl.ds(top, 2 * width)], scratch[0:5])
+        plane_a = plane_sum(count, p, gap, grads.at[pl.ds(0, top)], scratch[5:10])
+    vector = vector_sum("dp", count, p, vecp, vec, scratch[10:13])
     vecp[...] = jnp.zeros_like(vecp)
     lane = lax.broadcasted_iota(jnp.int32, (1, columns), 1)
 
@@ -629,12 +743,15 @@
     def rows_of(h):
         return pl.ds(h * half, half)
 
-    def over_rows(h, body, init=0):
+    def quarter_of(q):
+        return pl.ds(q * quarter, quarter)
+
+    def over_rows(q, body, init=0):
         def step(i, carry):
-            first = h * half + i * ROW_STEP
+            first = q * quarter + i * ROW_STEP
             return body(pl.ds(pl.multiple_of(first, ROW_STEP), ROW_STEP), carry)
 
-        return lax.fori_loop(0, half // ROW_STEP, step, init)
+        return lax.fori_loop(0, quarter // ROW_STEP, step, init)
 
     def fold(values):
         return values.reshape(ROW_STEP // 8, 8, values.shape[1]).sum(axis=0)
@@ -671,7 +788,7 @@
         ctx_s[r] = low
         part_s[r] = dot(low, wo[...]).astype(BF)
 
-    def up(h):
+    def up(q):
         def norm(r, carry):
             z = x[r].astype(F32) + red_s[r].astype(F32) + rp[0:1]
             center = z - jnp.mean(z, axis=-1, keepdims=True)
@@ -682,23 +799,23 @@
             h1l_s[r] = (normed * rp[2:3] + rp[3:4]).astype(BF)
             return carry
 
-        over_rows(h, norm)
-        u_s[rows_of(h)] = dot(h1l_s[rows_of(h)], wu[...])
+        over_rows(q, norm)
+        u_s[quarter_of(q)] = dot(h1l_s[quarter_of(q)], wu[...])
 
         def gelu(r, carry):
-            u = u_s[r] + fb[0:1]
+            u = u_s[r] + fb[...].reshape(1, width)
             cdf = 0.5 * (1.0 + lax.erf(u * (1.0 / math.sqrt(2.0))))
             act_s[r] = (u * cdf).astype(BF)
             slope_s[r] = cdf + u * jnp.exp(-0.5 * u * u) * (1.0 / math.sqrt(2.0 * math.pi))
             return carry
 
-        over_rows(h, gelu)
-
-    def down(h):
-        r = rows_of(h)
+        over_rows(q, gelu)
+
+    def down(q):
+        r = quarter_of(q)
         part_s[r] = dot(act_s[r], wd[...]).astype(BF)
 
-    def out_back(h):
+    def out_back(q):
         def norm(r, carry):
             s_dz2, s_dyn, s_dy = carry
             h1 = n1_s[r] * rp[2:3] + rp[3:4]
@@ -717,26 +834,26 @@
             return s_dz2 + fold(dz2), s_dyn + fold(dy * normed), s_dy + fold(dy)
 
         zero = jnp.zeros((8, width), F32)
-        for row, total in zip((1, 4, 5), over_rows(h, norm, (zero, zero, zero))):
+        for row, total in zip((1, 4, 5), over_rows(q, norm, (zero, zero, zero))):
             add_vec(row, total)
-        u_s[rows_of(h)] = dot_t(dm_s[rows_of(h)], wd[...])
+        u_s[quarter_of(q)] = dot_t(dm_s[quarter_of(q)], wd[...])
 
         def slope(r, carry):
             du = (u_s[r] * slope_s[r]).astype(BF)
             du_s[r] = du
             return carry + fold(du.astype(F32))
 
-        add_vec(6, over_rows(h, slope, zero))
-
-    def up_back(h):
-        r = rows_of(h)
+        add_vec(6, over_rows(q, slope, zero))
+
+    def up_back(q):
+        r = quarter_of(q)
         part_s[r] = dot_t(du_s[r], wu[...]).astype(BF)
 
     def grads_b():
         gbp[0:width] = tdot(h1l_s[...], du_s[...]).astype(BF)
         gbp[width : 2 * width] = tdot(act_s[...], dm_s[...]).astype(BF)
 
-    def attention_back(h):
+    def norm_back(q):
         def norm(r, carry):
             s_dz1, s_dhn, s_dh = carry
             dh1 = red_s[r].astype(F32) + dz2_s[r]
@@ -750,8 +867,10 @@
             return s_dz1 + fold(grad), s_dhn + fold(dh1 * normed), s_dh + fold(dh1)
 
         zero = jnp.zeros((8, width), F32)
-        for row, total in zip((0, 2, 3), over_rows(h, norm, (zero, zero, zero))):
+        for row, total in zip((0, 2, 3), over_rows(q, norm, (zero, zero, zero))):
             add_vec(row, total)
+
+    def attention_back(h):
         r = rows_of(h)
         dc = dot_t(da_s[r], wo[...]).astype(BF)
         q, k, v = q_s[r], k_s[r], v_s[r]
@@ -781,57 +900,39 @@
         total = dot(dq_s[r], wq[0]) + dot(dk_s[r], wq[1]) + dot(dv_s[r], wq[2])
         bt[r] = total.astype(BF)
 
-    (a_start, a_mix, a_settle, a_pass, a_end), (b_start, b_mix, b_settle, b_pass, b_end) = sums
+    start, mix, settle, pass_on, end = (
+        (lambda q, place=place: sums[q][place]()) for place in range(5)
+    )
+
+    def round_trip(first, second):
+        end(0), first(0), pass_on(1), second(0), settle(2), mix(3), start(0)
+        end(1), first(1), pass_on(2), settle(3), second(1), mix(0), start(1)
+        end(2), first(2), pass_on(3), second(2), settle(0), mix(1), start(2)
+        end(3), first(3), pass_on(0), second(3), settle(1), mix(2), start(3)
+
+    loads[4].wait()
     narrow(0, wq_f, wq)
     narrow(1, wo_f, wo)
     attention(0)
-    a_start()
+    start(0), start(1)
     attention(1)
-    a_mix()
-    b_start()
+    mix(0), start(2), mix(1), settle(0), start(3)
     narrow(2, wu_f, wu)
-    a_settle()
-    b_mix()
-    a_pass()
-    b_settle()
+    mix(2), settle(1), pass_on(0)
     narrow(3, wd_f, wd)
-    a_end()
-    up(0)
-    b_pass()
-    down(0)
-    a_start()
-    b_end()
-    up(1)
-    a_mix()
-    down(1)
-    b_start()
-    a_settle()
-    b_mix()
-    a_pass()
-    b_settle()
-    a_end()
-    out_back(0)
-    b_pass()
-    up_back(0)
-    a_start()
-    b_end()
-    out_back(1)
-    a_mix()
-    up_back(1)
-    b_start()
+    loads[5].wait()
+    round_trip(up, down)
+    round_trip(out_back, up_back)
     grads_b()
     plane_b[0]()
-    a_settle()
-    b_mix()
+    end(0), norm_back(0), pass_on(1), settle(2), mix(3)
     plane_b[1]()
-    a_pass()
-    b_settle()
-    a_end()
+    end(1), norm_back(1), pass_on(2), settle(3)
+    attention_back(0)
+    end(2), norm_back(2), pass_on(3)
     if count == 8:
         plane_b[2]()
-    attention_back(0)
-    b_pass()
-    b_end()
+    end(3), norm_back(3)
     attention_back(1)
     grads_a()
     plane_a[0]()
@@ -846,7 +947,7 @@
     vector[1]()
     moved = 0.5 * mh[...] + vec[7:9, 0:columns]
     squares[0:2] = jnp.broadcast_to(jnp.sum(moved * moved, axis=1, keepdims=True), (2, 128))
-    moved = 0.5 * mf[...] + vec[6:7]
+    moved = 0.5 * mf[...].reshape(1, width) + vec[6:7]
     squares[2:3] = jnp.broadcast_to(jnp.sum(moved * moved, axis=1, keepdims=True), (1, 128))
     squares[3:8] = jnp.zeros((5, 128), F32)
     plane_a[3]()
@@ -872,7 +973,8 @@
         return jax.ShapeDtypeStruct(shape, dtype)
 
     scratch = (
-        [full(*weight.shape) for weight in weights]
+        [low(rows, width)] * 2
+        + [full(*weight.shape) for weight in weights]
         + [low(*weight.shape) for weight in weights]
         + [low(rows, columns)] * 4
         + [full(2 * heads, half, half), full(rows, width), full(rows, 128), low(rows, width)]
@@ -881,8 +983,8 @@
         + [low(rows, columns)] * 3
         + [low(rows, width)] * 2
         + [low(4 * columns, width), low(2 * width, width), full(16, width)]
-        + [pltpu.SemaphoreType.DMA((4,))]
-        + line_scratch(half, width, BF) * 2
+        + [pltpu.SemaphoreType.DMA((6,))]
+        + relay_scratch(rows // 4, width, BF) * 4
         + (reduce_scratch(2 * width, width) if count == 8 else plane_scratch(count, 2 * width, width))
         + (
             reduce_scratch(4 * columns, width)
@@ -901,12 +1003,12 @@
             out((16, width), F32),
             out((8, 128), F32),
         ),
-        in_specs=[IN_VMEM] * 8 + [IN_ANY] * 4,
+        in_specs=[IN_VMEM] * 6 + [IN_HBM] * 6,
         out_specs=(IN_VMEM,) * 6,
         scratch_shapes=scratch,
         compiler_params=params(collective_id, 56),
         name="layer",
-    )(tokens, cotangent, segments, *small, *weights)
+    )(segments, *small, tokens, cotangent, *weights)
 
 
 def cut(values):
@@ -1161,12 +1263,89 @@
             out(squares.shape, F32),
             out(back.shape, BF),
         ),
-        in_specs=[IN_ANY] * 5 + [IN_VMEM] * 3,
+        in_specs=[IN_HBM] * 5 + [IN_VMEM] * 3,
         out_specs=(IN_VMEM,) * 4,
         scratch_shapes=scratch,
         compiler_params=params(collective_id, 44),
         name="muon",
     )(*moments, grads, squares, back, grad_first)
+
+
+def apply_kernel(factors, *refs):
+    ins, outs = refs[:26], refs[26:]
+    small_in, small_out = ins[18:], outs[14:]
+    for index, factor in enumerate(factors):
+        weight, moment, grad, step = (ins[4 * index + i] for i in range(4))
+        new_moment, new, low = (outs[3 * index + i] for i in range(3))
+        new_moment[...] = 0.5 * moment[...] + grad[...].astype(F32)
+        value = weight[...] - factor * step[...].astype(F32)
+        new[...] = value
+        low[...] = value.astype(BF)
+    for source, target in zip(ins[16:18], outs[12:14]):
+        target[...] = source[...]
+
+    @pl.when(pl.program_id(0) == 0)
+    def _():
+        vec, totals, heads, ff, rows, mom_heads, mom_ff, mom_rows = small_in
+        columns = heads.shape[1]
+        wide = ff.shape[0]
+        moment = 0.5 * mom_heads[...] + vec[7:9, 0:columns]
+        small_out[0][...] = moment
+        scale = lax.rsqrt(totals[0:2, 0:1] * (1.0 / (4 * columns)) + 1e-06)
+        small_out[1][...] = heads[...] - 0.1 * moment * scale
+        moment = 0.5 * mom_ff[...].reshape(1, wide) + vec[6:7]
+        small_out[2][...] = moment.reshape(wide)
+        scale = lax.rsqrt(totals[2:3, 0:1] * (1.0 / (4 * wide)) + 1e-06)
+        value = ff[...].reshape(1, wide) - 0.1 * moment * scale
+        small_out[3][...] = value.reshape(wide)
+        moment = 0.5 * mom_rows[...] + vec[0:6]
+        small_out[4][...] = moment
+        mean = jnp.mean(moment * moment, axis=-1, keepdims=True)
+        small_out[5][...] = rows[...] - 0.1 * moment * lax.rsqrt(mean + 1e-06)
+
+
+APPLY_STEPS = 4
+
+
+def apply(sizes, factors, weights, moments, grads, steps, passed, small):
+    width = grads.shape[1]
+    in_specs, operands, out_specs, out_shape = [], [], [], []
+
+    def block(rows, first=0):
+        share = rows // APPLY_STEPS
+        return pl.BlockSpec((share, width), lambda i, skip=first // share: (skip + i, 0))
+
+    def whole(array):
+        return pl.BlockSpec(array.shape, lambda i, n=array.ndim: (0,) * n)
+
+    first = 0
+    for rows, weight, moment in zip(sizes, weights, moments):
+        in_specs += [block(rows), block(rows), block(rows, first), block(rows, first)]
+        operands += [weight, moment, grads, steps]
+        out_specs += [block(rows)] * 3
+        out_shape += [jax.ShapeDtypeStruct((rows, width), kind) for kind in (F32, F32, BF)]
+        first += rows
+    for array in passed:
+        in_specs.append(block(array.shape[0]))
+        operands.append(array)
+        out_specs.append(block(array.shape[0]))
+        out_shape.append(jax.ShapeDtypeStruct(array.shape, array.dtype))
+    for array in small:
+        in_specs.append(whole(array))
+        operands.append(array)
+    for array in small[2:5]:
+        for _ in range(2):
+            out_specs.append(whole(array))
+            out_shape.append(jax.ShapeDtypeStruct(array.shape, F32))
+    return pl.pallas_call(
+        functools.partial(apply_kernel, factors),
+        grid=(APPLY_STEPS,),
+        out_shape=tuple(out_shape),
+        in_specs=in_specs,
+        out_specs=tuple(out_specs),
+        compiler_params=pltpu.CompilerParams(vmem_limit_bytes=40 * 1024 * 1024),
+        name="apply",
+    )(*operands)
 
 
 def vector_step(param, moment, mean_sq):
@@ -1187,18 +1366,29 @@
     wq_rows = w_qkv.transpose(0, 2, 1)
     output_rows, grad_first, back_terms, grads, vector_total, squares = layer(
         count, tokens, cotangent, segments,
-        (row_params, head_bias, ff_bias.reshape(1, ff_cols), mom_heads, mom_ff.reshape(1, ff_cols)),
+        (row_params, head_bias, ff_bias, mom_heads, mom_ff),
         (wq_rows, w_out, w_up, w_down), 1,
     )
-    new_mom_heads = 0.5 * mom_heads + vector_total[7:9, :columns]
-    new_mom_ff = 0.5 * mom_ff + vector_total[6]
-    new_mom_params = 0.5 * mom_params + vector_total[0:6]
     moments = (mom_qkv.transpose(0, 2, 1).reshape(qkv_rows, width), mom_out, mom_up, mom_down)
     steps, gathered, totals, grad_inputs = muon(
         count, moments, grads, squares, back_terms, grad_first, 2
     )
+    wide = math.sqrt(ff_cols * tensor_size / width)
     if count == 8:
-        grads = gathered
+        sizes = (qkv_rows, columns, width, ff_cols)
+        factors = (0.8 * math.sqrt(3.0), 0.8, 0.8 * wide, 0.8 * wide)
+        done = apply(
+            sizes, factors, (wq_rows.reshape(qkv_rows, width), w_out, w_up, w_down), moments,
+            gathered, steps, (output_rows, grad_inputs),
+            (
+                vector_total, totals, head_bias, ff_bias, row_params,
+                mom_heads, mom_ff, mom_params,
+            ),
+        )
+        qkv_new = [rows.reshape(3, columns, width).transpose(0, 2, 1) for rows in done[0:3]]
+        return (
+            *done[12:14], *qkv_new, *done[3:12], *done[14:20],
+        )
 
     def to_qkv(rows):
         return rows.reshape(3, columns, width).transpose(0, 2, 1)
@@ -1209,15 +1399,17 @@
         return grads[bounds[index] : bounds[index] + rows].astype(F32)
 
     def step_of(index, rows):
-        first = bounds[index] if count == 8 else PLACE[index] * width
+        first = PLACE[index] * width
         part = steps[first : first + rows].astype(F32)
-        return part.T if index == 2 and count != 8 else part
-
+        return part.T if index == 2 else part
+
+    new_mom_heads = 0.5 * mom_heads + vector_total[7:9, :columns]
+    new_mom_ff = 0.5 * mom_ff + vector_total[6]
+    new_mom_params = 0.5 * mom_params + vector_total[0:6]
     new_mom_qkv = 0.5 * mom_qkv + to_qkv(grad_of(0, qkv_rows))
     new_mom_out = 0.5 * mom_out + grad_of(1, columns)
     new_mom_up = 0.5 * mom_up + grad_of(2, width)
     new_mom_down = 0.5 * mom_down + grad_of(3, ff_cols)
-    wide = math.sqrt(ff_cols * tensor_size / width)
     new_qkv = w_qkv - 0.8 * math.sqrt(3.0) * to_qkv(step_of(0, qkv_rows))
     new_out = w_out - 0.8 * step_of(1, columns)
     new_up = w_up - 0.8 * wide * step_of(2, width)

time: 249 us -> 223 us (0.90)
  other arithmetic: 14.4 us -> 0 us
  local copies, waits for them, and re-layouts: 10.6 us -> 4.56 us
  Pallas kernels: 222 us -> 217 us
    pallas_call x1, Pallas kernels: 114 us -> 101 us  [layer(): pl.pallas_call(functools.partial(layer_kernel, count), out_shape=(out((ro...]
    pallas_call x0 -> x1, Pallas kernels: none -> 10.9 us  [apply(): pl.pallas_call(functools.partial(apply_kernel, factors), grid=(APPLY_STEP...]
    add x1 -> x0, other arithmetic: 6.13 us -> none  [local(): new_mom_down = 0.5 * mom_down + grad_of(3, ff_cols)]
    convert_element_type x2 -> x0, other arithmetic: 4.59 us -> none  [the longest x1 2.36 us: local(): new_qkv.astype(BF)]
    pallas_call x1, Pallas kernels: 108 us -> 105 us  [muon(): pl.pallas_call(functools.partial(muon_kernel, count, sizes), out_shape=(o...]
    reshape x2 -> x0, local copies, waits for them, and re-layouts: 2.54 us -> none  [the longest x1 1.27 us: local(): ff_bias.reshape(1, ff_cols)]
    unnamed x44 -> x38, local copies, waits for them, and re-layouts: 6.32 us -> 4.56 us
where the time goes in v5:
time: 223 us
  Pallas kernels  217 us (97%)
  local copies, waits for them, and re-layouts  4.56 us (2%)
    pallas_call x1, Pallas kernels, muon(): pl.pallas_call(functools.partial(muon_kernel, count, sizes), out_shape=(o...  105 us
    pallas_call x1, Pallas kernels, layer(): pl.pallas_call(functools.partial(layer_kernel, count), out_shape=(out((ro...  101 us
    pallas_call x1, Pallas kernels, apply(): pl.pallas_call(functools.partial(apply_kernel, factors), grid=(APPLY_STEP...  10.9 us
    unnamed x38, local copies, waits for them, and re-layouts  4.56 us

profile of v5, /device:TPU:13, one launch (start us, length us, event | category | flops | bytes accessed | tf_op | source)
XLA Modules:
  0.0 223.1 jit_solution(8325606007424107010)
XLA Ops:
  0.7 0.0 copy-start
  0.7 0.0 copy-start.4
  0.7 0.0 copy-start.5
  0.7 101.3 %layer.1 = (bf16[512,768]{1,0:T(8,128)(2,1)}, f32[512,768]{1,0:T(8,128)}, bf16[512,768]{1,0:T(8,128)(2,1)}, bf16[768,768]{1,0:T(8,128)(2,1)}, f32[16,768]{1,0:T(8,128)}, /*index=5*/f32[8,128]{1,0:T(8,128)}) custom-call(s32[2,256]{1,0:T(2,128)} %seg.1, f32[6,768]{1,0:T(8,128)} %refs_22_.1, f32[2,192]{1,0:T(2,128)} %refs_20_.1, f32[768]{0:T(1024)} %refs_21_.1, ...), custom_call_target="tpu_custom_call" | custom-call | tf_op jit(solution)/shard_map/layer/pallas_call | solution.py:996
  102.0 0.0 copy-done
  102.0 0.0 copy-done.4
  102.0 0.0 copy-done.5
  102.0 0.0 copy-start.7
  102.0 1.4 copy-done.7
  103.4 0.0 copy-start.8
  103.4 1.3 copy-done.8
  104.7 0.0 copy-start.9
  104.7 1.1 copy-done.9
  105.8 0.0 copy-start.18
  105.8 0.7 copy-done.18
  106.5 0.0 copy-start.1
  106.5 0.0 copy-start.2
  106.5 0.0 copy-start.3
  106.5 0.0 copy-start.6
  106.5 0.0 copy-start.10
  106.5 0.0 copy-start.11
  106.5 0.0 copy-start.12
  106.5 0.0 copy-start.13
  106.6 0.0 copy-start.14
  106.6 0.0 copy-start.15
  106.6 0.0 copy-start.16
  106.6 0.0 copy-start.17
  106.6 105.2 %muon.1 = (bf16[2304,768]{1,0:T(8,128)(2,1)}, bf16[2304,768]{1,0:T(8,128)(2,1)}, f32[8,128]{1,0:T(8,128)S(1)}, bf16[512,768]{1,0:T(8,128)(2,1)S(1)}) custom-call(f32[576,768]{1,0:T(8,128)S(1)} %bitcast.17, f32[192,768]{1,0:T(8,128)S(1)} %copy-done.5, f32[768,768]{1,0:T(8,128)S(1)} %copy-done, f32[768,768]{1,0:T(8,128)} %refs_13_.1, ...), custom_call_target="tpu_custom_call" | custom-call | tf_op jit(solution)/shard_map/muon/pallas_call | solution.py:1258
  211.8 0.0 copy-done.1
  211.9 0.0 copy-done.2
  211.9 0.0 copy-done.3
  211.9 0.0 copy-done.6
  211.9 0.0 copy-done.10
  211.9 0.0 copy-done.11
  211.9 0.0 copy-done.12
  211.9 0.0 copy-done.13
  211.9 0.0 copy-done.14
  211.9 0.0 copy-done.15
  211.9 0.0 copy-done.16
  212.0 0.0 copy-done.17
  212.0 10.9 %apply.1 = (f32[576,768]{1,0:T(8,128)}, f32[576,768]{1,0:T(8,128)}, bf16[576,768]{1,0:T(8,128)(2,1)}, f32[192,768]{1,0:T(8,128)}, f32[192,768]{1,0:T(8,128)}, /*...) custom-call(f32[576,768]{1,0:T(8,128)S(1)} %bitcast.16, ...), custom_call_target="tpu_custom_call" | custom-call | tf_op jit(solution)/shard_map/apply/pallas_call | solution.py:1340
Async XLA Ops:
  0.7 101.3 %copy-start = (f32[768,768]{1,0:T(8,128)S(1)}, f32[768,768]{1,0:T(8,128)}, u32[]{:S(2)}) copy-start(f32[768,768]{1,0:T(8,128)} %refs_9_.1) | copy-start | bytes 7077892
  0.7 101.3 %copy-start.4 = (f32[3,768,192]{1,2,0:T(8,128)S(1)}, f32[3,768,192]{1,2,0:T(8,128)}, u32[]{:S(2)}) copy-start(f32[3,768,192]{1,2,0:T(8,128)} %param.27) | copy-start | bytes 5308420
  0.7 101.3 %copy-start.5 = (f32[192,768]{1,0:T(8,128)S(1)}, f32[192,768]{1,0:T(8,128)}, u32[]{:S(2)}) copy-start(f32[192,768]{1,0:T(8,128)} %refs_5_.1) | copy-start | bytes 1769476
  102.0 1.4 copy-start.7
  103.4 1.3 copy-start.8
  104.7 1.1 copy-start.9
  105.8 0.7 copy-start.18
  106.5 105.3 %copy-start.1 = (f32[768,768]{1,0:T(8,128)S(1)}, f32[768,768]{1,0:T(8,128)}, u32[]{:S(2)}) copy-start(f32[768,768]{1,0:T(8,128)} %refs_8_.1) | copy-start | bytes 7077892
  106.5 105.4 %copy-start.2 = (f32[768,768]{1,0:T(8,128)S(1)}, f32[768,768]{1,0:T(8,128)}, u32[]{:S(2)}) copy-start(f32[768,768]{1,0:T(8,128)} %refs_12_.1) | copy-start | bytes 7077892
  106.5 105.4 %copy-start.3 = (f32[3,768,192]{1,2,0:T(8,128)S(1)}, f32[3,768,192]{1,2,0:T(8,128)}, u32[]{:S(2)}) copy-start(f32[3,768,192]{1,2,0:T(8,128)} %param.20) | copy-start | bytes 5308420
  106.5 105.4 %copy-start.6 = (f32[192,768]{1,0:T(8,128)S(1)}, f32[192,768]{1,0:T(8,128)}, u32[]{:S(2)}) copy-start(f32[192,768]{1,0:T(8,128)} %refs_4_.1) | copy-start | bytes 1769476
  106.5 105.4 %copy-start.10 = (bf16[512,768]{1,0:T(8,128)(2,1)S(1)}, bf16[512,768]{1,0:T(8,128)(2,1)}, u32[]{:S(2)}) copy-start(bf16[512,768]{1,0:T(8,128)(2,1)} %get-tuple-element.56.refs_16_) | copy-start | bytes 2359300
  106.5 105.4 %copy-start.11 = (f32[6,768]{1,0:T(8,128)S(1)}, f32[6,768]{1,0:T(8,128)}, u32[]{:S(2)}) copy-start(f32[6,768]{1,0:T(8,128)} %refs_22_.1) | copy-start | bytes 55300
  106.5 105.4 %copy-start.12 = (f32[16,768]{1,0:T(8,128)S(1)}, f32[16,768]{1,0:T(8,128)}, u32[]{:S(2)}) copy-start(f32[16,768]{1,0:T(8,128)} %get-tuple-element.58.refs_18_) | copy-start | bytes 147460
  106.5 105.4 %copy-start.13 = (f32[6,768]{1,0:T(8,128)S(1)}, f32[6,768]{1,0:T(8,128)}, u32[]{:S(2)}) copy-start(f32[6,768]{1,0:T(8,128)} %refs_25_.1) | copy-start | bytes 55300
  106.6 105.4 %copy-start.14 = (f32[768]{0:T(1024)S(1)}, f32[768]{0:T(1024)}, u32[]{:S(2)}) copy-start(f32[768]{0:T(1024)} %refs_21_.1) | copy-start | bytes 9220
  106.6 105.4 %copy-start.15 = (f32[768]{0:T(1024)S(1)}, f32[768]{0:T(1024)}, u32[]{:S(2)}) copy-start(f32[768]{0:T(1024)} %refs_24_.1) | copy-start | bytes 9220
  106.6 105.4 %copy-start.16 = (f32[2,192]{1,0:T(2,128)S(1)}, f32[2,192]{1,0:T(2,128)}, u32[]{:S(2)}) copy-start(f32[2,192]{1,0:T(2,128)} %refs_20_.1) | copy-start | bytes 4612
  106.6 105.4 %copy-start.17 = (f32[2,192]{1,0:T(2,128)S(1)}, f32[2,192]{1,0:T(2,128)}, u32[]{:S(2)}) copy-start(f32[2,192]{1,0:T(2,128)} %refs_23_.1) | copy-start | bytes 4612
